TPU v7x, 32 devices: a whole 2x2x4 slice. The times are simulated.
32 devices in a mesh: dp: 8 (over z, y), mp: 4 (over x, core).
Axes of the slice: x: 2, y: 2, z: 4, core: 2. Of those that a mesh axis runs over, the one named last changes fastest.
Arguments:
- patches: bfloat16 [32768, 768], P(('dp', 'mp')), may hold values from -6 to 6
- patch_pos: int32 [32768], P(('dp', 'mp')), may hold values from 0 to 127
- owner: int32 [32768, 1], P(('dp', 'mp')), may hold values from 0 to 3; in each aligned block of 1024 rows (0 to 1023, 1024 to 2047, ...) at most 384 rows name the same one
- local_row: int32 [32768], P(('dp', 'mp')), may hold values from 0 to 8255
- counts: int32 [32, 3], replicated, may hold values from 1 to 1023, as said below
- task: int32 [32], replicated, may hold values from 0 to 31
- table: float32 [33024, 768], P(('mp', 'dp'))
- table_mom: float32 [33024, 768], P(('mp', 'dp')), may hold values from -1.9073486e-05 to 1.9073486e-05
- table_avg: float32 [33024, 768], P(('mp', 'dp')), may hold values from -0.21875 to 0.21875
- patch_w: float32 [896, 768], P(('dp', 'mp')), may hold values from -0.21875 to 0.21875
- patch_mom: float32 [896, 768], P(('dp', 'mp')), may hold values from -1.9073486e-05 to 1.9073486e-05
- patch_avg: float32 [896, 768], P(('dp', 'mp')), may hold values from -0.21875 to 0.21875
- attn_w: float32 [768, 3072], P(('dp', 'mp'))
- attn_mom: float32 [768, 3072], P(('dp', 'mp')), may hold values from -1.9073486e-05 to 1.9073486e-05
- attn_avg: float32 [768, 3072], P(('dp', 'mp')), may hold values from -0.21875 to 0.21875
- up_w: float32 [768, 3072], P(('dp', 'mp')), may hold values from -0.21875 to 0.21875
- up_mom: float32 [768, 3072], P(('dp', 'mp')), may hold values from -1.9073486e-05 to 1.9073486e-05
- up_avg: float32 [768, 3072], P(('dp', 'mp')), may hold values from -0.21875 to 0.21875
- down_w: float32 [3072, 768], P(('dp', 'mp')), may hold values from -0.109375 to 0.109375
- down_mom: float32 [3072, 768], P(('dp', 'mp')), may hold values from -1.9073486e-05 to 1.9073486e-05
- down_avg: float32 [3072, 768], P(('dp', 'mp')), may hold values from -0.109375 to 0.109375
- gains: float32 [3, 768], P(None, ('dp', 'mp'))
- gain_mom: float32 [3, 768], P(None, ('dp', 'mp')), may hold values from -7.6293945e-05 to 7.6293945e-05
- gain_avg: float32 [3, 768], P(None, ('dp', 'mp')), may hold values from 0.5 to 1.5
Outputs:
- table_new: float32 [33024, 768], P(('mp', 'dp'))
- table_mom_new: float32 [33024, 768], P(('mp', 'dp'))
- table_avg_new: float32 [33024, 768], P(('mp', 'dp'))
- table_half: bfloat16 [33024, 768], P(('mp', 'dp'))
- patch_new: float32 [896, 768], P(('dp', 'mp'))
- patch_mom_new: float32 [896, 768], P(('dp', 'mp'))
- patch_avg_new: float32 [896, 768], P(('dp', 'mp'))
- patch_half: bfloat16 [896, 768], P(('dp', 'mp'))
- attn_new: float32 [768, 3072], P(('dp', 'mp'))
- attn_mom_new: float32 [768, 3072], P(('dp', 'mp'))
- attn_avg_new: float32 [768, 3072], P(('dp', 'mp'))
- attn_half: bfloat16 [768, 3072], P(('dp', 'mp'))
- up_new: float32 [768, 3072], P(('dp', 'mp'))
- up_mom_new: float32 [768, 3072], P(('dp', 'mp'))
- up_avg_new: float32 [768, 3072], P(('dp', 'mp'))
- up_half: bfloat16 [768, 3072], P(('dp', 'mp'))
- down_new: float32 [3072, 768], P(('dp', 'mp'))
- down_mom_new: float32 [3072, 768], P(('dp', 'mp'))
- down_avg_new: float32 [3072, 768], P(('dp', 'mp'))
- down_half: bfloat16 [3072, 768], P(('dp', 'mp'))
- gains_new: float32 [3, 768], P(None, ('dp', 'mp'))
- gain_mom_new: float32 [3, 768], P(None, ('dp', 'mp'))
- gain_avg_new: float32 [3, 768], P(None, ('dp', 'mp'))
- loss_sum: float32 [], replicated
- loss_count: float32 [], replicated
- clip_norm: float32 [], replicated
- rms_stats: float32 [4], replicated
Inputs may be any that keep to these rules, and one draw needn't show every extreme that they name: In the rows of one device no owner is named more than 384 times; some owner exactly 384 times. `counts`: column 0 (patch tokens) is 1 to 768; column 1 (table tokens) is 256 or more, with columns 0 and 1 summing to 1024 at most; column 2 (scored tokens) is 1 to 256, reached.
All inputs are finite; a program needn't handle non-finite values.
Results may differ from a plain program's by a relative error of at most 0.013.
The roundings to bfloat16 on the way count: a program that leaves them out, or rounds other values in their place, can miss the bound.
Values may be sent and summed in bfloat16 or wider, within the bound.
No kernel may reach another device: no remote copies, remote signals or barrier semaphores. Data moves between devices by JAX's collectives and lax.ppermute only.
A program may use at most 512 MiB of HBM per device.

v0:
```python
import math

import jax
import jax.numpy as jnp
from jax import lax
from jax.sharding import PartitionSpec as P

D = 768
HEADS = 24
HDIM = 32
POSN = 128
SEQ_LEN = 1024
LOSS = 256
TASKS = 32


NORM_EPS = 1e-05
STEP_RATE = 5000.0
MOMENTUM = 0.5
AVERAGE_DECAY = 0.5
CLIP_LIMIT = 0.02


def combined_all(value, axis, join):
    pieces = jax.tree.map(lambda part: lax.all_gather(part, axis), value)
    head = jax.tree.map(lambda part: part[0], pieces)
    tail = jax.tree.map(lambda part: part[1:], pieces)
    running, _ = lax.scan(lambda running, slab: (join(running, slab), None), head, tail)
    return running


def layer_norm(values, gain):
    row_mean = jnp.mean(values, -1, keepdims=True)
    centred = values - row_mean
    spread = jnp.mean(centred * centred, -1, keepdims=True)
    return centred * lax.rsqrt(spread + NORM_EPS) * gain


def gelu_tanh(values):
    return jax.nn.gelu(values, approximate=True)


def outer(left, right):
    return lax.dot_general(
        left, right, (((0,), (0,)), ((), ())), preferred_element_type=jnp.float32
    )


def inner(left, right):
    return lax.dot_general(
        left, right, (((1,), (1,)), ((), ())), preferred_element_type=jnp.float32
    )


def block_scores(query_part, key_part, offset):
    scores = jnp.einsum(
        "qhd,khd->hqk", query_part, key_part, preferred_element_type=jnp.float32
    ) * HDIM ** (-0.5)
    seq_length = key_part.shape[0]
    query_pos = offset + jnp.arange(query_part.shape[0])
    allowed = jnp.arange(seq_length)[None, :] <= query_pos[:, None]
    return jnp.where(allowed[None], scores, -1e30)


def split_heads(projected, count_seq):
    shaped = projected.reshape(count_seq, SEQ_LEN, 3, HEADS, HDIM)
    return (shaped[:, :, 0], shaped[:, :, 1], shaped[:, :, 2])


def attention_forward(query_rows, key_rows, value_rows):
    count_seq = query_rows.shape[0]
    block_rows = min(512, SEQ_LEN)
    block_count = SEQ_LEN // block_rows

    def one_block(block_index):
        sequence = block_index // block_count
        offset = block_index % block_count * block_rows
        query_part = lax.dynamic_slice_in_dim(query_rows[sequence], offset, block_rows, 0)
        scores = block_scores(query_part, key_rows[sequence], offset)
        row_top = jnp.max(scores, -1, keepdims=True)
        exponent = jnp.exp(scores - row_top)
        row_total = jnp.sum(exponent, -1, keepdims=True)
        probability = (exponent / row_total).astype(jnp.bfloat16)
        attended = jnp.einsum(
            "hqk,khd->qhd", probability, value_rows[sequence], preferred_element_type=jnp.float32
        )
        return (attended.astype(jnp.bfloat16), (row_top + jnp.log(row_total))[..., 0])

    attended, log_total = lax.map(one_block, jnp.arange(count_seq * block_count))
    return (attended.reshape(count_seq * SEQ_LEN, HEADS * HDIM), log_total)


def attention_backward(query_rows, key_rows, value_rows, grad_attended, log_total):
    count_seq = query_rows.shape[0]
    block_rows = min(512, SEQ_LEN)
    block_count = SEQ_LEN // block_rows
    grad_heads = grad_attended.reshape(count_seq, SEQ_LEN, HEADS, HDIM)

    def one_block(block_index):
        sequence = block_index // block_count
        offset = block_index % block_count * block_rows
        query_part = lax.dynamic_slice_in_dim(query_rows[sequence], offset, block_rows, 0)
        grad_part = lax.dynamic_slice_in_dim(grad_heads[sequence], offset, block_rows, 0)
        scores = block_scores(query_part, key_rows[sequence], offset)
        probability = jnp.exp(scores - log_total[block_index][..., None])
        grad_prob = jnp.einsum(
            "qhd,khd->hqk", grad_part, value_rows[sequence], preferred_element_type=jnp.float32
        )
        inner_sum = jnp.sum(probability * grad_prob, -1, keepdims=True)
        grad_scores = (probability * (grad_prob - inner_sum)).astype(jnp.bfloat16)
        grad_query = jnp.einsum(
            "hqk,khd->qhd", grad_scores, key_rows[sequence], preferred_element_type=jnp.float32
        ) * HDIM ** (-0.5)
        grad_keys = jnp.einsum(
            "hqk,qhd->khd", grad_scores, query_part, preferred_element_type=jnp.float32
        ) * HDIM ** (-0.5)
        grad_values = jnp.einsum(
            "hqk,qhd->khd",
            probability.astype(jnp.bfloat16),
            grad_part,
            preferred_element_type=jnp.float32,
        )
        return (grad_query, grad_keys, grad_values)

    grad_query, grad_keys, grad_values = lax.map(one_block, jnp.arange(count_seq * block_count))
    grad_query = grad_query.reshape(count_seq, SEQ_LEN, HEADS, HDIM)
    grad_keys = jnp.sum(grad_keys.reshape(count_seq, block_count, SEQ_LEN, HEADS, HDIM), 1)
    grad_values = jnp.sum(grad_values.reshape(count_seq, block_count, SEQ_LEN, HEADS, HDIM), 1)
    return jnp.stack([grad_query, grad_keys, grad_values], 2).reshape(count_seq * SEQ_LEN, 3 * D)


def layer_forward(embedded, wattn, wup, wdown, gain_all, count_seq):
    normed_first = layer_norm(embedded, gain_all[0]).astype(jnp.bfloat16)
    projected = jnp.dot(normed_first, wattn[:, : 3 * D], preferred_element_type=jnp.float32).astype(
        jnp.bfloat16
    )
    query_rows, key_rows, value_rows = split_heads(projected, count_seq)
    attended, log_total = attention_forward(query_rows, key_rows, value_rows)
    branch = jnp.dot(attended, wattn[:, 3 * D :], preferred_element_type=jnp.float32)
    middle = embedded + branch
    normed_second = layer_norm(middle, gain_all[1]).astype(jnp.bfloat16)
    hidden = jnp.dot(normed_second, wup, preferred_element_type=jnp.float32)
    active = gelu_tanh(hidden).astype(jnp.bfloat16)
    second = jnp.dot(active, wdown, preferred_element_type=jnp.float32)
    result = middle + second
    saved = (normed_first, projected, attended, log_total, middle, normed_second, hidden, active)
    return (result, branch, second, saved)


def layer_backward(grad_result, embedded, saved, wattn, wup, wdown, gain_all, count_seq):
    normed_first, projected, attended, log_total, middle, normed_second, hidden, active = saved
    grad_second = grad_result.astype(jnp.bfloat16)
    grad_down = outer(active, grad_second)
    grad_active = inner(grad_second, wdown)
    grad_hidden = jax.vjp(gelu_tanh, hidden)[1](grad_active)[0].astype(jnp.bfloat16)
    grad_up = outer(normed_second, grad_hidden)
    grad_normed = inner(grad_hidden, wup)
    grad_middle, grad_gain_mid = jax.vjp(layer_norm, middle, gain_all[1])[1](grad_normed)
    grad_middle = grad_result + grad_middle
    grad_branch = grad_middle.astype(jnp.bfloat16)
    grad_out_proj = outer(attended, grad_branch)
    grad_attended = inner(grad_branch, wattn[:, 3 * D :]).astype(jnp.bfloat16)
    query_rows, key_rows, value_rows = split_heads(projected, count_seq)
    grad_projected = attention_backward(
        query_rows, key_rows, value_rows, grad_attended, log_total
    ).astype(jnp.bfloat16)
    grad_in_proj = outer(normed_first, grad_projected)
    grad_normed = inner(grad_projected, wattn[:, : 3 * D])
    grad_embedded, grad_gain_first = jax.vjp(layer_norm, embedded, gain_all[0])[1](grad_normed)
    grad_embedded = grad_middle + grad_embedded
    grad_attn = jnp.concatenate([grad_in_proj, grad_out_proj], 1)
    return (grad_embedded, grad_attn, grad_up, grad_down, grad_gain_first, grad_gain_mid)


def renew(weight, moment, average, gradient, factor):
    clipped = gradient * factor
    moment_new = MOMENTUM * moment + clipped
    weight_new = weight - STEP_RATE * (clipped + MOMENTUM * moment_new)
    average_new = AVERAGE_DECAY * average + (1.0 - AVERAGE_DECAY) * weight_new
    return (weight_new, moment_new, average_new)


def shards(
    patches,
    patch_pos,
    owner,
    local_row,
    counts,
    task,
    table,
    table_mom,
    table_avg,
    patch_w,
    patch_mom,
    patch_avg,
    attn_w,
    attn_mom,
    attn_avg,
    up_w,
    up_mom,
    up_avg,
    down_w,
    down_mom,
    down_avg,
    gains,
    gain_mom,
    gain_avg,
):
    wpatch, wattn, wup, wdown, wgain = (
        lax.all_gather(patch_w.astype(jnp.bfloat16), ("dp", "mp"), axis=0, tiled=True),
        lax.all_gather(attn_w.astype(jnp.bfloat16), ("dp", "mp"), axis=0, tiled=True),
        lax.all_gather(up_w.astype(jnp.bfloat16), ("dp", "mp"), axis=0, tiled=True),
        lax.all_gather(down_w.astype(jnp.bfloat16), ("dp", "mp"), axis=0, tiled=True),
        lax.all_gather(gains.astype(jnp.bfloat16), ("dp", "mp"), axis=1, tiled=True),
    )
    gain_all = wgain.astype(jnp.float32)
    table_shard = lax.all_gather(table.astype(jnp.bfloat16), "dp", axis=0, tiled=True)
    owners = lax.axis_size("mp")
    tokens_here = patches.shape[0]
    count_seq = tokens_here // SEQ_LEN
    capacity = 3 * tokens_here // (2 * owners)
    vocab_here = table_shard.shape[0]
    place = lax.axis_index("dp") * owners + lax.axis_index("mp")
    my_counts = lax.dynamic_slice_in_dim(counts, place * count_seq, count_seq, 0)
    positions = jnp.arange(SEQ_LEN, dtype=jnp.int32)[None, :]
    first_tok = my_counts[:, 0:1]
    alive = my_counts[:, 1:2]
    is_patch = (positions < first_tok).reshape(tokens_here, 1)
    is_token = ((positions >= first_tok) & (positions < first_tok + alive)).reshape(tokens_here)
    is_valid = (positions < first_tok + alive).reshape(tokens_here, 1)
    target_owner = owner[:, 0]
    choose = ((target_owner[:, None] == jnp.arange(owners)[None, :]) & is_token[:, None]).astype(
        jnp.int32
    )
    slot_rank = jnp.sum(choose * (jnp.cumsum(choose, 0) - 1), 1)
    flat_slot = jnp.where(is_token, target_owner * capacity + slot_rank, owners * capacity)
    send_ids = (
        jnp.full((owners * capacity,), -1, jnp.int32).at[flat_slot].set(local_row, mode="drop")
    )
    received = lax.all_to_all(
        send_ids.reshape(owners, capacity), "mp", split_axis=0, concat_axis=0, tiled=True
    )
    found = jnp.where(
        (received >= 0)[..., None],
        table_shard[jnp.maximum(received, 0)],
        jnp.zeros((), jnp.bfloat16),
    )
    fetched = lax.all_to_all(found, "mp", split_axis=0, concat_axis=0, tiled=True)
    safe_slot = jnp.minimum(flat_slot, owners * capacity - 1)
    looked = jnp.where(
        is_token[:, None],
        fetched.reshape(owners * capacity, D)[safe_slot],
        jnp.zeros((), jnp.bfloat16),
    )
    position_code = (patch_pos[:, None] == jnp.arange(POSN)[None, :]).astype(jnp.bfloat16)
    patch_in = jnp.concatenate([patches, position_code], 1)
    from_patch = jnp.dot(patch_in, wpatch, preferred_element_type=jnp.float32)
    embed_scale = math.sqrt(D)
    embedded = jnp.where(is_patch, from_patch, 0.0) + embed_scale * looked.astype(jnp.float32)
    result, branch, second, saved = layer_forward(embedded, wattn, wup, wdown, gain_all, count_seq)
    final_rows, final_back = jax.vjp(layer_norm, result, gain_all[2])
    pick_rows = (
        jnp.arange(count_seq)[:, None] * SEQ_LEN + first_tok - 1 + jnp.arange(LOSS)[None, :]
    ).reshape(-1)
    own_rows = final_rows[pick_rows].astype(jnp.bfloat16)
    target_rows = looked[pick_rows + 1]
    every_rows = lax.all_gather(own_rows, "mp", axis=0, tiled=True)
    logits = inner(every_rows, table_shard)
    local_top = jnp.max(logits, 1)
    local_sum = jnp.sum(jnp.exp(logits - local_top[:, None]), 1)

    def combine(first_part, second_part):
        joint_top = jnp.maximum(first_part[0], second_part[0])
        joint_sum = first_part[1] * jnp.exp(first_part[0] - joint_top) + second_part[1] * jnp.exp(
            second_part[0] - joint_top
        )
        return (joint_top, joint_sum)

    top_all, sum_all = combined_all((local_top, local_sum), "mp", combine)
    log_total = top_all + jnp.log(sum_all)
    own_count = count_seq * LOSS
    own_total = lax.dynamic_slice_in_dim(log_total, lax.axis_index("mp") * own_count, own_count, 0)
    picked = jnp.sum(own_rows.astype(jnp.float32) * target_rows.astype(jnp.float32), 1)
    scored_all = counts[:, 2].astype(jnp.float32)
    per_task = (task[:, None] == jnp.arange(TASKS)[None, :]).astype(jnp.float32)
    task_total = jnp.sum(per_task * scored_all[:, None], 0)
    present = jnp.sum((task_total > 0).astype(jnp.float32))
    inverse_seq = jnp.sum(per_task / jnp.maximum(task_total, 1.0)[None, :], 1)
    row_live = (jnp.arange(LOSS)[None, :] < counts[:, 2:3]).astype(jnp.float32) * inverse_seq[
        :, None
    ]
    group_weight = lax.dynamic_slice_in_dim(
        row_live, lax.axis_index("dp") * owners * count_seq, owners * count_seq, 0
    ).reshape(-1)
    own_weight = lax.dynamic_slice_in_dim(row_live, place * count_seq, count_seq, 0).reshape(-1)
    loss_part = jnp.sum(own_weight * (own_total - picked))

    def square_sum(values):
        return jnp.sum(jnp.where(is_valid, jnp.mean(values * values, 1, keepdims=True), 0.0))

    stat_sums = jnp.stack(
        [square_sum(embedded), square_sum(branch), square_sum(second), square_sum(result)]
    )
    loss_total, stat_total = lax.psum((loss_part, stat_sums), ("dp", "mp"))
    grad_logits = ((group_weight / present)[:, None] * jnp.exp(logits - log_total[:, None])).astype(
        jnp.bfloat16
    )
    table_head = outer(grad_logits, every_rows)
    grad_rows = lax.psum_scatter(
        jnp.dot(grad_logits, table_shard, preferred_element_type=jnp.float32).astype(jnp.bfloat16),
        "mp",
        scatter_dimension=0,
        tiled=True,
    ).astype(jnp.float32)
    scaled_weight = (own_weight / present)[:, None]
    grad_rows = grad_rows - scaled_weight * target_rows.astype(jnp.float32)
    grad_final = jnp.zeros((tokens_here, D), jnp.float32).at[pick_rows].add(grad_rows)
    grad_result, grad_gain_last = final_back(grad_final)
    grad_embedded, grad_attn, grad_up, grad_down, grad_gain_first, grad_gain_mid = layer_backward(
        grad_result, embedded, saved, wattn, wup, wdown, gain_all, count_seq
    )
    grad_looked = (
        (embed_scale * grad_embedded)
        .at[pick_rows + 1]
        .add(-scaled_weight * own_rows.astype(jnp.float32))
    )
    outgoing = (
        jnp.zeros((owners * capacity, D), jnp.bfloat16)
        .at[flat_slot]
        .set(grad_looked.astype(jnp.bfloat16), mode="drop")
        .reshape(owners, capacity, D)
    )
    incoming = lax.all_to_all(outgoing, "mp", split_axis=0, concat_axis=0, tiled=True)
    safe_ids = jnp.where(received >= 0, received, vocab_here).reshape(-1)
    table_embed = jax.ops.segment_sum(
        incoming.reshape(-1, D).astype(jnp.float32), safe_ids, vocab_here + 1
    )[:vocab_here]
    grad_table = lax.psum_scatter(
        (table_head + table_embed).astype(jnp.bfloat16), "dp", scatter_dimension=0, tiled=True
    ).astype(jnp.float32)
    grad_patch = outer(patch_in, jnp.where(is_patch, grad_embedded, 0.0).astype(jnp.bfloat16))
    grad_gain = jnp.stack([grad_gain_first, grad_gain_mid, grad_gain_last])
    summed_patch, summed_attn, summed_up, summed_down, summed_gain = (
        lax.psum_scatter(grad_patch, ("dp", "mp"), scatter_dimension=0, tiled=True),
        lax.psum_scatter(grad_attn, ("dp", "mp"), scatter_dimension=0, tiled=True),
        lax.psum_scatter(grad_up, ("dp", "mp"), scatter_dimension=0, tiled=True),
        lax.psum_scatter(grad_down, ("dp", "mp"), scatter_dimension=0, tiled=True),
        lax.psum_scatter(grad_gain, ("dp", "mp"), scatter_dimension=1, tiled=True),
    )
    gradient_list = (grad_table, summed_patch, summed_attn, summed_up, summed_down, summed_gain)
    squares = sum((jnp.sum(gradient * gradient) for gradient in gradient_list))
    clip_norm = jnp.sqrt(lax.psum(squares, ("dp", "mp")))
    factor = jnp.minimum(1.0, CLIP_LIMIT / clip_norm)
    states = (
        (table, table_mom, table_avg),
        (patch_w, patch_mom, patch_avg),
        (attn_w, attn_mom, attn_avg),
        (up_w, up_mom, up_avg),
        (down_w, down_mom, down_avg),
        (gains, gain_mom, gain_avg),
    )
    renewed = [
        renew(state[0], state[1], state[2], gradient, factor)
        for state, gradient in zip(states, gradient_list)
    ]
    valid_total = jnp.sum(counts[:, :2].astype(jnp.float32))
    rms_stats = jnp.sqrt(stat_total / valid_total)
    table_out, patch_out, attn_out, up_out, down_out, gain_out = renewed
    return (
        table_out[0],
        table_out[1],
        table_out[2],
        table_out[0].astype(jnp.bfloat16),
        patch_out[0],
        patch_out[1],
        patch_out[2],
        patch_out[0].astype(jnp.bfloat16),
        attn_out[0],
        attn_out[1],
        attn_out[2],
        attn_out[0].astype(jnp.bfloat16),
        up_out[0],
        up_out[1],
        up_out[2],
        up_out[0].astype(jnp.bfloat16),
        down_out[0],
        down_out[1],
        down_out[2],
        down_out[0].astype(jnp.bfloat16),
        gain_out[0],
        gain_out[1],
        gain_out[2],
        loss_total,
        present,
        clip_norm,
        rms_stats,
    )


def solution(mesh):
    in_specs = (
        P(("dp", "mp"), None),
        P(("dp", "mp")),
        P(("dp", "mp"), None),
        P(("dp", "mp")),
        P(),
        P(),
        P(("mp", "dp"), None),
        P(("mp", "dp"), None),
        P(("mp", "dp"), None),
        P(("dp", "mp"), None),
        P(("dp", "mp"), None),
        P(("dp", "mp"), None),
        P(("dp", "mp"), None),
        P(("dp", "mp"), None),
        P(("dp", "mp"), None),
        P(("dp", "mp"), None),
        P(("dp", "mp"), None),
        P(("dp", "mp"), None),
        P(("dp", "mp"), None),
        P(("dp", "mp"), None),
        P(("dp", "mp"), None),
        P(None, ("dp", "mp")),
        P(None, ("dp", "mp")),
        P(None, ("dp", "mp")),
    )
    out_specs = (
        P(("mp", "dp"), None),
        P(("mp", "dp"), None),
        P(("mp", "dp"), None),
        P(("mp", "dp"), None),
        P(("dp", "mp"), None),
        P(("dp", "mp"), None),
        P(("dp", "mp"), None),
        P(("dp", "mp"), None),
        P(("dp", "mp"), None),
        P(("dp", "mp"), None),
        P(("dp", "mp"), None),
        P(("dp", "mp"), None),
        P(("dp", "mp"), None),
        P(("dp", "mp"), None),
        P(("dp", "mp"), None),
        P(("dp", "mp"), None),
        P(("dp", "mp"), None),
        P(("dp", "mp"), None),
        P(("dp", "mp"), None),
        P(("dp", "mp"), None),
        P(None, ("dp", "mp")),
        P(None, ("dp", "mp")),
        P(None, ("dp", "mp")),
        P(),
        P(),
        P(),
        P(),
    )
    return jax.shard_map(shards, mesh=mesh, in_specs=in_specs, out_specs=out_specs, check_vma=False)
```

profile of v0, /device:TPU:0, one launch (start us, length us, event | category | flops | bytes accessed | tf_op | source)
XLA Modules:
  0.0 1491.0 jit_solution(6429187516079355673)
XLA Ops:
  23.0 7.8 all_to_all.22
  31.4 159.8 %all-gather.11.cloned.1.call-done = bf16[8256,768]{1,0:T(8,128)(2,1)} async-done(((bf16[1032,768]{1,0:T(8,128)(2,1)}), bf16[8256,768]{1,0:T(8,128)(2,1)}) %all-gather.11.cloned.1.call-update) | async-done | bytes 12681232 | tf_op jit(solution)/shard_map/all_gather | solution.py:217
  191.2 12.3 gather_fusion
  210.5 59.7 %all-gather.3 = bf16[32,24,3]{1,2,0:T(4,128)(2,1)S(1)} all-gather(bf16[1,24,3]{1,2,0:T(4,128)(2,1)S(1)} %convert_bitcast_fusion.3), channel_id=1, replica_groups=mesh['dp'=8,'mp'=4] {'dp','mp'}, dimensions={0}, use_global_device_ids=true | all-gather | bytes 4752 | tf_op jit(solution)/shard_map/all_gather | solution.py:214
  288.3 26.6 %all-gather.13.cloned.1.call-done = bf16[768,3072]{1,0:T(8,128)(2,1)} async-done(((bf16[24,3072]{1,0:T(8,128)(2,1)}), bf16[768,3072]{1,0:T(8,128)(2,1)}) %all-gather.13.cloned.1.call-update) | async-done | bytes 4718608 | tf_op jit(solution)/shard_map/all_gather | solution.py:211
  314.9 7.7 convolution_convert_fusion
  322.7 6.7 copy.112
  334.1 138.9 %while.42 = (s32[]{:T(128)}, bf16[2,512,24,32]{1,3,2,0:T(8,128)(2,1)}, f32[2,24,512]{2,1,0:T(8,128)S(1)}, s32[2]{0:T(128)S(1)}, bf16[1,1024,24,32]{1,3,2,0:T(8,1...) while((s32[]{:T(128)}, ...), condition=%wide.region_12.13_spmd, body=%wide.region_9.12_spmd.sunk | while | flops 1762513408 | bytes 177082768 | solution.py:89
  337.3 22.1 %fusion.165 = (f32[24,512]{1,0:T(8,128)S(1)}, f32[24,512,1024]{2,1,0:T(8,128)}) fusion(pred[512,1024]{1,0:T(8,128)(4,1)S(1)} %iota_compare_fusion.12, bf16[1,1024,24,32]{1,3,2,0:T(8,128)(2,1)S(1)} %get-tuple-element.578, bf16[1,1024,24,32]{1,3,2,0:T(8,128)(2,1)} %get-tuple-element.577, s32[]{:T(128)S(6)} %select_n.247), kind=kOutput, calls=%fused_computation.12.clone.1 | convolution fusion | flops 843042816 | bytes 53264388 | tf_op jit(solution)/shard_map/while/body/eval_jaxpr/qhd,khd->hqk/dot_general | solution.py:56
  359.4 23.0 %fusion.166 = f32[24,512]{1,0:T(8,128)S(1)} fusion(f32[24,512,1024]{2,1,0:T(8,128)} %get-tuple-element.526, f32[24,512]{1,0:T(8,128)S(1)} %get-tuple-element.527, pred[512,1024]{1,0:T(8,128)(4,1)S(1)} %iota_compare_fusion.12), kind=kLoop, calls=%fused_computation.13.clone.1 | loop fusion | flops 50319360 | bytes 50954240 | tf_op jit(solution)/shard_map/while/body/eval_jaxpr/reduce_sum | solution.py:82
  382.4 20.0 %fusion.167 = bf16[2,512,24,32]{1,3,2,0:T(8,128)(2,1)S(1)} fusion(bf16[2,512,24,32]{1,3,2,0:T(8,128)(2,1)S(1)} %copy-done.28, s32[]{:T(128)S(6)} %copy.178, bf16[1,1024,24,32]{1,3,2,0:T(8,128)(2,1)S(1)} %copy-done.3, f32[24,512,1024]{2,1,0:T(8,128)} %get-tuple-element.526, f32[24,512]{1,0:T(8,128)S(1)} %fusion.166, ...), kind=kOutput, calls=%fused_computation.21.clone.1 | convolution fusion | flops 868614144 | bytes 53313540 | tf_op jit(solution)/shard_map/while/body/eval_jaxpr/hqk,khd->qhd/dot_general | solution.py:84
  406.5 22.8 %fusion.165 = (f32[24,512]{1,0:T(8,128)S(1)}, f32[24,512,1024]{2,1,0:T(8,128)}) fusion(pred[512,1024]{1,0:T(8,128)(4,1)S(1)} %iota_compare_fusion.12, bf16[1,1024,24,32]{1,3,2,0:T(8,128)(2,1)S(1)} %get-tuple-element.578, bf16[1,1024,24,32]{1,3,2,0:T(8,128)(2,1)} %get-tuple-element.577, s32[]{:T(128)S(6)} %select_n.247), kind=kOutput, calls=%fused_computation.12.clone.1 | convolution fusion | flops 843042816 | bytes 53264388 | tf_op jit(solution)/shard_map/while/body/eval_jaxpr/qhd,khd->hqk/dot_general | solution.py:56
  429.3 22.3 %fusion.166 = f32[24,512]{1,0:T(8,128)S(1)} fusion(f32[24,512,1024]{2,1,0:T(8,128)} %get-tuple-element.526, f32[24,512]{1,0:T(8,128)S(1)} %get-tuple-element.527, pred[512,1024]{1,0:T(8,128)(4,1)S(1)} %iota_compare_fusion.12), kind=kLoop, calls=%fused_computation.13.clone.1 | loop fusion | flops 50319360 | bytes 50954240 | tf_op jit(solution)/shard_map/while/body/eval_jaxpr/reduce_sum | solution.py:82
  451.6 19.9 %fusion.167 = bf16[2,512,24,32]{1,3,2,0:T(8,128)(2,1)S(1)} fusion(bf16[2,512,24,32]{1,3,2,0:T(8,128)(2,1)S(1)} %copy-done.28, s32[]{:T(128)S(6)} %copy.178, bf16[1,1024,24,32]{1,3,2,0:T(8,128)(2,1)S(1)} %copy-done.3, f32[24,512,1024]{2,1,0:T(8,128)} %get-tuple-element.526, f32[24,512]{1,0:T(8,128)S(1)} %fusion.166, ...), kind=kOutput, calls=%fused_computation.21.clone.1 | convolution fusion | flops 868614144 | bytes 53313540 | tf_op jit(solution)/shard_map/while/body/eval_jaxpr/hqk,khd->qhd/dot_general | solution.py:84
  482.0 10.5 fusion.117
  492.5 12.5 fusion.129
  517.2 16.2 %all-gather.19.cloned.1.call-done = bf16[1024,768]{1,0:T(8,128)(2,1)} async-done(((bf16[256,768]{1,0:T(8,128)(2,1)}), bf16[1024,768]{1,0:T(8,128)(2,1)}) %all-gather.19.cloned.1.call-update) | async-done | bytes 1572880 | tf_op jit(solution)/shard_map/all_gather | solution.py:267
  533.4 22.8 %fusion.133 = (f32[1024]{0:T(1024)S(1)}, f32[1024,8256]{0,1:T(8,128)}) fusion(bf16[1024,768]{1,0:T(8,128)(2,1)} %all-gather.19.cloned.1.call-done, bf16[8256,768]{1,0:T(8,128)(2,1)} %all-gather.11.cloned.1.call-done), kind=kOutput, calls=%fused_computation.277 | convolution fusion | flops 12994018304 | bytes 48074752 | tf_op jit(solution)/shard_map/dot_general | solution.py:50
  561.4 13.3 exponential_reduce_fusion
  580.3 24.4 %fusion.69 = bf16[1024,768]{1,0:T(8,128)(2,1)} fusion(bf16[8256,768]{1,0:T(8,128)(2,1)} %all-gather.11.cloned.1.call-done, f32[1024,8256]{0,1:T(8,128)} %get-tuple-element.392, f32[1024]{0:T(1024)S(1)} %log_add_fusion, f32[1024]{0:T(1024)S(1)} %bitcast.236), kind=kOutput, calls=%fused_computation.122 | convolution fusion | flops 13011714048 | bytes 48078848 | tf_op jit(solution)/shard_map/dot_general | solution.py:310
  616.2 16.8 %reduce-scatter.9.cloned.1.call-done = bf16[256,768]{1,0:T(8,128)(2,1)} async-done(((bf16[1024,768]{1,0:T(8,128)(2,1)}), bf16[256,768]{1,0:T(8,128)(2,1)}) %reduce-scatter.9.cloned.1.call-update) | async-done | bytes 393232 | tf_op jit(solution)/shard_map/reduce_scatter | solution.py:309
  649.0 13.5 fusion.89
  662.6 17.3 %fusion.58 = bf16[1024,3072]{1,0:T(8,128)(2,1)S(1)} fusion(f32[1024,3072]{1,0:T(8,128)} %fusion.117, bf16[3072,768]{1,0:T(8,128)(2,1)} %all-gather.17.cloned.1.call-done, f32[1024,768]{0,1:T(8,128)} %copy-done.16, f32[1024]{0:T(1024)S(1)} %negate_multiply_fusion.2), kind=kOutput, calls=%fused_computation.78 | convolution fusion | flops 4896325632 | bytes 26742784 | tf_op jit(solution)/shard_map/dot_general | solution.py:50
  679.9 7.3 multiply_reduce_fusion.9
  692.1 7.6 fusion.116
  704.9 308.6 %while.44 = (s32[]{:T(128)}, bf16[2,512,24,32]{1,3,2,0:T(8,128)(2,1)}, f32[2,1024,24,32]{1,3,2,0:T(8,128)}, f32[2,1024,24,32]{1,3,2,0:T(8,128)}, s32[2]{0:T(128)...) while((s32[]{:T(128)}, ...), condition=%wide.region_29.30_spmd, body=%wide.region_27.29_spmd.sunk | while | flops 4216967680 | bytes 401953152 | solution.py:125
  709.6 21.2 %fusion.176 = f32[24,512,1024]{2,1,0:T(8,128)} fusion(bf16[1,1024,24,32]{1,3,2,0:T(8,128)(2,1)S(1)} %get-tuple-element.639, bf16[1,1024,24,32]{1,3,2,0:T(8,128)(2,1)} %get-tuple-element.638, s32[]{:T(128)S(6)} %select_n.252), kind=kOutput, calls=%fused_computation.46.clone.1 | convolution fusion | flops 805306368 | bytes 52690948 | tf_op jit(solution)/shard_map/while/body/eval_jaxpr/qhd,khd->hqk/dot_general | solution.py:56
  730.8 22.4 %bitcast_dynamic-update-slice_fusion.11 = f32[2,1024,24,32]{1,3,2,0:T(8,128)} fusion(f32[2,1024,24,32]{1,3,2,0:T(8,128)} %get-tuple-element.621, s32[]{:T(128)S(6)} %copy.197, f32[24,512,1024]{2,1,0:T(8,128)} %fusion.176, f32[24,512]{1,0:T(8,128)S(1)} %dynamic-slice_bitcast_fusion.2, pred[512,1024]{1,0:T(8,128)(4,1)S(1)} %iota_compare_fusion.13, ...), kind=kOutput, calls=%fused_computation.38.clone.1 | convolution fusion | flops 855638016 | bytes 54837256 | tf_op jit(solution)/shard_map/while/body/eval_jaxpr/hqk,qhd->khd/dot_general | solution.py:117
  753.2 36.3 %multiply_reduce_fusion.21 = (f32[24,512]{1,0:T(8,128)S(1)}, f32[24,512,1024]{2,1,0:T(8,128)}) fusion(f32[24,512,1024]{2,1,0:T(8,128)} %fusion.176, f32[24,512]{1,0:T(8,128)S(1)} %dynamic-slice_bitcast_fusion.2, pred[512,1024]{1,0:T(8,128)(4,1)S(1)} %iota_compare_fusion.13, bf16[1,1024,24,32]{1,3,2,0:T(8,128)(2,1)} %get-tuple-element.642, ...), kind=kOutput, calls=%fused_computation.33.clone.1 | convolution fusion | flops 868208640 | bytes 103645184 | tf_op jit(solution)/shard_map/while/body/eval_jaxpr/qhd,khd->hqk/dot_general | solution.py:106
  789.5 43.0 %multiply_convert_fusion.16 = bf16[24,512,1024]{2,1,0:T(8,128)(2,1)} fusion(f32[24,512,1024]{2,1,0:T(8,128)} %get-tuple-element.547, f32[24,512,1024]{2,1,0:T(8,128)} %fusion.176, f32[24,512]{1,0:T(8,128)S(1)} %get-tuple-element.548, f32[24,512]{1,0:T(8,128)S(1)} %dynamic-slice_bitcast_fusion.2, pred[512,1024]{1,0:T(8,128)(4,1)S(1)} %iota_compare_fusion.13), kind=kLoop, calls=%fused_computation.32.clone.1 | loop fusion | flops 75497472 | bytes 126451712 | tf_op jit(solution)/shard_map/while/body/eval_jaxpr/convert_element_type | solution.py:110
  832.5 14.1 bitcast_dynamic-update-slice_fusion.9
  846.7 14.3 bitcast_dynamic-update-slice_fusion.10
  865.2 21.5 %fusion.176 = f32[24,512,1024]{2,1,0:T(8,128)} fusion(bf16[1,1024,24,32]{1,3,2,0:T(8,128)(2,1)S(1)} %get-tuple-element.639, bf16[1,1024,24,32]{1,3,2,0:T(8,128)(2,1)} %get-tuple-element.638, s32[]{:T(128)S(6)} %select_n.252), kind=kOutput, calls=%fused_computation.46.clone.1 | convolution fusion | flops 805306368 | bytes 52690948 | tf_op jit(solution)/shard_map/while/body/eval_jaxpr/qhd,khd->hqk/dot_general | solution.py:56
  886.7 22.4 %bitcast_dynamic-update-slice_fusion.11 = f32[2,1024,24,32]{1,3,2,0:T(8,128)} fusion(f32[2,1024,24,32]{1,3,2,0:T(8,128)} %get-tuple-element.621, s32[]{:T(128)S(6)} %copy.197, f32[24,512,1024]{2,1,0:T(8,128)} %fusion.176, f32[24,512]{1,0:T(8,128)S(1)} %dynamic-slice_bitcast_fusion.2, pred[512,1024]{1,0:T(8,128)(4,1)S(1)} %iota_compare_fusion.13, ...), kind=kOutput, calls=%fused_computation.38.clone.1 | convolution fusion | flops 855638016 | bytes 54837256 | tf_op jit(solution)/shard_map/while/body/eval_jaxpr/hqk,qhd->khd/dot_general | solution.py:117
  909.2 36.5 %multiply_reduce_fusion.21 = (f32[24,512]{1,0:T(8,128)S(1)}, f32[24,512,1024]{2,1,0:T(8,128)}) fusion(f32[24,512,1024]{2,1,0:T(8,128)} %fusion.176, f32[24,512]{1,0:T(8,128)S(1)} %dynamic-slice_bitcast_fusion.2, pred[512,1024]{1,0:T(8,128)(4,1)S(1)} %iota_compare_fusion.13, bf16[1,1024,24,32]{1,3,2,0:T(8,128)(2,1)} %get-tuple-element.642, ...), kind=kOutput, calls=%fused_computation.33.clone.1 | convolution fusion | flops 868208640 | bytes 103645184 | tf_op jit(solution)/shard_map/while/body/eval_jaxpr/qhd,khd->hqk/dot_general | solution.py:106
  945.7 40.3 %multiply_convert_fusion.16 = bf16[24,512,1024]{2,1,0:T(8,128)(2,1)} fusion(f32[24,512,1024]{2,1,0:T(8,128)} %get-tuple-element.547, f32[24,512,1024]{2,1,0:T(8,128)} %fusion.176, f32[24,512]{1,0:T(8,128)S(1)} %get-tuple-element.548, f32[24,512]{1,0:T(8,128)S(1)} %dynamic-slice_bitcast_fusion.2, pred[512,1024]{1,0:T(8,128)(4,1)S(1)} %iota_compare_fusion.13), kind=kLoop, calls=%fused_computation.32.clone.1 | loop fusion | flops 75497472 | bytes 126451712 | tf_op jit(solution)/shard_map/while/body/eval_jaxpr/convert_element_type | solution.py:110
  986.0 13.2 bitcast_dynamic-update-slice_fusion.9
  999.2 14.2 bitcast_dynamic-update-slice_fusion.10
  1039.8 8.8 pad_maximum_fusion
  1048.6 7.9 multiply_reduce_fusion.7
  1067.9 7.0 scatter_custom_fusion.3
  1078.8 33.0 %all-to-all-done.2 = bf16[4,384,768]{2,1,0:T(8,128)(2,1)S(1)} async-done(((bf16[4,384,768]{2,1,0:T(8,128)(2,1)}), bf16[4,384,768]{2,1,0:T(8,128)(2,1)S(1)}, u32[]{:S(2)}, u32[]{:S(2)}) %all-to-all-start.2) | async-done | bytes 2359328 | tf_op jit(solution)/shard_map/all_to_all | solution.py:333
  1111.9 21.9 %scatter_custom_fusion.4 = f32[8257,768]{1,0:T(8,128)} fusion(s32[1536]{0:T(1024)S(1)} %fusion.100, f32[]{:T(128)} %constant.241.clone.1, bf16[1536,768]{1,0:T(8,128)(2,1)S(1)} %bitcast.214), kind=kCustom, calls=%fused_computation.70 | custom fusion | flops 2359296 | bytes 27724804 | tf_op jit(solution)/shard_map/scatter-add | solution.py:335
  1133.8 28.1 %fusion.49 = bf16[8256,768]{1,0:T(8,128)(2,1)} fusion(f32[8257,768]{1,0:T(8,128)} %scatter_custom_fusion.4, bf16[1024,768]{1,0:T(8,128)(2,1)} %all-gather.19.cloned.1.call-done, f32[1024,8256]{0,1:T(8,128)} %get-tuple-element.392, f32[1024]{0:T(1024)S(1)} %copy-done.80, f32[1024]{0:T(1024)S(1)} %bitcast.237), kind=kOutput, calls=%fused_computation.67 | convolution fusion | flops 13023608832 | bytes 73441280 | tf_op jit(solution)/shard_map/dot_general | solution.py:44
  1170.0 101.7 %fusion = f32[32,768]{1,0:T(8,128)S(1)} fusion(f32[896,768]{1,0:T(8,128)} %fusion.70), kind=kCustom, calls=%all-reduce-scatter | all-reduce-scatter fusion | flops 786433 | bytes 2850816
  1277.8 45.8 %all-reduce.1 = f32[3,768]{1,0:T(4,128)S(1)} all-reduce(f32[3,768]{1,0:T(4,128)S(1)} %pad_maximum_fusion.5), channel_id=10, replica_groups=mesh['dp'=8,'mp'=4] {'dp','mp'}, use_global_device_ids=true, to_apply=%region_50.51.clone | all-reduce | flops 2304 | bytes 18432
  1334.6 81.2 %reduce-scatter.11.cloned.1.call-done = bf16[1032,768]{1,0:T(8,128)(2,1)} async-done(((bf16[8256,768]{1,0:T(8,128)(2,1)}), bf16[1032,768]{1,0:T(8,128)(2,1)}) %reduce-scatter.11.cloned.1.call-update) | async-done | bytes 1585168 | tf_op jit(solution)/shard_map/reduce_scatter | solution.py:338
  1422.7 39.6 %all-reduce.3 = (f32[]{:T(128)}, f32[]{:T(128)}, f32[4]{0:T(128)}) all-reduce(f32[]{:T(128)S(6)} %add.400, f32[]{:T(128)} %get-tuple-element.386, f32[4]{0:T(128)S(1)} %pad_maximum_fusion.6), channel_id=1, replica_groups=mesh['dp'=8,'mp'=4] {'dp','mp'}, use_global_device_ids=true, to_apply=%region_52.53 | all-reduce | flops 6 | bytes 48 | tf_op jit(solution)/shard_map/psum | solution.py:352
  (403 shorter events, 208.2 us)
Async XLA Ops:
  7.3 184.0 %all-gather.11.cloned.1.call-start = ((), (), s32[]{:S(2)}) async-start(), calls=%async_computation.8 | async-start | bytes 14266368 | tf_op jit(solution)/shard_map/all_gather | solution.py:217
  10.6 262.1 %all-gather.21.cloned.1.call-start = ((), (), s32[]{:S(2)}) async-start(), calls=%async_computation.18 | async-start | bytes 1622016 | tf_op jit(solution)/shard_map/all_gather | solution.py:210
  11.4 303.6 %all-gather.13.cloned.1.call-start = ((), (), s32[]{:S(2)}) async-start(), calls=%async_computation.9 | async-start | bytes 4866048 | tf_op jit(solution)/shard_map/all_gather | solution.py:211
  12.1 469.6 %all-gather.15.cloned.1.call-start = ((), (), s32[]{:S(2)}) async-start(), calls=%async_computation.10 | async-start | bytes 4866048 | tf_op jit(solution)/shard_map/all_gather | solution.py:212
  18.5 185.1 %copy-start.84 = (s32[1024,1]{0,1:T(1,128)}, s32[1024,1]{0,1:T(1,128)S(1)}, u32[]{:S(2)}) copy-start(s32[1024,1]{0,1:T(1,128)S(1)} %compare_select_fusion.2) | copy-start | bytes 12292
  205.2 67.2 %copy-start.81 = (s32[1024]{0:T(1024)S(1)}, s32[1024]{0:T(1024)}, u32[]{:S(2)}) copy-start(s32[1024]{0:T(1024)} %param.31) | copy-start | bytes 12292
  205.2 70.8 %all-to-all-start.1 = ((bf16[4,384,768]{2,1,0:T(8,128)(2,1)}), bf16[4,384,768]{2,1,0:T(8,128)(2,1)S(1)}, u32[]{:S(2)}, u32[]{:S(2)}) async-start(bf16[4,384,768]{2,1,0:T(8,128)(2,1)} %broadcast_select_fusion), calls=%async_computation.1 | async-start | bytes 4718592 | tf_op jit(solution)/shard_map/all_to_all | solution.py:248
  209.0 283.5 %all-gather.17.cloned.1.call-start = ((), (), s32[]{:S(2)}) async-start(), calls=%async_computation.11 | async-start | bytes 4866048 | tf_op jit(solution)/shard_map/all_gather | solution.py:213
  209.8 323.6 %all-gather.19.cloned.1.call-start = ((), (), s32[]{:S(2)}) async-start(), calls=%async_computation.12 | async-start | bytes 1966080 | tf_op jit(solution)/shard_map/all_gather | solution.py:267
  272.4 42.5 %copy-start.76 = (f32[768]{0:T(1024)}, f32[768]{0:T(1024)S(1)}, u32[]{:S(2)}) copy-start(f32[768]{0:T(1024)S(1)} %get-tuple-element.291) | copy-start | bytes 9220
  287.0 35.7 %copy-start.9 = (f32[1024,768]{0,1:T(8,128)}, f32[1024,768]{0,1:T(8,128)S(1)}, u32[]{:S(2)}) copy-start(f32[1024,768]{0,1:T(8,128)S(1)} %get-tuple-element.390) | copy-start | bytes 9437188
  287.0 35.7 %copy-start.62 = (f32[1024]{0:T(1024)}, f32[1024]{0:T(1024)S(1)}, u32[]{:S(2)}) copy-start(f32[1024]{0:T(1024)S(1)} %broadcast_multiply_fusion.3) | copy-start | bytes 12292
  288.3 34.4 %copy-start.73 = (f32[1024]{0:T(1024)}, f32[1024]{0:T(1024)S(1)}, u32[]{:S(2)}) copy-start(f32[1024]{0:T(1024)S(1)} %fusion.107) | copy-start | bytes 12292
  359.4 23.0 %copy-start.3 = (bf16[1,1024,24,32]{1,3,2,0:T(8,128)(2,1)S(1)}, bf16[1,1024,24,32]{1,3,2,0:T(8,128)(2,1)}, u32[]{:S(2)}) copy-start(bf16[1,1024,24,32]{1,3,2,0:T(8,128)(2,1)} %get-tuple-element.579) | copy-start | bytes 4718596 | tf_op jit(solution)/shard_map/while
  359.4 23.0 %copy-start.28 = (bf16[2,512,24,32]{1,3,2,0:T(8,128)(2,1)S(1)}, bf16[2,512,24,32]{1,3,2,0:T(8,128)(2,1)}, u32[]{:S(2)}) copy-start(bf16[2,512,24,32]{1,3,2,0:T(8,128)(2,1)} %get-tuple-element.562) | copy-start | bytes 4718596 | tf_op jit(solution)/shard_map/while
  429.3 22.3 %copy-start.3 = (bf16[1,1024,24,32]{1,3,2,0:T(8,128)(2,1)S(1)}, bf16[1,1024,24,32]{1,3,2,0:T(8,128)(2,1)}, u32[]{:S(2)}) copy-start(bf16[1,1024,24,32]{1,3,2,0:T(8,128)(2,1)} %get-tuple-element.579) | copy-start | bytes 4718596 | tf_op jit(solution)/shard_map/while
  429.3 22.3 %copy-start.28 = (bf16[2,512,24,32]{1,3,2,0:T(8,128)(2,1)S(1)}, bf16[2,512,24,32]{1,3,2,0:T(8,128)(2,1)}, u32[]{:S(2)}) copy-start(bf16[2,512,24,32]{1,3,2,0:T(8,128)(2,1)} %get-tuple-element.562) | copy-start | bytes 4718596 | tf_op jit(solution)/shard_map/while
  514.8 118.3 %reduce-scatter.9.cloned.1.call-start = ((), (), s32[]{:S(2)}) async-start(), calls=%async_computation.13 | async-start | bytes 1966080 | tf_op jit(solution)/shard_map/reduce_scatter | solution.py:309
  517.2 63.1 %copy-start.85 = (f32[1,2,4,128]{3,1,2,0:T(2,128)}, f32[1,2,4,128]{3,1,2,0:T(2,128)S(1)}, u32[]{:S(2)}) copy-start(f32[1,2,4,128]{3,1,2,0:T(2,128)S(1)} %copy.164) | copy-start | bytes 12292
  580.3 24.4 %copy-start.79 = (f32[1024]{0:T(1024)}, f32[1024]{0:T(1024)S(1)}, u32[]{:S(2)}) copy-start(f32[1024]{0:T(1024)S(1)} %log_add_fusion) | copy-start | bytes 12292
  604.7 724.8 %reduce-scatter.17.cloned.1.call-start = ((), (), s32[]{:S(2)}) async-start(), calls=%async_computation.17 | async-start | bytes 9732096 | tf_op jit(solution)/shard_map/reduce_scatter | solution.py:347
  662.5 668.7 %reduce-scatter.15.cloned.1.call-start = ((), (), s32[]{:S(2)}) async-start(), calls=%async_computation.16 | async-start | bytes 9732096 | tf_op jit(solution)/shard_map/reduce_scatter | solution.py:346
  699.8 633.1 %reduce-scatter.13.cloned.1.call-start = ((), (), s32[]{:S(2)}) async-start(), calls=%async_computation.15 | async-start | bytes 9732096 | tf_op jit(solution)/shard_map/reduce_scatter | solution.py:345
  832.5 14.1 copy-start.2
  986.0 13.2 copy-start.2
  1075.0 36.9 %all-to-all-start.2 = ((bf16[4,384,768]{2,1,0:T(8,128)(2,1)}), bf16[4,384,768]{2,1,0:T(8,128)(2,1)S(1)}, u32[]{:S(2)}, u32[]{:S(2)}) async-start(bf16[4,384,768]{2,1,0:T(8,128)(2,1)} %bitcast.216), calls=%async_computation.3 | async-start | bytes 4718592 | tf_op jit(solution)/shard_map/all_to_all | solution.py:333
  1078.7 337.1 %reduce-scatter.11.cloned.1.call-start = ((), (), s32[]{:S(2)}) async-start(), calls=%async_computation.14 | async-start | bytes 14266368 | tf_op jit(solution)/shard_map/reduce_scatter | solution.py:338
  1111.9 21.9 %copy-start.80 = (f32[1024]{0:T(1024)S(1)}, f32[1024]{0:T(1024)}, u32[]{:S(2)}) copy-start(f32[1024]{0:T(1024)} %copy-done.79) | copy-start | bytes 12292
  1111.9 21.9 %copy-start.86 = (f32[1,2,4,128]{3,1,2,0:T(2,128)S(1)}, f32[1,2,4,128]{3,1,2,0:T(2,128)}, u32[]{:S(2)}) copy-start(f32[1,2,4,128]{3,1,2,0:T(2,128)} %copy-done.85) | copy-start | bytes 12292
  1164.3 111.5 %copy-start.71 = (f32[768]{0:T(1024)S(1)}, f32[768]{0:T(1024)}, u32[]{:S(2)}) copy-start(f32[768]{0:T(1024)} %get-tuple-element.285) | copy-start | bytes 9220
  1164.3 111.5 %copy-start.72 = (f32[768]{0:T(1024)S(1)}, f32[768]{0:T(1024)}, u32[]{:S(2)}) copy-start(f32[768]{0:T(1024)} %get-tuple-element.281) | copy-start | bytes 9220
  1164.4 159.9 %copy-start.75 = (f32[1024]{0:T(1024)S(1)}, f32[1024]{0:T(1024)}, u32[]{:S(2)}) copy-start(f32[1024]{0:T(1024)} %get-tuple-element.288) | copy-start | bytes 12292
  1170.0 293.1 %copy-start.50 = (f32[28,768]{1,0:T(8,128)S(1)}, f32[28,768]{1,0:T(8,128)}, u32[]{:S(2)}) copy-start(f32[28,768]{1,0:T(8,128)} %param.39) | copy-start | bytes 258052
  1170.0 299.6 %copy-start.36 = (f32[24,3072]{1,0:T(8,128)S(1)}, f32[24,3072]{1,0:T(8,128)}, u32[]{:S(2)}) copy-start(f32[24,3072]{1,0:T(8,128)} %param.45) | copy-start | bytes 884740
  1170.0 299.6 %copy-start.55 = (f32[24,3072]{1,0:T(8,128)S(1)}, f32[24,3072]{1,0:T(8,128)}, u32[]{:S(2)}) copy-start(f32[24,3072]{1,0:T(8,128)} %param.46) | copy-start | bytes 884740
  1271.7 198.7 %copy-start.52 = (f32[24,3072]{1,0:T(8,128)S(1)}, f32[24,3072]{1,0:T(8,128)}, u32[]{:S(2)}) copy-start(f32[24,3072]{1,0:T(8,128)} %param.47) | copy-start | bytes 884740
  1271.7 56.5 %collective-permute-start.2 = (f32[32,768]{1,0:T(8,128)S(1)}, f32[32,768]{1,0:T(8,128)S(1)}, u32[]{:S(2)}, u32[]{:S(2)}) collective-permute-start(f32[32,768]{1,0:T(8,128)S(1)} %fusion), channel_id=1, source_target_pairs={{0,3},{1,4},{2,5},{3,6},{4,7},{5,8},{6,9},{7,10},{8,11},{9,12},{10... | collective-permute-start | bytes 294920
  1273.2 55.0 %collective-permute-start.1 = (f32[32,768]{1,0:T(8,128)S(1)}, f32[32,768]{1,0:T(8,128)S(1)}, u32[]{:S(2)}, u32[]{:S(2)}) collective-permute-start(f32[32,768]{1,0:T(8,128)S(1)} %fusion), channel_id=1, source_target_pairs={{0,2},{1,3},{2,4},{3,5},{4,6},{5,7},{6,8},{7,9},{8,10},{9,11},{10,... | collective-permute-start | bytes 294920
  1274.5 53.8 %collective-permute-start = (f32[32,768]{1,0:T(8,128)S(1)}, f32[32,768]{1,0:T(8,128)S(1)}, u32[]{:S(2)}, u32[]{:S(2)}) collective-permute-start(f32[32,768]{1,0:T(8,128)S(1)} %fusion), channel_id=1, source_target_pairs={{0,1},{1,2},{2,3},{3,4},{4,5},{5,6},{6,7},{7,8},{8,9},{9,10},{10,1... | collective-permute-start | bytes 294920
  1276.5 51.7 %collective-permute-start.3 = (f32[28,768]{1,0:T(8,128)S(1)}, f32[28,768]{1,0:T(8,128)S(1)}, u32[]{:S(2)}, u32[]{:S(2)}) collective-permute-start(f32[28,768]{1,0:T(8,128)S(1)} %slice.110), channel_id=1, source_target_pairs={{0,4},{1,5},{2,6},{3,7},{4,8},{5,9},{6,10},{7,11},{8,12},{9,13},{1... | collective-permute-start | bytes 258056
  1328.9 142.3 %copy-start.38 = (f32[24,3072]{1,0:T(8,128)S(1)}, f32[24,3072]{1,0:T(8,128)}, u32[]{:S(2)}) copy-start(f32[24,3072]{1,0:T(8,128)} %param.42) | copy-start | bytes 884740
  1331.2 138.4 %copy-start.42 = (f32[24,3072]{1,0:T(8,128)S(1)}, f32[24,3072]{1,0:T(8,128)}, u32[]{:S(2)}) copy-start(f32[24,3072]{1,0:T(8,128)} %reduce-scatter.15.cloned.1.call-done) | copy-start | bytes 884740
  1332.9 138.3 %copy-start.43 = (f32[24,3072]{1,0:T(8,128)S(1)}, f32[24,3072]{1,0:T(8,128)}, u32[]{:S(2)}) copy-start(f32[24,3072]{1,0:T(8,128)} %reduce-scatter.13.cloned.1.call-done) | copy-start | bytes 884740
  1334.6 139.0 %copy-start.53 = (f32[24,3072]{1,0:T(8,128)S(1)}, f32[24,3072]{1,0:T(8,128)}, u32[]{:S(2)}) copy-start(f32[24,3072]{1,0:T(8,128)} %param.44) | copy-start | bytes 884740
  1415.8 58.5 %copy-start.41 = (f32[96,768]{1,0:T(8,128)S(1)}, f32[96,768]{1,0:T(8,128)}, u32[]{:S(2)}) copy-start(f32[96,768]{1,0:T(8,128)} %reduce-scatter.17.cloned.1.call-done) | copy-start | bytes 884740
  1415.8 60.3 %copy-start.54 = (f32[96,768]{1,0:T(8,128)S(1)}, f32[96,768]{1,0:T(8,128)}, u32[]{:S(2)}) copy-start(f32[96,768]{1,0:T(8,128)} %param.50) | copy-start | bytes 884740
  1418.7 55.6 %copy-start.40 = (f32[96,768]{1,0:T(8,128)S(1)}, f32[96,768]{1,0:T(8,128)}, u32[]{:S(2)}) copy-start(f32[96,768]{1,0:T(8,128)} %param.48) | copy-start | bytes 884740
  1463.0 14.0 copy-start.24
  (69 other events, 304.7 us)
Sparse Core Ops, SparseCore 0:
  10.8 180.3 all-gather.10
  194.6 54.7 all-gather.20
  252.9 61.9 all-gather.12
  318.3 62.4 all-gather.14
  384.1 62.5 all-gather.16
  514.9 18.4 all-gather.18
  604.8 28.1 reduce-scatter.8
  662.6 135.5 reduce-scatter.16
  804.2 134.5 reduce-scatter.14
  1048.7 137.5 reduce-scatter.12
  1189.9 225.8 reduce-scatter.10
where the time goes:
time: 1500 us; the launch traced here: 1490 us
  matrix products  486 us (32%)
  waiting for transfers between devices  334 us (22%)
  other arithmetic  272 us (18%)
  blocking collectives  265 us (18%)
  local copies, waits for them, and re-layouts  84.9 us (6%)
  between operations  23.3 us (2%)
    all_gather x1, waiting for transfers between devices, shards(): lax.all_gather(table.astype(jnp.bfloat16), 'dp', axis=0, tiled=True)  160 us
    unnamed x2, blocking collectives  147 us
    dot_general x4, matrix products, block_scores(): jnp.einsum('qhd,khd->hqk', query_part, key_part, preferred_element_type=j...  87.6 us
    convert_element_type x2, other arithmetic, one_block(): grad_scores = (probability * (grad_prob - inner_sum)).astype(jnp.bfloat16)  83.3 us
    reduce_scatter x1, waiting for transfers between devices, shards(): lax.psum_scatter((table_head + table_embed).astype(jnp.bfloat16), 'dp', s...  81.2 us
    dot_general x2, matrix products, one_block(): jnp.einsum('qhd,khd->hqk', grad_part, value_rows[sequence], preferred_ele...  72.8 us
    dot_general x6, matrix products, outer(): lax.dot_general(left, right, (((0,), (0,)), ((), ())), preferred_element_...  63.8 us
    dot_general x5, matrix products, inner(): lax.dot_general(left, right, (((1,), (1,)), ((), ())), preferred_element_...  60.4 us
  transfers between devices with their start and end apart: 17, of which 6 were waited for; matrix products, arithmetic and copies ran while one was open for 53% of the time, Pallas kernels for 0%

commit v1 on v0

v1 whole, which is shorter than its diff:
```python
import math

import jax
import jax.numpy as jnp
from jax import lax
from jax.experimental import pallas as pl
from jax.experimental.pallas import tpu as pltpu
from jax.sharding import PartitionSpec as P

D = 768
HEADS = 24
HDIM = 32
POSN = 128
SEQ_LEN = 1024
LOSS = 256
TASKS = 32

NORM_EPS = 1e-05
STEP_RATE = 5000.0
MOMENTUM = 0.5
AVERAGE_DECAY = 0.5
CLIP_LIMIT = 0.02

AXES = ("dp", "mp")
LANES = 128
GROUP = LANES // HDIM
TILES = D // LANES
SCALE = HDIM ** (-0.5)
SCALE_LOG2 = SCALE * math.log2(math.e)
VMEM = 56 * 2**20
bf16 = jnp.bfloat16
f32 = jnp.float32


def contract(left, right, left_dim, right_dim):
    return lax.dot_general(
        left, right, (((left_dim,), (right_dim,)), ((), ())), preferred_element_type=f32
    )


def nn(left, right):
    return contract(left, right, 1, 0)


def nt(left, right):
    return contract(left, right, 1, 1)


def tn(left, right):
    return contract(left, right, 0, 0)


def layer_norm(values, gain):
    row_mean = jnp.mean(values, -1, keepdims=True)
    centred = values - row_mean
    spread = jnp.mean(centred * centred, -1, keepdims=True)
    return centred * lax.rsqrt(spread + NORM_EPS) * gain


def gelu_tanh(values):
    return jax.nn.gelu(values, approximate=True)


def head_masks():
    lane = lax.broadcasted_iota(jnp.int32, (1, LANES), 1) // HDIM
    return [lane == head for head in range(GROUP)]


def only(mask, block):
    return jnp.where(mask, block, jnp.zeros((), block.dtype))


def attention_all_kernel(q_ref, k_ref, v_ref, o_ref, *, block):
    length = q_ref.shape[0]
    masks = head_masks()
    row = lax.broadcasted_iota(jnp.int32, (block, block), 0)
    col = lax.broadcasted_iota(jnp.int32, (block, block), 1)
    triangle = col <= row
    for index in range(length // block):
        start, end = index * block, (index + 1) * block
        q = q_ref[start:end, :]
        k, v = k_ref[0:end, :], v_ref[0:end, :]
        joined = jnp.zeros((block, LANES), f32)
        for mask in masks:
            scores = nt(only(mask, q), k)
            diagonal = jnp.where(triangle, scores[:, start:], -1e30)
            scores = jnp.concatenate([scores[:, :start], diagonal], 1) if index else diagonal
            top = jnp.max(scores, 1, keepdims=True) * SCALE_LOG2
            power = jnp.exp2(scores * SCALE_LOG2 - top)
            total = jnp.sum(power, 1, keepdims=True)
            joined = jnp.where(mask, nn(power.astype(bf16), v) / total, joined)
        o_ref[start:end, :] = joined.astype(bf16)


def attention_all(queries, key_values):
    length = queries.shape[0]
    return pl.pallas_call(
        lambda *refs: attention_all_kernel(*refs, block=512),
        grid=(TILES,),
        in_specs=[
            pl.BlockSpec((length, LANES), lambda g: (0, g)),
            pl.BlockSpec((length, LANES), lambda g: (0, g)),
            pl.BlockSpec((length, LANES), lambda g: (0, TILES + g)),
        ],
        out_specs=pl.BlockSpec((length, LANES), lambda g: (0, g)),
        out_shape=jax.ShapeDtypeStruct((length, D), bf16),
        compiler_params=pltpu.CompilerParams(vmem_limit_bytes=VMEM),
        cost_estimate=pl.CostEstimate(
            flops=2 * 2 * HEADS * length * length * LANES, bytes_accessed=8 * length * D,
            transcendentals=HEADS * length * length,
        ),
        name="attention_all",
    )(queries, key_values, key_values)


def attention_pick_kernel(first_ref, q_ref, k_ref, v_ref, o_ref, lse_ref):
    rows, length = q_ref.shape[0], k_ref.shape[0]
    masks = head_masks()
    row = lax.broadcasted_iota(jnp.int32, (rows, length), 0)
    col = lax.broadcasted_iota(jnp.int32, (rows, length), 1)
    allowed = col <= row + first_ref[0]
    lane = lax.broadcasted_iota(jnp.int32, (1, LANES), 1)
    q, k, v = q_ref[...], k_ref[...], v_ref[...]
    joined = jnp.zeros((rows, LANES), f32)
    stat = jnp.zeros((rows, LANES), f32)
    for head, mask in enumerate(masks):
        scores = jnp.where(allowed, nt(only(mask, q), k), -1e30)
        top = jnp.max(scores, 1, keepdims=True) * SCALE_LOG2
        power = jnp.exp2(scores * SCALE_LOG2 - top)
        total = jnp.sum(power, 1, keepdims=True)
        joined = jnp.where(mask, nn(power.astype(bf16), v) / total, joined)
        stat = jnp.where(lane == head, top + jnp.log2(total), stat)
    o_ref[...] = joined.astype(bf16)
    lse_ref[0] = stat.T[0:8, :]


def attention_pick(first, queries, key_values):
    rows, length = queries.shape[0], key_values.shape[0]
    return pl.pallas_call(
        attention_pick_kernel,
        grid_spec=pltpu.PrefetchScalarGridSpec(
            num_scalar_prefetch=1,
            grid=(TILES,),
            in_specs=[
                pl.BlockSpec((rows, LANES), lambda g, s: (0, g)),
                pl.BlockSpec((length, LANES), lambda g, s: (0, g)),
                pl.BlockSpec((length, LANES), lambda g, s: (0, TILES + g)),
            ],
            out_specs=[
                pl.BlockSpec((rows, LANES), lambda g, s: (0, g)),
                pl.BlockSpec((1, 8, rows), lambda g, s: (g, 0, 0)),
            ],
        ),
        out_shape=[
            jax.ShapeDtypeStruct((rows, D), bf16),
            jax.ShapeDtypeStruct((TILES, 8, rows), f32),
        ],
        compiler_params=pltpu.CompilerParams(vmem_limit_bytes=VMEM),
        cost_estimate=pl.CostEstimate(
            flops=2 * 2 * HEADS * rows * length * LANES, bytes_accessed=6 * length * D,
            transcendentals=HEADS * rows * length,
        ),
        name="attention_pick",
    )(first, queries, key_values, key_values)


def attention_back_kernel(
    first_ref, q_ref, k_ref, v_ref, o_ref, do_ref, lse_ref, dq_ref, dk_ref, dv_ref
):
    rows, length = q_ref.shape[0], k_ref.shape[0]
    masks = head_masks()
    key = lax.broadcasted_iota(jnp.int32, (length, rows), 0)
    query = lax.broadcasted_iota(jnp.int32, (length, rows), 1)
    allowed = key <= query + first_ref[0]
    q, k, v, do = q_ref[...], k_ref[...], v_ref[...], do_ref[...]
    share = (
        lax.broadcasted_iota(jnp.int32, (8, LANES), 0)
        == lax.broadcasted_iota(jnp.int32, (8, LANES), 1) // HDIM
    ).astype(f32)
    inner = lax.dot_general(
        share, do.astype(f32) * o_ref[...].astype(f32), (((1,), (1,)), ((), ())),
        preferred_element_type=f32, precision=lax.Precision.HIGHEST,
    )
    lse = lse_ref[0]
    dq = jnp.zeros((rows, LANES), f32)
    dk = jnp.zeros((length, LANES), f32)
    dv = jnp.zeros((length, LANES), f32)
    for head, mask in enumerate(masks):
        k_head = only(mask, k)
        scores = nt(k_head, q)
        chance = jnp.where(
            allowed, jnp.exp2(scores * SCALE_LOG2 - lse[head : head + 1, :]), 0.0
        )
        d_chance = nt(only(mask, v), do)
        d_scores = (chance * (d_chance - inner[head : head + 1, :])).astype(bf16)
        dv = jnp.where(mask, nn(chance.astype(bf16), do), dv)
        dk = jnp.where(mask, nn(d_scores, q), dk)
        dq = dq + tn(d_scores, k_head)
    dq_ref[...] = (dq * SCALE).astype(bf16)
    dk_ref[...] = (dk * SCALE).astype(bf16)
    dv_ref[...] = dv.astype(bf16)


def attention_back(first, queries, key_values, attended, grad_attended, lse):
    rows, length = queries.shape[0], key_values.shape[0]
    rows_spec = pl.BlockSpec((rows, LANES), lambda g, s: (0, g))
    all_spec = pl.BlockSpec((length, LANES), lambda g, s: (0, g))
    return pl.pallas_call(
        attention_back_kernel,
        grid_spec=pltpu.PrefetchScalarGridSpec(
            num_scalar_prefetch=1,
            grid=(TILES,),
            in_specs=[
                rows_spec,
                all_spec,
                pl.BlockSpec((length, LANES), lambda g, s: (0, TILES + g)),
                rows_spec,
                rows_spec,
                pl.BlockSpec((1, 8, rows), lambda g, s: (g, 0, 0)),
            ],
            out_specs=[rows_spec, all_spec, all_spec],
        ),
        out_shape=[
            jax.ShapeDtypeStruct((rows, D), bf16),
            jax.ShapeDtypeStruct((length, D), bf16),
            jax.ShapeDtypeStruct((length, D), bf16),
        ],
        compiler_params=pltpu.CompilerParams(vmem_limit_bytes=VMEM),
        cost_estimate=pl.CostEstimate(
            flops=5 * 2 * HEADS * rows * length * LANES, bytes_accessed=10 * length * D,
            transcendentals=HEADS * rows * length,
        ),
        name="attention_back",
    )(first, queries, key_values, key_values, attended, grad_attended, lse)


def split_high(values):
    high = lax.reduce_precision(values, 8, 7)
    return high, values - high


def with_lse(packed):
    lse = packed[..., D : D + 3].astype(f32)
    return packed[..., :D].astype(f32), lse[..., 0:1] + lse[..., 1:2] + lse[..., 2:3]


def pack_lse(mean, lse):
    high, low = split_high(lse)
    low, rest = split_high(low)
    return jnp.concatenate(
        [mean, high, low, rest, jnp.zeros(mean.shape[:-1] + (LANES - 3,), f32)], -1
    ).astype(bf16)


def merge(first, second):
    joint = jnp.logaddexp(first[1], second[1])
    mean = first[0] * jnp.exp(first[1] - joint) + second[0] * jnp.exp(second[1] - joint)
    return mean, joint


def head_scan_kernel(rows_ref, *refs, carried, last):
    split = len(refs) - (1 if last else 2)
    refs, outs = refs[:split], refs[split:]
    rows = rows_ref[...]
    top = total = mixed = None
    if carried:
        mixed, top = refs[0][...].astype(f32), refs[1][...]
        total = jnp.ones_like(top)
        refs = refs[2:]
    for at in range(0, len(refs), 2):
        chunk = refs[at][...]
        if at + 1 < len(refs):
            chunk = jnp.concatenate([chunk, refs[at + 1][...]], 0)
        logits = nt(rows, chunk)
        here = jnp.max(logits, 1, keepdims=True)
        if top is None:
            top = here
            power = jnp.exp(logits - top)
            total = jnp.sum(power, 1, keepdims=True)
            mixed = nn(power.astype(bf16), chunk)
        else:
            joint = jnp.maximum(top, here)
            shrink = jnp.exp(top - joint)
            power = jnp.exp(logits - joint)
            total = total * shrink + jnp.sum(power, 1, keepdims=True)
            mixed = mixed * shrink + nn(power.astype(bf16), chunk)
            top = joint
    lse = top + jnp.log(total)
    if len(outs) == 2:
        outs[0][...], outs[1][...] = mixed / total, lse
    else:
        outs[0][:, :D] = (mixed / total).astype(bf16)
        high = lse.astype(bf16).astype(f32)
        low = (lse - high).astype(bf16).astype(f32)
        rest = lse - high - low
        lane = lax.broadcasted_iota(jnp.int32, (1, LANES), 1)
        tail = jnp.where(lane == 0, high, jnp.where(lane == 1, low, jnp.where(lane == 2, rest, 0.0)))
        outs[0][:, D:] = tail.astype(bf16)


def head_scan(rows, chunks, carry=(), last=True):
    count, block = rows.shape[0], 512
    vocab = sum(chunk.shape[0] for chunk in chunks)
    wide = pl.BlockSpec((block, D), lambda i: (i, 0))
    thin = pl.BlockSpec((block, 1), lambda i: (i, 0))
    if last:
        out_specs = [pl.BlockSpec((block, D + LANES), lambda i: (i, 0))]
        out_shape = [jax.ShapeDtypeStruct((count, D + LANES), bf16)]
    else:
        out_specs = [wide, thin]
        out_shape = [jax.ShapeDtypeStruct((count, D), f32), jax.ShapeDtypeStruct((count, 1), f32)]
    return pl.pallas_call(
        lambda *refs: head_scan_kernel(*refs, carried=bool(carry), last=last),
        grid=(count // block,),
        in_specs=[wide]
        + [wide, thin][: len(carry)]
        + [
            pl.BlockSpec(chunk.shape, lambda i: (0, 0), pipeline_mode=pl.Buffered(1))
            for chunk in chunks
        ],
        out_specs=out_specs,
        out_shape=out_shape,
        compiler_params=pltpu.CompilerParams(vmem_limit_bytes=VMEM),
        cost_estimate=pl.CostEstimate(
            flops=4 * count * vocab * D, bytes_accessed=2 * vocab * D + 4 * count * D,
            transcendentals=count * vocab,
        ),
        name="head_scan",
    )(rows, *carry, *chunks)


def head_grad_kernel(table_ref, rows_ref, weight_ref, out_ref):
    rows = rows_ref[:, :D]
    tail = rows_ref[:, D:].astype(f32).T
    logits = nt(table_ref[...], rows)
    lse = tail[0:1] + tail[1:2] + tail[2:3]
    grad = (jnp.exp(logits - lse) * weight_ref[0]).astype(bf16)
    part = nn(grad, rows)

    @pl.when(pl.program_id(0) == 0)
    def _():
        out_ref[...] = part

    @pl.when(pl.program_id(0) > 0)
    def _():
        out_ref[...] += part


def head_grad(table_low, rows, weight):
    vocab, count, block = table_low.shape[0], rows.shape[0], 2048
    steps = count // block
    return pl.pallas_call(
        head_grad_kernel,
        grid=(steps,),
        in_specs=[
            pl.BlockSpec((vocab, D), lambda i: (0, 0)),
            pl.BlockSpec((block, D + LANES), lambda i: (i, 0)),
            pl.BlockSpec((1, 1, block), lambda i: (i, 0, 0)),
        ],
        out_specs=pl.BlockSpec((vocab, D), lambda i: (0, 0)),
        out_shape=jax.ShapeDtypeStruct((vocab, D), f32),
        compiler_params=pltpu.CompilerParams(vmem_limit_bytes=VMEM),
        cost_estimate=pl.CostEstimate(
            flops=4 * count * vocab * D, bytes_accessed=2 * count * D + 6 * vocab * D,
            transcendentals=count * vocab,
        ),
        name="head_grad",
    )(table_low, rows, weight.reshape(steps, 1, block))


def permute(value, axis, target):
    return lax.ppermute(value, axis, [(i, target(i)) for i in range(lax.axis_size(axis))])


def other_core(value):
    return permute(value, "mp", lambda i: i ^ 1)


def along_x(value, step):
    chips = lax.axis_size("mp") // 2
    return permute(value, "mp", lambda i: (i // 2 + step) % chips * 2 + i % 2)


def ring_order(count):
    return list(range(0, count, 2)) + list(range(count - 1, 0, -2))


def after(value, *others):
    return lax.optimization_barrier((value, *others))[0]


def ring_hop(upward, downward):
    count = lax.axis_size("dp")
    order = ring_order(count)
    spot = [order.index(i) for i in range(count)]
    return (
        permute(upward, "dp", lambda i: order[(spot[i] + 1) % count]),
        permute(downward, "dp", lambda i: order[(spot[i] - 1) % count]),
    )


def ring_rest(first, gates):
    count = lax.axis_size("dp")
    upward, downward = first
    pieces = []
    for step in range(2, count // 2 + 1):
        upward, downward, _ = lax.optimization_barrier(
            (upward, downward, gates[min(step - 2, len(gates) - 1)])
        )
        if 2 * step == count:
            half = upward.shape[0] // 32 * 16
            upward, downward = upward[:half], downward[half:]
        upward, downward = ring_hop(upward, downward)
        pieces += [upward, downward]
    return pieces


def sum_everywhere(values):
    world = lax.axis_size(AXES)
    row = jnp.pad(values, (0, LANES - values.shape[0]))
    spread = jnp.broadcast_to(row[None, :], (world, LANES))
    return jnp.sum(lax.all_to_all(spread, AXES, 0, 0, tiled=True), 0)[: values.shape[0]]


def one_hot(index, count):
    return (index[:, None] == jnp.arange(count, dtype=jnp.int32)[None, :]).astype(bf16)


def placed(index, values, count):
    hit = index[None, :] == jnp.arange(count, dtype=jnp.int32)[:, None]
    return jnp.max(jnp.where(hit, values[None, :], -1), 1)


def rank_before(choice):
    count = choice.shape[0]
    earlier = (
        jnp.arange(count)[None, :] < jnp.arange(count)[:, None]
    ).astype(bf16)
    return jnp.dot(earlier, choice.astype(bf16), preferred_element_type=f32)


def unblocks(packed, rows):
    return jnp.concatenate(
        [packed[j : j + rows] for j in range(0, packed.shape[0], rows)], 1
    )


def grad_pack_kernel(core_ref, *refs, plan, rows_of, world):
    refs = dict(enumerate(refs))
    for left, right, held in plan:
        refs[held][...] = tn(refs[left][...], refs[right][...])
    mine_ref, theirs_ref = refs[rows_of[-1][0]], refs[rows_of[-1][0] + 1]
    second = core_ref[0] == 1
    total = mine_ref.shape[1]
    for j in range(world // 2):
        mine, theirs, filled = [], [], 0
        for held, rows, column in rows_of[:-1]:
            low = refs[held][2 * j * rows : (2 * j + 1) * rows, column : column + D]
            high = refs[held][(2 * j + 1) * rows : (2 * j + 2) * rows, column : column + D]
            mine.append(jnp.where(second, high, low))
            theirs.append(jnp.where(second, low, high))
            filled += rows
        if filled < total:
            mine.append(jnp.zeros((total - filled, D), f32))
            theirs.append(mine[-1])
        mine_ref[j] = jnp.concatenate(mine, 0).astype(bf16)
        theirs_ref[j] = jnp.concatenate(theirs, 0).astype(bf16)


def grad_pack(products, rows, world):
    core = jnp.reshape(lax.axis_index("mp") % 2, (1,)).astype(jnp.int32)
    operands = [value for product in products for value in product] + list(rows)
    inputs, count = len(operands), len(products)
    plan = [(2 * i, 2 * i + 1, inputs + 2 + i) for i in range(count)]
    pieces, scratch, flops = [], [], 0
    for i, (left, right) in enumerate(products):
        flops += 2 * left.shape[0] * left.shape[1] * right.shape[1]
        scratch.append(pltpu.VMEM((left.shape[1], right.shape[1]), f32))
        for column in range(0, right.shape[1], D):
            pieces.append((inputs + 2 + i, left.shape[1] // world, column))
    for i, value in enumerate(rows):
        pieces.append((2 * count + i, value.shape[0] // world, 0))
    total = -(-sum(piece[1] for piece in pieces) // 16) * 16
    pieces.append((inputs, 0, 0))
    shape = jax.ShapeDtypeStruct((world // 2, total, D), bf16)
    return pl.pallas_call(
        lambda *refs: grad_pack_kernel(*refs, plan=plan, rows_of=pieces, world=world),
        in_specs=[pl.BlockSpec(memory_space=pltpu.SMEM)]
        + [pl.BlockSpec(memory_space=pltpu.VMEM)] * inputs,
        out_specs=[pl.BlockSpec(memory_space=pltpu.VMEM)] * 2,
        out_shape=[shape, shape],
        scratch_shapes=scratch,
        compiler_params=pltpu.CompilerParams(vmem_limit_bytes=VMEM),
        cost_estimate=pl.CostEstimate(
            flops=flops, bytes_accessed=4 * world // 2 * total * D, transcendentals=0
        ),
        name="grad_pack",
    )(core, *operands)


class RingSum:

    def __init__(self, mine, theirs):
        self.count = lax.axis_size("dp")
        self.chips = lax.axis_size("mp") // 2
        shape = (self.count, self.chips, -1, D)
        self.got = other_core(theirs).reshape(shape)
        self.mine = mine.reshape(shape)
        self.order = ring_order(self.count)
        spot = [self.order.index(i) for i in range(self.count)]
        self.here = jnp.asarray(spot, jnp.int32)[lax.axis_index("dp")]
        self.up_steps, self.down_steps = self.count // 2, (self.count - 1) // 2
        self.upward = self.part(self.up_steps).astype(bf16)
        self.downward = self.part(-self.down_steps).astype(bf16)
        self.step = 0

    def part(self, step):
        at = jnp.asarray(self.order, jnp.int32)[(self.here + step) % self.count]
        return lax.dynamic_index_in_dim(self.mine, at, 0, keepdims=False).astype(f32) + (
            lax.dynamic_index_in_dim(self.got, at, 0, keepdims=False).astype(f32)
        )

    def hop(self):
        self.step += 1
        step, down = self.step, self.downward
        self.upward, down = ring_hop(self.upward, down)
        if step <= self.down_steps:
            self.downward = down
        if step < self.up_steps:
            self.upward = (self.upward.astype(f32) + self.part(self.up_steps - step)).astype(bf16)
        if step < self.down_steps:
            self.downward = (self.downward.astype(f32) + self.part(step - self.down_steps)).astype(
                bf16
            )

    def before(self, value):
        return lax.optimization_barrier((value, self.upward, self.downward))[0]

    def total(self, gate=None):
        while self.step < self.up_steps:
            self.hop()
        line = (
            self.part(0) + self.upward.astype(f32) + self.downward.astype(f32)
        ).astype(bf16)
        if gate is not None:
            line = after(line, gate)
        chip = lax.axis_index("mp") // 2
        total = lax.dynamic_index_in_dim(line, chip, 0, keepdims=False).astype(f32)
        for step in range(1, self.chips):
            going = lax.dynamic_index_in_dim(line, (chip + step) % self.chips, 0, keepdims=False)
            total = total + along_x(going, step).astype(f32)
        return total


def renew(weight, moment, average, gradient, factor):
    clipped = gradient * factor
    moment_new = MOMENTUM * moment + clipped
    weight_new = weight - STEP_RATE * (clipped + MOMENTUM * moment_new)
    average_new = AVERAGE_DECAY * average + (1.0 - AVERAGE_DECAY) * weight_new
    return (weight_new, moment_new, average_new)


def shards(
    patches,
    patch_pos,
    owner,
    local_row,
    counts,
    task,
    table,
    table_mom,
    table_avg,
    patch_w,
    patch_mom,
    patch_avg,
    attn_w,
    attn_mom,
    attn_avg,
    up_w,
    up_mom,
    up_avg,
    down_w,
    down_mom,
    down_avg,
    gains,
    gain_mom,
    gain_avg,
):
    groups, owners = lax.axis_size("dp"), lax.axis_size("mp")
    world = groups * owners
    tokens_here = patches.shape[0]
    rows_own = table.shape[0]
    rows_attn, rows_patch, rows_down = attn_w.shape[0], patch_w.shape[0], down_w.shape[0]
    cols_gain = gains.shape[1]
    place = lax.axis_index("dp") * owners + lax.axis_index("mp")

    table_low = table.astype(bf16)
    gain_row = jnp.pad(gains.astype(bf16).reshape(1, 3 * cols_gain), ((0, 0), (0, 4 * D - 3 * cols_gain)))
    patch_rows = jnp.pad(patch_w.astype(bf16), ((0, -rows_patch % 4), (0, 0)))
    early = jnp.concatenate([attn_w.astype(bf16), patch_rows.reshape(-1, 4 * D), gain_row], 0)
    late = jnp.concatenate(
        [
            up_w.astype(bf16),
            jnp.concatenate(
                [down_w[j : j + rows_attn] for j in range(0, rows_down, rows_attn)], 1
            ).astype(bf16),
        ],
        0,
    )
    early_all, late_all = (
        lax.all_gather(jnp.pad(w, ((0, -w.shape[0] % 8), (0, 0))), AXES, axis=0, tiled=False)
        for w in (early, late)
    )
    first_pieces = ring_hop(table_low, table_low)

    my_counts = lax.dynamic_slice_in_dim(counts, place, 1, 0)
    first_tok, alive = my_counts[0, 0], my_counts[0, 1]
    positions = jnp.arange(tokens_here, dtype=jnp.int32)
    is_patch = (positions < first_tok)[:, None]
    is_token = (positions >= first_tok) & (positions < first_tok + alive)
    is_valid = (positions < first_tok + alive)[:, None]
    target_owner = owner[:, 0]

    share = -(-3 * tokens_here // (2 * world) // 16) * 16
    identity = target_owner * (rows_own * groups) + local_row
    same = (identity[:, None] == identity[None, :]) & is_token[None, :]
    first_same = jnp.min(jnp.where(same, positions[None, :], tokens_here), 1)
    leads = is_token & (first_same == positions)
    dest = identity // rows_own
    leads_to = (dest[:, None] == jnp.arange(world)[None, :]) & leads[:, None]
    lead_rank = jnp.sum(jnp.where(leads_to, rank_before(leads_to), 0.0), 1).astype(jnp.int32)
    far_rank = jnp.max(
        jnp.where(first_same[:, None] == positions[None, :], lead_rank[None, :], 0), 1
    )
    far_row = identity - dest * rows_own
    most = jnp.max(jnp.sum(leads_to.astype(jnp.int32), 0))

    def far_slots(start, share):
        within = far_rank - start
        fits = is_token & (within >= 0) & (within < share)
        return jnp.where(fits, dest * share + within, -1)

    def far_ids(slots, extra, share):
        ids = placed(slots, far_row, world * share).reshape(world, share)
        ids = jnp.concatenate([ids, jnp.full((world, 1), extra, jnp.int32)], 1)
        return lax.all_to_all(ids, ("mp", "dp"), split_axis=0, concat_axis=0, tiled=True)

    first_slots = far_slots(0, share)
    first_ids = far_ids(first_slots, most, share)
    few = 16
    turns = (jnp.max(first_ids[:, share]) - share + few - 1) // few

    def far_fetch(slots, ids, share):
        spread = one_hot(ids[:, :share].reshape(-1), rows_own)
        rows = jnp.dot(spread, table_low, preferred_element_type=f32).astype(bf16)
        rows = lax.optimization_barrier((rows, *first_pieces))[0]
        arrived = lax.all_to_all(
            rows.reshape(world, share, D), ("mp", "dp"), split_axis=0, concat_axis=0, tiled=True
        ).reshape(world * share, D)
        return arrived, jnp.dot(one_hot(slots, world * share), arrived, preferred_element_type=f32)

    def far_pack(slots, values, share):
        return jnp.dot(
            one_hot(slots, world * share).T, values, preferred_element_type=f32
        ).astype(bf16)

    def far_send(packed, share):
        return lax.all_to_all(
            packed.reshape(world, share, D),
            ("mp", "dp"), split_axis=0, concat_axis=0, tiled=True,
        ).reshape(world * share, D)

    def far_add(arrived, ids, share):
        spread = one_hot(ids[:, :share].reshape(-1), rows_own)
        return tn(spread, arrived)

    arrived, looked = far_fetch(first_slots, first_ids, share)

    def fetch_turn(turn, total):
        slots = far_slots(share + turn * few, few)
        return total + far_fetch(slots, far_ids(slots, 0, few), few)[1]

    looked = lax.fori_loop(0, turns, fetch_turn, looked)

    def columns(gathered, low, high):
        return gathered[:, :rows_attn, low * D : high * D].reshape(-1, (high - low) * D)

    w_q, w_kv, w_out = columns(early_all, 0, 1), columns(early_all, 1, 3), columns(early_all, 3, 4)
    gain_at = rows_attn + patch_rows.shape[0] // 4
    w_patch = (
        early_all[:, rows_attn:gain_at].reshape(world, -1, D)[:, :rows_patch].reshape(-1, D)
    )
    gain_all = (
        early_all[:, gain_at, : 3 * cols_gain]
        .reshape(world, 3, cols_gain).transpose(1, 0, 2).reshape(3, D).astype(f32)
    )
    w_up = columns(late_all, 0, 4)
    w_down = jnp.concatenate(
        [late_all[:, rows_attn : 2 * rows_attn, j : j + D] for j in range(0, 4 * D, D)], 1
    ).reshape(world * rows_down, D)

    position_code = (patch_pos[:, None] == jnp.arange(POSN)[None, :]).astype(bf16)
    patch_in = jnp.concatenate([patches, position_code], 1)
    from_patch = jnp.dot(patch_in, w_patch, preferred_element_type=f32)
    embed_scale = math.sqrt(D)
    embedded = jnp.where(is_patch, from_patch, 0.0) + embed_scale * looked
    normed_first, first_back = jax.vjp(layer_norm, embedded, gain_all[0])
    normed_first = normed_first.astype(bf16)
    key_values = jnp.dot(normed_first, w_kv, preferred_element_type=f32).astype(bf16)

    pick = first_tok - 1
    pick_at = jnp.reshape(pick, (1,))

    def picked_rows(values, start=pick):
        return lax.dynamic_slice_in_dim(values, start, LOSS, 0)

    normed_pick = picked_rows(normed_first)
    query_pick = jnp.dot(normed_pick, w_q, preferred_element_type=f32).astype(bf16)
    attended_pick, lse_pick = attention_pick(pick_at, query_pick, key_values)
    branch_pick = jnp.dot(attended_pick, w_out, preferred_element_type=f32)
    middle_pick = picked_rows(embedded) + branch_pick
    normed_mid, mid_back = jax.vjp(layer_norm, middle_pick, gain_all[1])
    normed_mid = normed_mid.astype(bf16)
    query_all = jnp.dot(normed_first, w_q, preferred_element_type=f32).astype(bf16)
    attended = attention_all(query_all, key_values)
    normed_mid = after(normed_mid, attended)
    hidden_pick = jnp.dot(normed_mid, w_up, preferred_element_type=f32)
    active_f32, gelu_back = jax.vjp(gelu_tanh, hidden_pick)
    active_pick = active_f32.astype(bf16)
    result_pick = middle_pick + jnp.dot(active_pick, w_down, preferred_element_type=f32)
    final_rows, final_back = jax.vjp(layer_norm, result_pick, gain_all[2])
    own_rows = final_rows.astype(bf16)
    pieces = ring_rest(first_pieces, (arrived, attended, own_rows))
    chunks = [table_low, *first_pieces, *pieces]
    target_rows = picked_rows(looked, first_tok)

    chips = owners // 2
    line = jnp.stack([own_rows] + [along_x(own_rows, step) for step in range(1, chips)])
    group_rows = jnp.stack([line, other_core(line)])
    group_rows = group_rows.reshape(-1, D)
    near = 5
    carry = head_scan(group_rows, chunks[:near], last=False)
    (scanned,) = head_scan(group_rows, chunks[near:], carry)
    scanned = scanned.reshape(2, chips, LOSS, D + LANES)
    there = other_core(scanned[1])
    line = pack_lse(*merge(with_lse(scanned[0]), with_lse(there)))
    own = with_lse(line[0])
    for step in range(1, chips):
        own = merge(own, with_lse(along_x(line[step], -step)))
    mean_own, own_total = own[0], own[1][:, 0]

    picked = jnp.sum(own_rows.astype(f32) * target_rows, 1)
    scored_all = counts[:, 2].astype(f32)
    per_task = (task[:, None] == jnp.arange(TASKS)[None, :]).astype(f32)
    task_total = jnp.sum(per_task * scored_all[:, None], 0)
    present = jnp.sum((task_total > 0).astype(f32))
    inverse_seq = jnp.sum(per_task / jnp.maximum(task_total, 1.0)[None, :], 1)
    row_live = (jnp.arange(LOSS)[None, :] < counts[:, 2:3]).astype(f32) * inverse_seq[:, None]
    own_weight = lax.dynamic_slice_in_dim(row_live, place, 1, 0)[0]
    loss_part = jnp.sum(own_weight * (own_total - picked))

    rows_all = lax.all_gather(
        pack_lse(own_rows.astype(f32), own_total[:, None]), AXES, axis=0, tiled=True
    )

    scaled_weight = (own_weight / present)[:, None]
    grad_rows = scaled_weight * (mean_own - target_rows)
    grad_result, grad_gain_last = final_back(grad_rows)
    grad_second = grad_result.astype(bf16)
    grad_hidden = gelu_back(nt(grad_second, w_down))[0].astype(bf16)
    grad_middle, grad_gain_mid = mid_back(nt(grad_hidden, w_up))
    grad_middle = grad_result + grad_middle
    grad_branch = grad_middle.astype(bf16)
    late_mine, late_theirs = grad_pack(
        [(normed_mid, grad_hidden), (active_pick, grad_second), (attended_pick, grad_branch)],
        [], world,
    )
    late_sum = RingSum(late_mine, late_theirs)
    grad_attended = late_sum.before(nt(grad_branch, w_out).astype(bf16))
    late_sum.hop()
    grad_q, grad_k, grad_v = attention_back(
        pick_at, query_pick, key_values, attended_pick, grad_attended, lse_pick
    )
    grad_kv = late_sum.before(jnp.concatenate([grad_k, grad_v], 1))
    late_sum.hop()
    def back_in_place(rows, start):
        whole = jnp.zeros((tokens_here, D), f32)
        return lax.dynamic_update_slice_in_dim(whole, rows, start, 0)

    grad_normed = nt(grad_kv, w_kv) + back_in_place(nt(grad_q, w_q), pick)
    grad_normed = late_sum.before(grad_normed)
    late_sum.hop()
    grad_embedded, grad_gain_first = first_back(grad_normed)
    grad_embedded = grad_embedded + back_in_place(grad_middle, pick)
    grad_looked = (
        embed_scale * grad_embedded
        + back_in_place(-scaled_weight * own_rows.astype(f32), first_tok)
    ).astype(bf16)
    grad_looked = late_sum.before(grad_looked)
    packed = far_pack(first_slots, grad_looked, share)
    grad_patch_rows = jnp.where(is_patch, grad_embedded, 0.0).astype(bf16)
    grad_gain = jnp.stack([grad_gain_first, grad_gain_mid, grad_gain_last])
    gain_part = grad_gain.reshape(3, world, cols_gain).transpose(1, 0, 2)
    gain_part = jnp.pad(gain_part.reshape(world, 3 * cols_gain), ((0, 0), (0, D - 3 * cols_gain)))
    early_mine, early_theirs = grad_pack(
        [
            (normed_pick, grad_q),
            (normed_first, grad_k),
            (normed_first, grad_v),
            (patch_in, after(grad_patch_rows, packed)),
        ],
        [gain_part], world,
    )
    table_head = head_grad(table_low, after(rows_all, early_theirs), row_live / present)
    grad_arrived = far_send(packed, share)
    summed_early = RingSum(early_mine, early_theirs).total()
    summed_late = late_sum.total(grad_arrived)
    grad_table = table_head + far_add(grad_arrived, first_ids, share)

    def next_turn(turn, total):
        slots = far_slots(share + turn * few, few)
        return total + far_add(
            far_send(far_pack(slots, grad_looked, few), few), far_ids(slots, 0, few), few
        )

    grad_table = lax.fori_loop(0, turns, next_turn, grad_table)

    attended = after(attended, late_theirs)
    branch = jnp.dot(attended, w_out, preferred_element_type=f32)
    middle = embedded + branch
    normed_second = layer_norm(middle, gain_all[1]).astype(bf16)
    hidden = jnp.dot(normed_second, w_up, preferred_element_type=f32)
    second = jnp.dot(gelu_tanh(hidden).astype(bf16), w_down, preferred_element_type=f32)
    result = middle + second

    def square_sum(values):
        return jnp.sum(jnp.where(is_valid, jnp.mean(values * values, 1, keepdims=True), 0.0))

    edge = 3 * rows_attn
    summed_up = unblocks(summed_late[: 4 * rows_attn], rows_attn)
    summed_down = summed_late[4 * rows_attn : 4 * rows_attn + rows_down]
    out_at = 4 * rows_attn + rows_down
    summed_attn = jnp.concatenate(
        [unblocks(summed_early[:edge], rows_attn), summed_late[out_at : out_at + rows_attn]], 1
    )
    summed_patch = summed_early[edge : edge + rows_patch]
    summed_gain = summed_early[edge + rows_patch, : 3 * cols_gain].reshape(3, cols_gain)
    gradient_list = (grad_table, summed_patch, summed_attn, summed_up, summed_down, summed_gain)
    squares = sum((jnp.sum(gradient * gradient) for gradient in gradient_list))
    totals = sum_everywhere(
        jnp.stack(
            [
                squares,
                loss_part,
                square_sum(embedded),
                square_sum(branch),
                square_sum(second),
                square_sum(result),
            ]
        )
    )
    clip_norm = jnp.sqrt(totals[0])
    loss_total = totals[1]
    factor = jnp.minimum(1.0, CLIP_LIMIT / clip_norm)
    states = (
        (table, table_mom, table_avg),
        (patch_w, patch_mom, patch_avg),
        (attn_w, attn_mom, attn_avg),
        (up_w, up_mom, up_avg),
        (down_w, down_mom, down_avg),
        (gains, gain_mom, gain_avg),
    )
    renewed = [
        renew(state[0], state[1], state[2], gradient, factor)
        for state, gradient in zip(states, gradient_list)
    ]
    valid_total = jnp.sum(counts[:, :2].astype(f32))
    rms_stats = jnp.sqrt(totals[2:6] / valid_total)
    outputs = []
    for state in renewed[:-1]:
        outputs.extend([state[0], state[1], state[2], state[0].astype(bf16)])
    outputs.extend(renewed[-1])
    return (*outputs, loss_total, present, clip_norm, rms_stats)


def solution(mesh):
    whole, split = P(), P(AXES)
    rows, vocab, columns = P(AXES, None), P(("mp", "dp"), None), P(None, AXES)
    in_specs = (rows, split, rows, split, whole, whole) + (vocab,) * 3 + (rows,) * 12 + (columns,) * 3
    out_specs = (vocab,) * 4 + (rows,) * 16 + (columns,) * 3 + (whole,) * 4
    return jax.shard_map(shards, mesh=mesh, in_specs=in_specs, out_specs=out_specs, check_vma=False)
```

time: 1500 us -> 767 us (0.51)
  matrix products: 486 us -> 74.5 us
  blocking collectives: 265 us -> 42 us
  Pallas kernels: 0 us -> 167 us
  other arithmetic: 272 us -> 108 us
  waiting for transfers between devices: 334 us -> 188 us
  starting transfers between devices: 13.3 us -> 48.7 us
  between operations: 23.3 us -> 48.8 us
    dot_general x31 -> x19, matrix products: 486 us -> 74.5 us  [the longest x6 18.6 us: contract(): lax.dot_general(left, right, (((left_dim,), (right_dim,)), ((), ())), pre...]
    all_gather x6 -> x3, waiting for transfers between devices: 203 us -> 0.04 us  [the longest x2 0.04 us: shards(): lax.all_gather(jnp.pad(w, ((0, -w.shape[0] % 8), (0, 0))), AXES, axis=0,...]
    pallas_call x0 -> x8, Pallas kernels: none -> 167 us  [the longest x2 46.7 us: head_scan(): pl.pallas_call(lambda *refs: head_scan_kernel(*refs, carried=bool(carry),...]
    unnamed x2 -> x0, blocking collectives: 147 us -> none
    ppermute x0 -> x30, waiting for transfers between devices: none -> 117 us  [permute(): lax.ppermute(value, axis, [(i, target(i)) for i in range(lax.axis_size(ax...]
    reduce_scatter x5 -> x0, waiting for transfers between devices: 98.1 us -> none  [the longest x1 81.2 us: shards(): lax.psum_scatter((table_head + table_embed).astype(jnp.bfloat16), 'dp', s...]
    all_gather x3 -> x0, blocking collectives: 70.1 us -> none  [the longest x1 59.7 us: shards(): lax.all_gather(gains.astype(jnp.bfloat16), ('dp', 'mp'), axis=1, tiled=True)]
    reduce_sum x9 -> x7, other arithmetic: 71.4 us -> 7.87 us  [the longest x1 3.31 us: layer_norm(): row_mean = jnp.mean(values, -1, keepdims=True)]
  transfers between devices with their start and end apart: 17 -> 36, of which waited for: 6 -> 17; matrix products, arithmetic and copies ran while one was open for 53% -> 26% of each run, Pallas kernels for 0% -> 15%
where the time goes in v1:
time: 767 us; the launch traced here: 756 us
  waiting for transfers between devices  188 us (25%)
  Pallas kernels  167 us (22%)
  other arithmetic  108 us (14%)
  local copies, waits for them, and re-layouts  78.5 us (10%)
  matrix products  74.5 us (10%)
  between operations  48.8 us (6%)
  starting transfers between devices  48.7 us (6%)
  blocking collectives  42 us (5%)
    ppermute x30, waiting for transfers between devices, permute(): lax.ppermute(value, axis, [(i, target(i)) for i in range(lax.axis_size(ax...  117 us
    all_to_all x1, waiting for transfers between devices, far_fetch(): lax.all_to_all(rows.reshape(world, share, D), ('mp', 'dp'), split_axis=0,...  64.9 us
    pallas_call x2, Pallas kernels, head_scan(): pl.pallas_call(lambda *refs: head_scan_kernel(*refs, carried=bool(carry),...  46.7 us
    all_to_all x1, blocking collectives, far_ids(): lax.all_to_all(ids, ('mp', 'dp'), split_axis=0, concat_axis=0, tiled=True)  42 us
    ppermute x30, starting transfers between devices, permute(): lax.ppermute(value, axis, [(i, target(i)) for i in range(lax.axis_size(ax...  38.2 us
    pallas_call x1, Pallas kernels, head_grad(): pl.pallas_call(head_grad_kernel, grid=(steps,), in_specs=[pl.BlockSpec((v...  32.8 us
    pallas_call x1, Pallas kernels, attention_all(): pl.pallas_call(lambda *refs: attention_all_kernel(*refs, block=512), grid...  30 us
    pallas_call x1, Pallas kernels, attention_back(): pl.pallas_call(attention_back_kernel, grid_spec=pltpu.PrefetchScalarGridS...  21.1 us
  transfers between devices with their start and end apart: 36, of which 17 were waited for; matrix products, arithmetic and copies ran while one was open for 26% of the time, Pallas kernels for 15%

profile of v1, /device:TPU:0, one launch (start us, length us, event | category | flops | bytes accessed | tf_op | source)
XLA Modules:
  0.0 756.4 jit_solution(2775630682931596861)
XLA Ops:
  25.8 42.0 %all_to_all.70 = s32[32,1,49]{2,1,0:T(1,128)S(1)} all-to-all(s32[32,1,49]{2,1,0:T(1,128)S(1)} %bitcast.271), channel_id=1, replica_groups=mesh['dp'=8,'mp'=4] {'mp','dp'}, dimensions={0} | all-to-all | bytes 12544 | tf_op jit(solution)/shard_map/all_to_all | solution.py:646
  68.0 4.8 fusion.39
  80.4 64.9 %all-to-all-done.5 = bf16[32,48,768]{2,1,0:T(8,128)(2,1)S(1)} async-done(((bf16[32,48,768]{2,1,0:T(8,128)(2,1)}), bf16[32,48,768]{2,1,0:T(8,128)(2,1)S(1)}, u32[]{:S(2)}, u32[]{:S(2)}) %all-to-all-start.5) | async-done | bytes 2359328 | tf_op jit(solution)/shard_map/all_to_all | solution.py:657
  147.4 4.5 fusion.31
  155.5 3.3 slice.293
  158.7 3.6 reshape_reshape.3
  163.7 3.9 fusion.121
  170.8 3.9 convolution_convert_fusion.k_ref.v_ref.refs_1_.refs_2_
  181.1 30.0 %attention_all.1 = bf16[1024,768]{1,0:T(8,128)(2,1)} custom-call(bf16[1024,768]{1,0:T(8,128)(2,1)} %convolution_convert_fusion.1.refs_0_, bf16[1024,1536]{1,0:T(8,128)(2,1)} %convolution_convert_fusion.k_ref.v_ref.refs_1_.refs_2_, bf16[1024,1536]{1,0:T(8,128)(2,1)} %convolution_convert_fusion.k_ref.v_ref.refs_1_.refs_2_), custom_call_target="tpu_custom_call" | custom-call | flops 12884901888 | bytes 6291456 | tf_op jit(solution)/shard_map/attention_all/pallas_call | solution.py:97
  211.1 10.1 %collective-permute-done.5.refs_5_ = bf16[1032,768]{1,0:T(8,128)(2,1)} collective-permute-done((bf16[1032,768]{1,0:T(8,128)(2,1)}, bf16[1032,768]{1,0:T(8,128)(2,1)}, u32[]{:S(2)}, u32[]{:S(2)}) %collective-permute-start.5) | collective-permute-done | bytes 1585184 | tf_op jit(solution)/shard_map/ppermute | solution.py:372
  227.3 15.9 %attention_pick.1 = (bf16[256,768]{1,0:T(8,128)(2,1)}, f32[6,8,256]{2,1,0:T(8,128)}) custom-call(s32[1]{0:T(128)} %bitcast.8.first_ref, bf16[256,768]{1,0:T(8,128)(2,1)} %convolution_convert_fusion.3.q_ref, bf16[1024,1536]{1,0:T(8,128)(2,1)} %convolution_convert_fusion.k_ref.v_ref.refs_1_.refs_2_, ...), custom_call_target="tpu_custom_call" | custom-call | flops 3221225472 | bytes 4718592 | tf_op jit(solution)/shard_map/attention_pick/pallas_call | solution.py:139
  256.1 3.7 multiply_convert_fusion.1
  265.8 8.5 %collective-permute-done.2 = bf16[256,768]{1,0:T(8,128)(2,1)S(1)} collective-permute-done((bf16[256,768]{1,0:T(8,128)(2,1)S(1)}, bf16[256,768]{1,0:T(8,128)(2,1)S(1)}, u32[]{:S(2)}, u32[]{:S(2)}) %collective-permute-start.2) | collective-permute-done | bytes 393248 | tf_op jit(solution)/shard_map/ppermute | solution.py:372
  280.8 26.2 %head_scan.2 = (f32[1024,768]{1,0:T(8,128)}, f32[1024,1]{1,0:T(8,128)}) custom-call(bf16[1024,768]{1,0:T(8,128)(2,1)} %bitcast.261, bf16[1032,768]{1,0:T(8,128)(2,1)S(1)} %copy-done.31, bf16[1032,768]{1,0:T(8,128)(2,1)} %collective-permute-done.refs_2_, bf16[1032,768]{1,0:T(8,128)(2,1)} %collective-permute-done.1.refs_3_, ...), custom_call_target="tpu_custom_call" | custom-call | flops 16231956480 | bytes 11071488 | tf_op jit(solution)/shard_map/head_scan/pallas_call | solution.py:312
  307.9 20.6 %head_scan.3 = bf16[1024,896]{1,0:T(8,128)(2,1)} custom-call(bf16[1024,768]{1,0:T(8,128)(2,1)} %bitcast.262, f32[1024,768]{1,0:T(8,128)} %get-tuple-element.157.refs_1_, f32[1024,1]{1,0:T(8,128)} %get-tuple-element.158.refs_2_, bf16[1032,768]{1,0:T(8,128)(2,1)} %collective-permute-done.6.refs_3_, bf16[1032,768]{1,0:T(8,128)(2,1)} %collective-permute-done.7.refs_4_, ...), custom_call_target="tpu_custom_call" | custom-call | flops 9739173888 | bytes 7901184 | tf_op jit(solution)/shard_map/head_scan/pallas_call | solution.py:312
  336.7 3.1 concatenate.49
  341.8 11.9 %collective-permute-done.11 = bf16[256,896]{1,0:T(8,128)(2,1)S(1)} collective-permute-done((bf16[256,896]{1,0:T(8,128)(2,1)S(1)}, bf16[256,896]{1,0:T(8,128)(2,1)S(1)}, u32[]{:S(2)}, u32[]{:S(2)}) %collective-permute-start.11) | collective-permute-done | bytes 458784 | tf_op jit(solution)/shard_map/ppermute | solution.py:372
  371.1 5.8 fusion.46.refs_2_
  380.0 9.5 %grad_pack.2 = (bf16[16,224,768]{2,1,0:T(8,128)(2,1)}, bf16[16,224,768]{2,1,0:T(8,128)(2,1)}) custom-call(s32[1]{0:T(128)} %bitcast.27.refs_0_, bf16[256,768]{1,0:T(8,128)(2,1)} %copy-done.63, bf16[256,3072]{1,0:T(8,128)(2,1)} %copy-done.119, bf16[256,3072]{1,0:T(8,128)(2,1)} %copy-done.118, bf16[256,768]{1,0:T(8,128)(2,1)} %copy-done.64, ...), custom_call_target="tpu_custom_call" | custom-call | flops 2717908992 | bytes 11010048 | tf_op jit(solution)/shard_map/grad_pack/pallas_call | solution.py:486
  401.4 3.3 fusion.65
  415.8 5.5 multiply_reduce_fusion.4
  421.3 4.1 copy.127
  432.0 21.1 %attention_back.1 = (bf16[256,768]{1,0:T(8,128)(2,1)}, bf16[1024,768]{1,0:T(8,128)(2,1)}, bf16[1024,768]{1,0:T(8,128)(2,1)}) custom-call(s32[1]{0:T(128)} %bitcast.8.first_ref, bf16[256,768]{1,0:T(8,128)(2,1)} %convolution_convert_fusion.3.q_ref, bf16[1024,1536]{1,0:T(8,128)(2,1)} %convolution_convert_fusion.k_ref.v_ref.refs_1_.refs_2_, ...), custom_call_target="tpu_custom_call" | custom-call | flops 8053063680 | bytes 7864320 | tf_op jit(solution)/shard_map/attention_back/pallas_call | solution.py:208
  455.3 20.3 %collective-permute-done.14 = bf16[2,224,768]{2,1,0:T(8,128)(2,1)S(1)} collective-permute-done((bf16[2,224,768]{2,1,0:T(8,128)(2,1)S(1)}, bf16[2,224,768]{2,1,0:T(8,128)(2,1)S(1)}, u32[]{:S(2)}, u32[]{:S(2)}) %collective-permute-start.14) | collective-permute-done | bytes 688160 | tf_op jit(solution)/shard_map/ppermute | solution.py:372
  475.6 3.6 fusion.57
  485.4 3.7 add.719
  489.2 7.6 collective-permute-done.16
  498.8 3.8 fusion.55
  505.4 3.3 fusion.105
  511.2 3.7 add.734
  518.0 3.2 add.735
  521.1 3.2 convert_element_type.480
  526.7 4.8 fusion.38
  531.5 11.1 %grad_pack.3 = (bf16[16,112,768]{2,1,0:T(8,128)(2,1)}, bf16[16,112,768]{2,1,0:T(8,128)(2,1)}) custom-call(s32[1]{0:T(128)} %bitcast.27.refs_0_, bf16[256,768]{1,0:T(8,128)(2,1)} %copy-done.35, bf16[256,768]{1,0:T(8,128)(2,1)} %get-tuple-element.167.refs_2_, bf16[1024,768]{1,0:T(8,128)(2,1)} %copy-done.25, bf16[1024,768]{1,0:T(8,128)(2,1)} %get-tuple-element.168.refs_4_, ...), custom_call_target="tpu_custom_call" | custom-call | flops 4127195136 | bytes 5505024 | tf_op jit(solution)/shard_map/grad_pack/pallas_call | solution.py:486
  543.0 5.0 collective-permute-done.19
  565.6 3.6 all-to-all-start.6
  569.3 20.4 %collective-permute-done.21 = bf16[2,112,768]{2,1,0:T(8,128)(2,1)} collective-permute-done((bf16[2,112,768]{2,1,0:T(8,128)(2,1)}, bf16[2,112,768]{2,1,0:T(8,128)(2,1)}, u32[]{:S(2)}, u32[]{:S(2)}) %collective-permute-start.21) | collective-permute-done | bytes 344096 | tf_op jit(solution)/shard_map/ppermute | solution.py:372
  594.5 15.8 %multiply_reduce_fusion.2 = (f32[1024]{0:T(1024)S(1)}, f32[1024,768]{0,1:T(8,128)}) fusion(bf16[3072,768]{1,0:T(8,128)(2,1)} %bitcast.245, bf16[768,3072]{1,0:T(8,128)(2,1)} %bitcast.239, f32[1024,768]{1,0:T(8,128)S(1)} %copy-done.2, f32[768]{0:T(1024)S(1)} %copy-done.75, f32[1024]{0:T(1024)S(1)} %add_rsqrt_fusion, f32[1024]{0:T(1024)S(1)} %broadcast_multiply_fusion.1), kind=kOutput, calls=%fused_computation.79 | convolution fusion | flops 9696705536 | bytes 15744000 | tf_op jit(solution)/shard_map/dot_general | solution.py:833
  610.3 3.5 copy.128
  613.8 13.4 %collective-permute-done.22 = bf16[2,112,768]{2,1,0:T(8,128)(2,1)S(1)} collective-permute-done((bf16[2,112,768]{2,1,0:T(8,128)(2,1)}, bf16[2,112,768]{2,1,0:T(8,128)(2,1)S(1)}, u32[]{:S(2)}, u32[]{:S(2)}) %collective-permute-start.22) | collective-permute-done | bytes 344096 | tf_op jit(solution)/shard_map/ppermute | solution.py:372
  628.9 13.0 %collective-permute-start.23 = (bf16[2,112,768]{2,1,0:T(8,128)(2,1)S(1)}, bf16[2,112,768]{2,1,0:T(8,128)(2,1)S(1)}, u32[]{:S(2)}, u32[]{:S(2)}) collective-permute-start(bf16[2,112,768]{2,1,0:T(8,128)(2,1)S(1)} %get-tuple-element.333), channel_id=1, source_target_pairs={{0,8},{4,0},{8,16},{12,4},{16,24},{20,12},{24,28},{28,20},{1,9},{5... | collective-permute-start | bytes 1032200 | tf_op jit(solution)/shard_map/ppermute | solution.py:372
  660.9 4.9 collective-permute-done.29
  668.2 32.8 %head_grad.1 = f32[1032,768]{1,0:T(8,128)} custom-call(bf16[1032,768]{1,0:T(8,128)(2,1)S(1)} %copy-done.32, bf16[8192,896]{1,0:T(8,128)(2,1)} %all-gather.6.cloned.1.call-done.rows_ref, f32[4,1,2048]{2,1,0:T(1,128)} %fusion.84.weight_ref), custom_call_target="tpu_custom_call" | custom-call | flops 25971130368 | bytes 17338368 | tf_op jit(solution)/shard_map/head_grad/pallas_call | solution.py:352
  701.0 5.9 fusion.35
  712.5 3.2 stack.67
  716.3 4.0 all-to-all-start.7
  720.9 6.5 all-to-all-done.7
  736.1 5.1 fusion.104
  (484 shorter events, 192.2 us)
Async XLA Ops:
  7.2 144.7 %all-gather.8.cloned.1.call-start = ((), (), s32[]{:S(2)}) async-start(), calls=%async_computation.9 | async-start | bytes 6488064 | tf_op jit(solution)/shard_map/all_gather | solution.py:611
  10.8 238.0 %all-gather.10.cloned.1.call-start = ((), (), s32[]{:S(2)}) async-start(), calls=%async_computation.10 | async-start | bytes 9732096 | tf_op jit(solution)/shard_map/all_gather | solution.py:611
  12.9 59.8 %copy-start.30 = (bf16[1032,768]{1,0:T(8,128)(2,1)}, bf16[1032,768]{1,0:T(8,128)(2,1)S(1)}, u32[]{:S(2)}) copy-start(bf16[1032,768]{1,0:T(8,128)(2,1)S(1)} %convert_element_type.420.refs_1_.table_ref) | copy-start | bytes 4755460
  12.9 59.8 %collective-permute-start = (bf16[1032,768]{1,0:T(8,128)(2,1)S(1)}, bf16[1032,768]{1,0:T(8,128)(2,1)}, u32[]{:S(2)}, u32[]{:S(2)}) collective-permute-start(bf16[1032,768]{1,0:T(8,128)(2,1)S(1)} %convert_element_type.420.refs_1_.table_ref), channel_id=1, source_target_pairs={{0,8},{4,0},{8,16},{12,4},{16,24},{20,12},{24,28},{28,20},{1,9},{5... | collective-permute-start | bytes 4755464 | tf_op jit(solution)/shard_map/ppermute | solution.py:372
  16.0 56.8 %collective-permute-start.1 = (bf16[1032,768]{1,0:T(8,128)(2,1)S(1)}, bf16[1032,768]{1,0:T(8,128)(2,1)}, u32[]{:S(2)}, u32[]{:S(2)}) collective-permute-start(bf16[1032,768]{1,0:T(8,128)(2,1)S(1)} %convert_element_type.420.refs_1_.table_ref), channel_id=1, source_target_pairs={{0,4},{4,12},{8,0},{12,20},{16,8},{20,28},{24,16},{28,24},{1,5},{5... | collective-permute-start | bytes 4755464 | tf_op jit(solution)/shard_map/ppermute | solution.py:372
  19.4 144.3 %copy-start.102 = (pred[1024]{0:T(1024)(128)(4,1)}, pred[1024]{0:T(1024)(128)(4,1)S(1)}, u32[]{:S(2)}) copy-start(pred[1024]{0:T(1024)(128)(4,1)S(1)} %get-tuple-element.401) | copy-start | bytes 3076
  23.4 124.0 %copy-start.105 = (s32[1024]{0:T(1024)}, s32[1024]{0:T(1024)S(1)}, u32[]{:S(2)}) copy-start(s32[1024]{0:T(1024)S(1)} %get-tuple-element.369) | copy-start | bytes 12292
  72.8 72.6 %all-to-all-start.5 = ((bf16[32,48,768]{2,1,0:T(8,128)(2,1)}), bf16[32,48,768]{2,1,0:T(8,128)(2,1)S(1)}, u32[]{:S(2)}, u32[]{:S(2)}) async-start(bf16[32,48,768]{2,1,0:T(8,128)(2,1)} %bitcast.257), calls=%async_computation.5 | async-start | bytes 4718592 | tf_op jit(solution)/shard_map/all_to_all | solution.py:657
  75.6 592.6 %all-gather.6.cloned.1.call-start = ((), (), s32[]{:S(2)}) async-start(), calls=%async_computation.8 | async-start | bytes 15138816 | tf_op jit(solution)/shard_map/all_gather | solution.py:762
  79.1 84.7 %copy-start.42 = (bf16[1024,128]{1,0:T(8,128)(2,1)}, bf16[1024,128]{1,0:T(8,128)(2,1)S(1)}, u32[]{:S(2)}) copy-start(bf16[1024,128]{1,0:T(8,128)(2,1)S(1)} %fusion.73) | copy-start | bytes 786436
  145.4 65.8 %collective-permute-start.4 = (bf16[1032,768]{1,0:T(8,128)(2,1)}, bf16[1032,768]{1,0:T(8,128)(2,1)}, u32[]{:S(2)}, u32[]{:S(2)}) collective-permute-start(bf16[1032,768]{1,0:T(8,128)(2,1)} %collective-permute-done.refs_2_), channel_id=1, source_target_pairs={{0,8},{4,0},{8,16},{12,4},{16,24},{20,12},{24,28},{28,20},{1,9},{5... | collective-permute-start | bytes 4755464 | tf_op jit(solution)/shard_map/ppermute | solution.py:372
  146.8 74.4 %collective-permute-start.5 = (bf16[1032,768]{1,0:T(8,128)(2,1)}, bf16[1032,768]{1,0:T(8,128)(2,1)}, u32[]{:S(2)}, u32[]{:S(2)}) collective-permute-start(bf16[1032,768]{1,0:T(8,128)(2,1)} %collective-permute-done.1.refs_3_), channel_id=1, source_target_pairs={{0,4},{4,12},{8,0},{12,20},{16,8},{20,28},{24,16},{28,24},{1,5},{5... | collective-permute-start | bytes 4755464 | tf_op jit(solution)/shard_map/ppermute | solution.py:372
  221.2 53.3 %collective-permute-start.6 = (bf16[1032,768]{1,0:T(8,128)(2,1)}, bf16[1032,768]{1,0:T(8,128)(2,1)}, u32[]{:S(2)}, u32[]{:S(2)}) collective-permute-start(bf16[1032,768]{1,0:T(8,128)(2,1)} %collective-permute-done.4.refs_4_), channel_id=1, source_target_pairs={{0,8},{4,0},{8,16},{12,4},{16,24},{20,12},{24,28},{28,20},{1,9},{5... | collective-permute-start | bytes 4755464 | tf_op jit(solution)/shard_map/ppermute | solution.py:372
  221.2 53.3 %collective-permute-start.7 = (bf16[1032,768]{1,0:T(8,128)(2,1)}, bf16[1032,768]{1,0:T(8,128)(2,1)}, u32[]{:S(2)}, u32[]{:S(2)}) collective-permute-start(bf16[1032,768]{1,0:T(8,128)(2,1)} %collective-permute-done.5.refs_5_), channel_id=1, source_target_pairs={{0,4},{4,12},{8,0},{12,20},{16,8},{20,28},{24,16},{28,24},{1,5},{5... | collective-permute-start | bytes 4755464 | tf_op jit(solution)/shard_map/ppermute | solution.py:372
  223.5 22.4 %copy-start.73 = (f32[768]{0:T(1024)}, f32[768]{0:T(1024)S(1)}, u32[]{:S(2)}) copy-start(f32[768]{0:T(1024)S(1)} %mul.569) | copy-start | bytes 9220
  227.3 15.9 %copy-start.16 = (bf16[32,24,768]{2,1,0:T(8,128)(2,1)S(1)}, bf16[32,24,768]{2,1,0:T(8,128)(2,1)}, u32[]{:S(2)}) copy-start(bf16[32,24,768]{2,1,0:T(8,128)(2,1)} %get-tuple-element.331) | copy-start | bytes 3538948
  264.6 9.7 %collective-permute-start.2 = (bf16[256,768]{1,0:T(8,128)(2,1)S(1)}, bf16[256,768]{1,0:T(8,128)(2,1)S(1)}, u32[]{:S(2)}, u32[]{:S(2)}) collective-permute-start(bf16[256,768]{1,0:T(8,128)(2,1)S(1)} %get-tuple-element.304), channel_id=1, source_target_pairs={{0,2},{1,3},{2,0},{3,1},{4,6},{5,7},{6,4},{7,5},{8,10},{9,11},{10,... | collective-permute-start | bytes 1179656 | tf_op jit(solution)/shard_map/ppermute | solution.py:372
  274.4 5.0 collective-permute-start.3
  275.8 31.1 %collective-permute-start.9 = (bf16[520,768]{1,0:T(8,128)(2,1)S(1)}, bf16[520,768]{1,0:T(8,128)(2,1)S(1)}, u32[]{:S(2)}, u32[]{:S(2)}) collective-permute-start(bf16[520,768]{1,0:T(8,128)(2,1)S(1)} %slice.242), channel_id=1, source_target_pairs={{0,4},{4,12},{8,0},{12,20},{16,8},{20,28},{24,16},{28,24},{1,5},{5... | collective-permute-start | bytes 2396168 | tf_op jit(solution)/shard_map/ppermute | solution.py:372
  277.4 29.6 %collective-permute-start.8 = (bf16[512,768]{1,0:T(8,128)(2,1)S(1)}, bf16[512,768]{1,0:T(8,128)(2,1)}, u32[]{:S(2)}, u32[]{:S(2)}) collective-permute-start(bf16[512,768]{1,0:T(8,128)(2,1)S(1)} %slice.241), channel_id=1, source_target_pairs={{0,8},{4,0},{8,16},{12,4},{16,24},{20,12},{24,28},{28,20},{1,9},{5... | collective-permute-start | bytes 2359304 | tf_op jit(solution)/shard_map/ppermute | solution.py:372
  330.1 2.5 collective-permute-start.10
  341.0 12.6 %collective-permute-start.11 = (bf16[256,896]{1,0:T(8,128)(2,1)S(1)}, bf16[256,896]{1,0:T(8,128)(2,1)S(1)}, u32[]{:S(2)}, u32[]{:S(2)}) collective-permute-start(bf16[256,896]{1,0:T(8,128)(2,1)S(1)} %get-tuple-element.344), channel_id=1, source_target_pairs={{0,2},{1,3},{2,0},{3,1},{4,6},{5,7},{6,4},{7,5},{8,10},{9,11},{10,... | collective-permute-start | bytes 1376264 | tf_op jit(solution)/shard_map/ppermute | solution.py:372
  380.0 16.8 %copy-start.78 = (s32[8]{0:T(128)S(1)}, s32[8]{0:T(128)}, u32[]{:S(2)}) copy-start(s32[8]{0:T(128)} %constant.350.clone) | copy-start | bytes 100
  389.6 15.4 %copy-start.43 = (bf16[1024,128]{1,0:T(8,128)(2,1)S(1)}, bf16[1024,128]{1,0:T(8,128)(2,1)}, u32[]{:S(2)}) copy-start(bf16[1024,128]{1,0:T(8,128)(2,1)} %copy-done.42) | copy-start | bytes 786436
  389.6 11.8 %collective-permute-start.12 = (bf16[16,224,768]{2,1,0:T(8,128)(2,1)}, bf16[16,224,768]{2,1,0:T(8,128)(2,1)}, u32[]{:S(2)}, u32[]{:S(2)}) collective-permute-start(bf16[16,224,768]{2,1,0:T(8,128)(2,1)} %get-tuple-element.164), channel_id=1, source_target_pairs={{0,1},{1,0},{2,3},{3,2},{4,5},{5,4},{6,7},{7,6},{8,9},{9,8},{10,11... | collective-permute-start | bytes 16515080 | tf_op jit(solution)/shard_map/ppermute | solution.py:372
  404.7 25.3 %collective-permute-start.13 = (bf16[2,224,768]{2,1,0:T(8,128)(2,1)}, bf16[2,224,768]{2,1,0:T(8,128)(2,1)}, u32[]{:S(2)}, u32[]{:S(2)}) collective-permute-start(bf16[2,224,768]{2,1,0:T(8,128)(2,1)} %get-tuple-element.326), channel_id=1, source_target_pairs={{0,8},{4,0},{8,16},{12,4},{16,24},{20,12},{24,28},{28,20},{1,9},{5... | collective-permute-start | bytes 2064392 | tf_op jit(solution)/shard_map/ppermute | solution.py:372
  428.1 47.5 %collective-permute-start.14 = (bf16[2,224,768]{2,1,0:T(8,128)(2,1)S(1)}, bf16[2,224,768]{2,1,0:T(8,128)(2,1)S(1)}, u32[]{:S(2)}, u32[]{:S(2)}) collective-permute-start(bf16[2,224,768]{2,1,0:T(8,128)(2,1)S(1)} %copy-done.44), channel_id=1, source_target_pairs={{0,4},{4,12},{8,0},{12,20},{16,8},{20,28},{24,16},{28,24},{1,5},{5... | collective-permute-start | bytes 2064392 | tf_op jit(solution)/shard_map/ppermute | solution.py:372
  431.8 43.8 %collective-permute-start.15 = (bf16[2,224,768]{2,1,0:T(8,128)(2,1)S(1)}, bf16[2,224,768]{2,1,0:T(8,128)(2,1)S(1)}, u32[]{:S(2)}, u32[]{:S(2)}) collective-permute-start(bf16[2,224,768]{2,1,0:T(8,128)(2,1)S(1)} %fusion.59), channel_id=1, source_target_pairs={{0,8},{4,0},{8,16},{12,4},{16,24},{20,12},{24,28},{28,20},{1,9},{5... | collective-permute-start | bytes 2064392 | tf_op jit(solution)/shard_map/ppermute | solution.py:372
  455.3 26.1 %copy-start.27 = (bf16[32,24,1536]{2,1,0:T(8,128)(2,1)S(1)}, bf16[32,24,1536]{2,1,0:T(8,128)(2,1)}, u32[]{:S(2)}) copy-start(bf16[32,24,1536]{2,1,0:T(8,128)(2,1)} %slice.293) | copy-start | bytes 7077892
  479.2 17.6 %collective-permute-start.16 = (bf16[2,224,768]{2,1,0:T(8,128)(2,1)}, bf16[2,224,768]{2,1,0:T(8,128)(2,1)}, u32[]{:S(2)}, u32[]{:S(2)}) collective-permute-start(bf16[2,224,768]{2,1,0:T(8,128)(2,1)} %get-tuple-element.324), channel_id=1, source_target_pairs={{0,4},{4,12},{8,0},{12,20},{16,8},{20,28},{24,16},{28,24},{1,5},{5... | collective-permute-start | bytes 2064392 | tf_op jit(solution)/shard_map/ppermute | solution.py:372
  481.4 17.5 %collective-permute-start.17 = (bf16[2,224,768]{2,1,0:T(8,128)(2,1)}, bf16[2,224,768]{2,1,0:T(8,128)(2,1)}, u32[]{:S(2)}, u32[]{:S(2)}) collective-permute-start(bf16[2,224,768]{2,1,0:T(8,128)(2,1)} %get-tuple-element.323), channel_id=1, source_target_pairs={{0,8},{4,0},{8,16},{12,4},{16,24},{20,12},{24,28},{28,20},{1,9},{5... | collective-permute-start | bytes 2064392 | tf_op jit(solution)/shard_map/ppermute | solution.py:372
  502.6 24.0 %collective-permute-start.18 = (bf16[2,224,768]{2,1,0:T(8,128)(2,1)}, bf16[2,224,768]{2,1,0:T(8,128)(2,1)}, u32[]{:S(2)}, u32[]{:S(2)}) collective-permute-start(bf16[2,224,768]{2,1,0:T(8,128)(2,1)} %get-tuple-element.322), channel_id=1, source_target_pairs={{0,4},{4,12},{8,0},{12,20},{16,8},{20,28},{24,16},{28,24},{1,5},{5... | collective-permute-start | bytes 2064392 | tf_op jit(solution)/shard_map/ppermute | solution.py:372
  542.5 22.6 %copy-start.2 = (f32[1024,768]{1,0:T(8,128)S(1)}, f32[1024,768]{1,0:T(8,128)}, u32[]{:S(2)}) copy-start(f32[1024,768]{1,0:T(8,128)} %get-tuple-element.302) | copy-start | bytes 9437188
  542.6 5.4 collective-permute-start.19
  550.2 11.2 %collective-permute-start.20 = (bf16[2,112,768]{2,1,0:T(8,128)(2,1)}, bf16[2,112,768]{2,1,0:T(8,128)(2,1)}, u32[]{:S(2)}, u32[]{:S(2)}) collective-permute-start(bf16[2,112,768]{2,1,0:T(8,128)(2,1)} %get-tuple-element.337), channel_id=1, source_target_pairs={{0,8},{4,0},{8,16},{12,4},{16,24},{20,12},{24,28},{28,20},{1,9},{5... | collective-permute-start | bytes 1032200 | tf_op jit(solution)/shard_map/ppermute | solution.py:372
  556.4 97.6 %collective-permute-start.28 = (bf16[2,224,768]{2,1,0:T(8,128)(2,1)}, bf16[2,224,768]{2,1,0:T(8,128)(2,1)}, u32[]{:S(2)}, u32[]{:S(2)}) collective-permute-start(bf16[2,224,768]{2,1,0:T(8,128)(2,1)} %get-tuple-element.321), channel_id=1, source_target_pairs={{0,8},{4,0},{8,16},{12,4},{16,24},{20,12},{24,28},{28,20},{1,9},{5... | collective-permute-start | bytes 2064392 | tf_op jit(solution)/shard_map/ppermute | solution.py:372
  557.4 11.9 %collective-permute-start.24 = (bf16[2,112,768]{2,1,0:T(8,128)(2,1)S(1)}, bf16[2,112,768]{2,1,0:T(8,128)(2,1)}, u32[]{:S(2)}, u32[]{:S(2)}) collective-permute-start(bf16[2,112,768]{2,1,0:T(8,128)(2,1)S(1)} %get-tuple-element.338), channel_id=1, source_target_pairs={{0,4},{4,12},{8,0},{12,20},{16,8},{20,28},{24,16},{28,24},{1,5},{5... | collective-permute-start | bytes 1032200 | tf_op jit(solution)/shard_map/ppermute | solution.py:372
  563.4 26.3 %collective-permute-start.21 = (bf16[2,112,768]{2,1,0:T(8,128)(2,1)}, bf16[2,112,768]{2,1,0:T(8,128)(2,1)}, u32[]{:S(2)}, u32[]{:S(2)}) collective-permute-start(bf16[2,112,768]{2,1,0:T(8,128)(2,1)} %fusion.70), channel_id=1, source_target_pairs={{0,8},{4,0},{8,16},{12,4},{16,24},{20,12},{24,28},{28,20},{1,9},{5... | collective-permute-start | bytes 1032200 | tf_op jit(solution)/shard_map/ppermute | solution.py:372
  565.6 28.9 %copy-start.75 = (f32[768]{0:T(1024)S(1)}, f32[768]{0:T(1024)}, u32[]{:S(2)}) copy-start(f32[768]{0:T(1024)} %copy-done.73) | copy-start | bytes 9220
  565.6 92.8 %all-to-all-start.6 = ((bf16[32,48,768]{2,1,0:T(8,128)(2,1)}), bf16[32,48,768]{2,1,0:T(8,128)(2,1)}, u32[]{:S(2)}, u32[]{:S(2)}) async-start(bf16[32,48,768]{2,1,0:T(8,128)(2,1)} %bitcast.255), calls=%async_computation.6 | async-start | bytes 4718592 | tf_op jit(solution)/shard_map/all_to_all | solution.py:668
  592.3 34.9 %collective-permute-start.22 = (bf16[2,112,768]{2,1,0:T(8,128)(2,1)}, bf16[2,112,768]{2,1,0:T(8,128)(2,1)S(1)}, u32[]{:S(2)}, u32[]{:S(2)}) collective-permute-start(bf16[2,112,768]{2,1,0:T(8,128)(2,1)} %get-tuple-element.335), channel_id=1, source_target_pairs={{0,8},{4,0},{8,16},{12,4},{16,24},{20,12},{24,28},{28,20},{1,9},{5... | collective-permute-start | bytes 1032200 | tf_op jit(solution)/shard_map/ppermute | solution.py:372
  592.3 34.9 %collective-permute-start.25 = (bf16[2,112,768]{2,1,0:T(8,128)(2,1)}, bf16[2,112,768]{2,1,0:T(8,128)(2,1)}, u32[]{:S(2)}, u32[]{:S(2)}) collective-permute-start(bf16[2,112,768]{2,1,0:T(8,128)(2,1)} %get-tuple-element.336), channel_id=1, source_target_pairs={{0,4},{4,12},{8,0},{12,20},{16,8},{20,28},{24,16},{28,24},{1,5},{5... | collective-permute-start | bytes 1032200 | tf_op jit(solution)/shard_map/ppermute | solution.py:372
  628.9 19.8 %collective-permute-start.23 = (bf16[2,112,768]{2,1,0:T(8,128)(2,1)S(1)}, bf16[2,112,768]{2,1,0:T(8,128)(2,1)S(1)}, u32[]{:S(2)}, u32[]{:S(2)}) collective-permute-start(bf16[2,112,768]{2,1,0:T(8,128)(2,1)S(1)} %get-tuple-element.333), channel_id=1, source_target_pairs={{0,8},{4,0},{8,16},{12,4},{16,24},{20,12},{24,28},{28,20},{1,9},{5... | collective-permute-start | bytes 1032200 | tf_op jit(solution)/shard_map/ppermute | solution.py:372
  641.8 9.8 %collective-permute-start.26 = (bf16[2,112,768]{2,1,0:T(8,128)(2,1)S(1)}, bf16[2,112,768]{2,1,0:T(8,128)(2,1)S(1)}, u32[]{:S(2)}, u32[]{:S(2)}) collective-permute-start(bf16[2,112,768]{2,1,0:T(8,128)(2,1)S(1)} %get-tuple-element.334), channel_id=1, source_target_pairs={{0,4},{4,12},{8,0},{12,20},{16,8},{20,28},{24,16},{28,24},{1,5},{5... | collective-permute-start | bytes 1032200 | tf_op jit(solution)/shard_map/ppermute | solution.py:372
  652.9 5.5 collective-permute-start.27
  658.5 7.3 collective-permute-start.29
  668.1 32.9 %copy-start.99 = (s32[1536]{0:T(1024)S(1)}, s32[1536]{0:T(1024)}, u32[]{:S(2)}) copy-start(s32[1536]{0:T(1024)} %copy-done.98) | copy-start | bytes 18436
  716.3 11.1 %all-to-all-start.7 = ((f32[32,1,128]{2,1,0:T(1,128)}), f32[32,1,128]{2,1,0:T(1,128)S(1)}, u32[]{:S(2)}, u32[]{:S(2)}) async-start(f32[32,1,128]{2,1,0:T(1,128)} %broadcast_in_dim.199), calls=%async_computation.7 | async-start | bytes 32768 | tf_op jit(solution)/shard_map/all_to_all | solution.py:422
  (111 other events, 583.7 us)
Sparse Core Ops, SparseCore 0:
  11.5 97.7 all-gather.7
  112.8 110.2 all-gather.9
  358.8 119.3 all-gather.5

commit v2 on v1

--- a/solution.py
+++ b/solution.py
@@ -28,6 +28,7 @@
 SCALE = HDIM ** (-0.5)
 SCALE_LOG2 = SCALE * math.log2(math.e)
 VMEM = 56 * 2**20
+HEAD_BLOCK = 2048
 bf16 = jnp.bfloat16
 f32 = jnp.float32
 
@@ -234,33 +235,109 @@
     )(first, queries, key_values, key_values, attended, grad_attended, lse)
 
 
-def split_high(values):
-    high = lax.reduce_precision(values, 8, 7)
-    return high, values - high
-
-
-def with_lse(packed):
-    lse = packed[..., D : D + 3].astype(f32)
-    return packed[..., :D].astype(f32), lse[..., 0:1] + lse[..., 1:2] + lse[..., 2:3]
-
-
-def pack_lse(mean, lse):
-    high, low = split_high(lse)
-    low, rest = split_high(low)
-    return jnp.concatenate(
-        [mean, high, low, rest, jnp.zeros(mean.shape[:-1] + (LANES - 3,), f32)], -1
-    ).astype(bf16)
-
-
-def merge(first, second):
-    joint = jnp.logaddexp(first[1], second[1])
-    mean = first[0] * jnp.exp(first[1] - joint) + second[0] * jnp.exp(second[1] - joint)
-    return mean, joint
+def first_back_kernel(
+    bounds_ref, k_ref, v_ref, wkv_ref, q_ref, wq_ref, x_ref, gain_ref, middle_ref, target_ref,
+    patch_ref, looked_ref, dgain_ref, normed, residual, pulled,
+):
+    length, block = x_ref.shape[0], 128
+    first = bounds_ref[0]
+    normed[0:length, :] = nt(k_ref[...], wkv_ref[:, :D]) + nt(v_ref[...], wkv_ref[:, D:])
+    residual[...] = jnp.zeros_like(residual)
+    pulled[...] = jnp.zeros_like(pulled)
+
+    def place(ref, rows, start):
+        base = pl.multiple_of(start // 8 * 8, 8)
+        padded = jnp.concatenate([rows, jnp.zeros((8, D), f32)], 0)
+        turned = pltpu.roll(padded, start - base, 0)
+        at = pl.ds(base, rows.shape[0] + 8)
+        ref[at, :] = ref[at, :] + turned
+
+    place(normed, nt(q_ref[...], wq_ref[...]), first - 1)
+    place(residual, middle_ref[...], first - 1)
+    place(pulled, target_ref[...], first)
+    gain = gain_ref[...]
+    dgain = jnp.zeros((1, D), f32)
+    for start in range(0, length, block):
+        at = slice(start, start + block)
+        x, grad = x_ref[at, :], normed[at, :]
+        centred = x - jnp.mean(x, 1, keepdims=True)
+        spread = lax.rsqrt(jnp.mean(centred * centred, 1, keepdims=True) + NORM_EPS)
+        unit = centred * spread
+        dgain = dgain + jnp.sum(grad * unit, 0, keepdims=True)
+        scaled = grad * gain
+        inner = jnp.mean(scaled * unit, 1, keepdims=True)
+        back = spread * (scaled - jnp.mean(scaled, 1, keepdims=True) - unit * inner)
+        back = back + residual[at, :]
+        row = start + lax.broadcasted_iota(jnp.int32, (block, 1), 0)
+        patch_ref[at, :] = jnp.where(row < first, back, 0.0).astype(bf16)
+        looked_ref[at, :] = (math.sqrt(D) * back + pulled[at, :]).astype(bf16)
+    dgain_ref[...] = dgain
+
+
+def first_back(first, grad_k, grad_v, w_kv, grad_q, w_q, embedded, gain, middle, target):
+    length = embedded.shape[0]
+    wide = jax.ShapeDtypeStruct((length, D), bf16)
+    return pl.pallas_call(
+        first_back_kernel,
+        in_specs=[pl.BlockSpec(memory_space=pltpu.SMEM)]
+        + [pl.BlockSpec(memory_space=pltpu.VMEM)] * 9,
+        out_specs=[pl.BlockSpec(memory_space=pltpu.VMEM)] * 3,
+        out_shape=[wide, wide, jax.ShapeDtypeStruct((1, D), f32)],
+        scratch_shapes=[pltpu.VMEM((length + 16, D), f32)] * 3,
+        compiler_params=pltpu.CompilerParams(vmem_limit_bytes=VMEM),
+        cost_estimate=pl.CostEstimate(
+            flops=2 * length * 2 * D * D, bytes_accessed=16 * length * D, transcendentals=0
+        ),
+        name="first_back",
+    )(first, grad_k, grad_v, w_kv, grad_q, w_q, embedded, gain, middle, target)
+
+
+def write_with_lse(ref, mean, lse):
+    ref[:, :D] = mean.astype(bf16)
+    high = lse.astype(bf16).astype(f32)
+    low = (lse - high).astype(bf16).astype(f32)
+    rest = lse - high - low
+    lane = lax.broadcasted_iota(jnp.int32, (1, LANES), 1)
+    tail = jnp.where(lane == 0, high, jnp.where(lane == 1, low, jnp.where(lane == 2, rest, 0.0)))
+    ref[:, D:] = tail.astype(bf16)
+
+
+def merge_kernel(*refs, count, last):
+    means, sums = [], []
+    for ref in refs[:count]:
+        means.append(ref[:, :D].astype(f32))
+        tail = ref[:, D:].astype(f32)
+        sums.append(tail[:, 0:1] + tail[:, 1:2] + tail[:, 2:3])
+    top = sums[0]
+    for value in sums[1:]:
+        top = jnp.maximum(top, value)
+    powers = [jnp.exp(value - top) for value in sums]
+    total = sum(powers[1:], powers[0])
+    mean = sum((m * p for m, p in zip(means[1:], powers[1:])), means[0] * powers[0]) / total
+    lse = top + jnp.log(total)
+    if last:
+        refs[count][...], refs[count + 1][...] = mean, lse
+    else:
+        write_with_lse(refs[count], mean, lse)
+
+
+def merge(parts, last=False):
+    rows = parts[0].shape[0]
+    shapes = [jax.ShapeDtypeStruct((rows, D + LANES), bf16)]
+    if last:
+        shapes = [jax.ShapeDtypeStruct((rows, D), f32), jax.ShapeDtypeStruct((rows, 1), f32)]
+    return pl.pallas_call(
+        lambda *refs: merge_kernel(*refs, count=len(parts), last=last),
+        in_specs=[pl.BlockSpec(memory_space=pltpu.VMEM)] * len(parts),
+        out_specs=[pl.BlockSpec(memory_space=pltpu.VMEM)] * len(shapes),
+        out_shape=shapes,
+        compiler_params=pltpu.CompilerParams(vmem_limit_bytes=VMEM),
+        name="merge",
+    )(*parts)
 
 
 def head_scan_kernel(rows_ref, *refs, carried, last):
-    split = len(refs) - (1 if last else 2)
-    refs, outs = refs[:split], refs[split:]
+    refs, outs = refs[:-2], refs[-2:]
     rows = rows_ref[...]
     top = total = mixed = None
     if carried:
@@ -286,26 +363,24 @@
             mixed = mixed * shrink + nn(power.astype(bf16), chunk)
             top = joint
     lse = top + jnp.log(total)
-    if len(outs) == 2:
+    if not last:
         outs[0][...], outs[1][...] = mixed / total, lse
     else:
-        outs[0][:, :D] = (mixed / total).astype(bf16)
-        high = lse.astype(bf16).astype(f32)
-        low = (lse - high).astype(bf16).astype(f32)
-        rest = lse - high - low
-        lane = lax.broadcasted_iota(jnp.int32, (1, LANES), 1)
-        tail = jnp.where(lane == 0, high, jnp.where(lane == 1, low, jnp.where(lane == 2, rest, 0.0)))
-        outs[0][:, D:] = tail.astype(bf16)
+        for part in range(2):
+
+            @pl.when(pl.program_id(0) == part)
+            def _():
+                write_with_lse(outs[part], mixed / total, lse)
 
 
 def head_scan(rows, chunks, carry=(), last=True):
-    count, block = rows.shape[0], 512
+    count, block = rows.shape[0], rows.shape[0] // 2
     vocab = sum(chunk.shape[0] for chunk in chunks)
     wide = pl.BlockSpec((block, D), lambda i: (i, 0))
     thin = pl.BlockSpec((block, 1), lambda i: (i, 0))
     if last:
-        out_specs = [pl.BlockSpec((block, D + LANES), lambda i: (i, 0))]
-        out_shape = [jax.ShapeDtypeStruct((count, D + LANES), bf16)]
+        out_specs = [pl.BlockSpec((block, D + LANES), lambda i: (0, 0))] * 2
+        out_shape = [jax.ShapeDtypeStruct((block, D + LANES), bf16)] * 2
     else:
         out_specs = [wide, thin]
         out_shape = [jax.ShapeDtypeStruct((count, D), f32), jax.ShapeDtypeStruct((count, 1), f32)]
@@ -329,43 +404,42 @@
     )(rows, *carry, *chunks)
 
 
-def head_grad_kernel(table_ref, rows_ref, weight_ref, out_ref):
-    rows = rows_ref[:, :D]
-    tail = rows_ref[:, D:].astype(f32).T
+def head_grad_kernel(table_ref, rows_ref, lse_ref, weight_ref, *refs):
+    out_ref = refs[-1]
+    rows = rows_ref[...]
     logits = nt(table_ref[...], rows)
-    lse = tail[0:1] + tail[1:2] + tail[2:3]
-    grad = (jnp.exp(logits - lse) * weight_ref[0]).astype(bf16)
+    grad = (jnp.exp(logits - lse_ref[0]) * weight_ref[0]).astype(bf16)
     part = nn(grad, rows)
 
     @pl.when(pl.program_id(0) == 0)
     def _():
-        out_ref[...] = part
+        out_ref[...] = part if len(refs) == 1 else refs[0][...] + part
 
     @pl.when(pl.program_id(0) > 0)
     def _():
         out_ref[...] += part
 
 
-def head_grad(table_low, rows, weight):
-    vocab, count, block = table_low.shape[0], rows.shape[0], 2048
+def head_grad(table_low, rows, lse, weight, half, carry=()):
+    vocab, count, block = table_low.shape[0], rows.shape[0], HEAD_BLOCK
     steps = count // block
+    part = steps // 2
+    stat = pl.BlockSpec((1, 1, block), lambda i: (i + half * part, 0, 0))
+    whole = pl.BlockSpec((vocab, D), lambda i: (0, 0))
     return pl.pallas_call(
         head_grad_kernel,
-        grid=(steps,),
-        in_specs=[
-            pl.BlockSpec((vocab, D), lambda i: (0, 0)),
-            pl.BlockSpec((block, D + LANES), lambda i: (i, 0)),
-            pl.BlockSpec((1, 1, block), lambda i: (i, 0, 0)),
-        ],
-        out_specs=pl.BlockSpec((vocab, D), lambda i: (0, 0)),
+        grid=(part,),
+        in_specs=[whole, pl.BlockSpec((block, D), lambda i: (i + half * part, 0)), stat, stat]
+        + [whole] * len(carry),
+        out_specs=whole,
         out_shape=jax.ShapeDtypeStruct((vocab, D), f32),
         compiler_params=pltpu.CompilerParams(vmem_limit_bytes=VMEM),
         cost_estimate=pl.CostEstimate(
-            flops=4 * count * vocab * D, bytes_accessed=2 * count * D + 6 * vocab * D,
-            transcendentals=count * vocab,
+            flops=2 * count * vocab * D, bytes_accessed=count * D + 6 * vocab * D,
+            transcendentals=count * vocab // 2,
         ),
         name="head_grad",
-    )(table_low, rows, weight.reshape(steps, 1, block))
+    )(table_low, rows, lse.reshape(steps, 1, block), weight, *carry)
 
 
 def permute(value, axis, target):
@@ -399,27 +473,16 @@
     )
 
 
-def ring_rest(first, gates):
-    count = lax.axis_size("dp")
+def ring_middle(first, gates):
     upward, downward = first
     pieces = []
-    for step in range(2, count // 2 + 1):
+    for step in range(2, lax.axis_size("dp") // 2):
         upward, downward, _ = lax.optimization_barrier(
             (upward, downward, gates[min(step - 2, len(gates) - 1)])
         )
-        if 2 * step == count:
-            half = upward.shape[0] // 32 * 16
-            upward, downward = upward[:half], downward[half:]
         upward, downward = ring_hop(upward, downward)
         pieces += [upward, downward]
     return pieces
-
-
-def sum_everywhere(values):
-    world = lax.axis_size(AXES)
-    row = jnp.pad(values, (0, LANES - values.shape[0]))
-    spread = jnp.broadcast_to(row[None, :], (world, LANES))
-    return jnp.sum(lax.all_to_all(spread, AXES, 0, 0, tiled=True), 0)[: values.shape[0]]
 
 
 def one_hot(index, count):
@@ -437,12 +500,6 @@
         jnp.arange(count)[None, :] < jnp.arange(count)[:, None]
     ).astype(bf16)
     return jnp.dot(earlier, choice.astype(bf16), preferred_element_type=f32)
-
-
-def unblocks(packed, rows):
-    return jnp.concatenate(
-        [packed[j : j + rows] for j in range(0, packed.shape[0], rows)], 1
-    )
 
 
 def grad_pack_kernel(core_ref, *refs, plan, rows_of, world):
@@ -455,6 +512,11 @@
     for j in range(world // 2):
         mine, theirs, filled = [], [], 0
         for held, rows, column in rows_of[:-1]:
+            if column is None:
+                mine.append(refs[held][...])
+                theirs.append(mine[-1])
+                filled += rows
+                continue
             low = refs[held][2 * j * rows : (2 * j + 1) * rows, column : column + D]
             high = refs[held][(2 * j + 1) * rows : (2 * j + 2) * rows, column : column + D]
             mine.append(jnp.where(second, high, low))
@@ -479,7 +541,7 @@
         for column in range(0, right.shape[1], D):
             pieces.append((inputs + 2 + i, left.shape[1] // world, column))
     for i, value in enumerate(rows):
-        pieces.append((2 * count + i, value.shape[0] // world, 0))
+        pieces.append((2 * count + i, value.shape[0], None))
     total = -(-sum(piece[1] for piece in pieces) // 16) * 16
     pieces.append((inputs, 0, 0))
     shape = jax.ShapeDtypeStruct((world // 2, total, D), bf16)
@@ -500,30 +562,53 @@
 
 class RingSum:
 
-    def __init__(self, mine, theirs):
+    def __init__(self, mine, theirs, x_first=False, gate=None):
         self.count = lax.axis_size("dp")
         self.chips = lax.axis_size("mp") // 2
+        self.x_first = x_first
         shape = (self.count, self.chips, -1, D)
-        self.got = other_core(theirs).reshape(shape)
-        self.mine = mine.reshape(shape)
-        self.order = ring_order(self.count)
-        spot = [self.order.index(i) for i in range(self.count)]
-        self.here = jnp.asarray(spot, jnp.int32)[lax.axis_index("dp")]
+        got = other_core(theirs)
+        got = (got if gate is None else after(got, gate)).reshape(shape)
+        self.terms = [mine.reshape(shape), got]
+        if x_first:
+            chip = lax.axis_index("mp") // 2
+
+            def for_chip(index):
+                return sum(
+                    lax.dynamic_index_in_dim(term, index, 1, keepdims=False).astype(f32)
+                    for term in self.terms
+                ).astype(bf16)
+
+            self.terms = [for_chip(chip)] + [
+                along_x(for_chip((chip + step) % self.chips), step)
+                for step in range(1, self.chips)
+            ]
+        side, at = lax.axis_index("dp") % 2, lax.axis_index("dp") // 2
+        self.here = jnp.where(side == 0, at, self.count - 1 - at)
         self.up_steps, self.down_steps = self.count // 2, (self.count - 1) // 2
+        self.upward = self.downward = None
+        self.step = 0
+
+    def ready(self, *gates):
+        if gates:
+            self.terms[-1] = after(self.terms[-1], *gates)
         self.upward = self.part(self.up_steps).astype(bf16)
         self.downward = self.part(-self.down_steps).astype(bf16)
-        self.step = 0
 
     def part(self, step):
-        at = jnp.asarray(self.order, jnp.int32)[(self.here + step) % self.count]
-        return lax.dynamic_index_in_dim(self.mine, at, 0, keepdims=False).astype(f32) + (
-            lax.dynamic_index_in_dim(self.got, at, 0, keepdims=False).astype(f32)
+        spot = lax.rem(self.here + step + self.count, self.count)
+        at = jnp.where(2 * spot < self.count, 2 * spot, 2 * (self.count - 1 - spot) + 1)
+        return sum(
+            lax.dynamic_index_in_dim(term, at, 0, keepdims=False).astype(f32)
+            for term in self.terms
         )
 
-    def hop(self):
+    def hop(self, gate=None):
         self.step += 1
         step, down = self.step, self.downward
         self.upward, down = ring_hop(self.upward, down)
+        if gate is not None:
+            self.upward, down, _ = lax.optimization_barrier((self.upward, down, gate))
         if step <= self.down_steps:
             self.downward = down
         if step < self.up_steps:
@@ -533,23 +618,22 @@
                 bf16
             )
 
-    def before(self, value):
-        return lax.optimization_barrier((value, self.upward, self.downward))[0]
-
-    def total(self, gate=None):
+    def wait(self, gate):
+        self.upward, self.downward, _ = lax.optimization_barrier((self.upward, self.downward, gate))
+
+    def total(self):
         while self.step < self.up_steps:
             self.hop()
-        line = (
-            self.part(0) + self.upward.astype(f32) + self.downward.astype(f32)
-        ).astype(bf16)
-        if gate is not None:
-            line = after(line, gate)
+        line = self.part(0) + self.upward.astype(f32) + self.downward.astype(f32)
+        if self.x_first:
+            return [line]
+        line = line.astype(bf16)
         chip = lax.axis_index("mp") // 2
-        total = lax.dynamic_index_in_dim(line, chip, 0, keepdims=False).astype(f32)
+        terms = [lax.dynamic_index_in_dim(line, chip, 0, keepdims=False)]
         for step in range(1, self.chips):
             going = lax.dynamic_index_in_dim(line, (chip + step) % self.chips, 0, keepdims=False)
-            total = total + along_x(going, step).astype(f32)
-        return total
+            terms.append(along_x(going, step))
+        return terms
 
 
 def renew(weight, moment, average, gradient, factor):
@@ -558,6 +642,80 @@
     weight_new = weight - STEP_RATE * (clipped + MOMENTUM * moment_new)
     average_new = AVERAGE_DECAY * average + (1.0 - AVERAGE_DECAY) * weight_new
     return (weight_new, moment_new, average_new)
+
+
+def finish_sum_kernel(row_ref, *refs):
+    terms, (total_ref, spread_ref) = refs[:-2], refs[-2:]
+    total = sum((term[...].astype(f32) for term in terms[1:]), terms[0][...].astype(f32))
+    total_ref[...] = total
+    squares = jnp.sum(jnp.sum(total * total, 0, keepdims=True), 1, keepdims=True)
+    lane = lax.broadcasted_iota(jnp.int32, (1, LANES), 1)
+    row = row_ref[...] + jnp.where(lane == 0, squares, 0.0)
+    spread_ref[...] = jnp.broadcast_to(row, spread_ref.shape)
+
+
+def finish_sum(terms, row, world):
+    vmem = pl.BlockSpec(memory_space=pltpu.VMEM)
+    return pl.pallas_call(
+        finish_sum_kernel,
+        in_specs=[vmem] * (1 + len(terms)),
+        out_specs=[vmem] * 2,
+        out_shape=[
+            jax.ShapeDtypeStruct(terms[0].shape, f32),
+            jax.ShapeDtypeStruct((world, LANES), f32),
+        ],
+        compiler_params=pltpu.CompilerParams(vmem_limit_bytes=VMEM),
+        name="finish_sum",
+    )(row, *terms)
+
+
+def clip_factor(totals):
+    return jnp.minimum(1.0, CLIP_LIMIT / jnp.sqrt(totals[:, 0:1]))
+
+
+def renew_kernel(spread_ref, early_ref, late_ref, *refs):
+    states, outs = [refs[i : i + 3] for i in range(0, 12, 3)], refs[12:]
+    totals = jnp.sum(spread_ref[...], 0, keepdims=True)
+    outs[-1][...] = totals
+    factor = clip_factor(totals)
+    rows = states[1][0].shape[0]
+    rows_patch, rows_down = states[0][0].shape[0], states[3][0].shape[0]
+    attn = [(early_ref, j * rows, rows) for j in range(3)]
+    attn.append((late_ref, 4 * rows + rows_down, rows))
+    pieces = (
+        [(early_ref, 3 * rows, rows_patch)],
+        attn,
+        [(late_ref, j * rows, rows) for j in range(4)],
+        [(late_ref, 4 * rows, rows_down)],
+    )
+    for index, (state, parts) in enumerate(zip(states, pieces)):
+        new = outs[4 * index : 4 * index + 4]
+        for j, (ref, start, count) in enumerate(parts):
+            at = slice(j * D, (j + 1) * D)
+            gradient = ref[start : start + count, :]
+            results = renew(
+                state[0][:, at], state[1][:, at], state[2][:, at], gradient, factor
+            )
+            for out, value in zip(new, results):
+                out[:, at] = value
+            new[3][:, at] = results[0].astype(bf16)
+
+
+def renew_matrices(spread, early, late, states):
+    vmem = pl.BlockSpec(memory_space=pltpu.VMEM)
+    shapes = []
+    for state in states:
+        shape = state[0].shape
+        shapes += [jax.ShapeDtypeStruct(shape, f32)] * 3 + [jax.ShapeDtypeStruct(shape, bf16)]
+    shapes.append(jax.ShapeDtypeStruct((1, LANES), f32))
+    return pl.pallas_call(
+        renew_kernel,
+        in_specs=[vmem] * 15,
+        out_specs=[vmem] * len(shapes),
+        out_shape=shapes,
+        compiler_params=pltpu.CompilerParams(vmem_limit_bytes=VMEM),
+        name="renew_matrices",
+    )(spread, early, late, *[value for state in states for value in state])
 
 
 def shards(
@@ -611,6 +769,7 @@
         lax.all_gather(jnp.pad(w, ((0, -w.shape[0] % 8), (0, 0))), AXES, axis=0, tiled=False)
         for w in (early, late)
     )
+
     first_pieces = ring_hop(table_low, table_low)
 
     my_counts = lax.dynamic_slice_in_dim(counts, place, 1, 0)
@@ -635,9 +794,9 @@
     far_row = identity - dest * rows_own
     most = jnp.max(jnp.sum(leads_to.astype(jnp.int32), 0))
 
-    def far_slots(start, share):
+    def far_slots(start, share, limit):
         within = far_rank - start
-        fits = is_token & (within >= 0) & (within < share)
+        fits = is_token & (within >= 0) & (within < limit)
         return jnp.where(fits, dest * share + within, -1)
 
     def far_ids(slots, extra, share):
@@ -645,24 +804,28 @@
         ids = jnp.concatenate([ids, jnp.full((world, 1), extra, jnp.int32)], 1)
         return lax.all_to_all(ids, ("mp", "dp"), split_axis=0, concat_axis=0, tiled=True)
 
-    first_slots = far_slots(0, share)
+    first_slots = far_slots(0, share, share - 1)
     first_ids = far_ids(first_slots, most, share)
     few = 16
-    turns = (jnp.max(first_ids[:, share]) - share + few - 1) // few
+    turns = (jnp.max(first_ids[:, share]) - (share - 1) + few - 1) // few
 
     def far_fetch(slots, ids, share):
         spread = one_hot(ids[:, :share].reshape(-1), rows_own)
         rows = jnp.dot(spread, table_low, preferred_element_type=f32).astype(bf16)
         rows = lax.optimization_barrier((rows, *first_pieces))[0]
-        arrived = lax.all_to_all(
+        return lax.all_to_all(
             rows.reshape(world, share, D), ("mp", "dp"), split_axis=0, concat_axis=0, tiled=True
         ).reshape(world * share, D)
-        return arrived, jnp.dot(one_hot(slots, world * share), arrived, preferred_element_type=f32)
-
-    def far_pack(slots, values, share):
-        return jnp.dot(
-            one_hot(slots, world * share).T, values, preferred_element_type=f32
-        ).astype(bf16)
+
+    def far_spread(slots, arrived, share):
+        return jnp.dot(one_hot(slots, world * share), arrived, preferred_element_type=f32)
+
+    def far_pack(slots, values, share, extra=None):
+        rows = jnp.dot(one_hot(slots, world * share).T, values, preferred_element_type=f32)
+        if extra is not None:
+            spare = lax.broadcasted_iota(jnp.int32, (world * share, 1), 0) % share == share - 1
+            rows = jnp.where(spare, extra, rows)
+        return rows.astype(bf16)
 
     def far_send(packed, share):
         return lax.all_to_all(
@@ -674,13 +837,6 @@
         spread = one_hot(ids[:, :share].reshape(-1), rows_own)
         return tn(spread, arrived)
 
-    arrived, looked = far_fetch(first_slots, first_ids, share)
-
-    def fetch_turn(turn, total):
-        slots = far_slots(share + turn * few, few)
-        return total + far_fetch(slots, far_ids(slots, 0, few), few)[1]
-
-    looked = lax.fori_loop(0, turns, fetch_turn, looked)
 
     def columns(gathered, low, high):
         return gathered[:, :rows_attn, low * D : high * D].reshape(-1, (high - low) * D)
@@ -694,18 +850,38 @@
         early_all[:, gain_at, : 3 * cols_gain]
         .reshape(world, 3, cols_gain).transpose(1, 0, 2).reshape(3, D).astype(f32)
     )
+    scored_all = counts[:, 2].astype(f32)
+    per_task = (task[:, None] == jnp.arange(TASKS)[None, :]).astype(f32)
+    task_total = jnp.sum(per_task * scored_all[:, None], 0)
+    present = jnp.sum((task_total > 0).astype(f32))
+    inverse_seq = jnp.sum(per_task / jnp.maximum(task_total, 1.0)[None, :], 1)
+    row_live = (jnp.arange(LOSS)[None, :] < counts[:, 2:3]).astype(f32) * inverse_seq[:, None]
+    head_weight = (row_live / present).reshape(-1, 1, HEAD_BLOCK)
+
+    arrived = far_fetch(first_slots, first_ids, share)
+    arrived, head_weight = lax.optimization_barrier((arrived, head_weight, w_kv, w_q, w_patch))[:2]
+    looked = far_spread(first_slots, arrived, share)
+
+    def fetch_turn(turn, total):
+        slots = far_slots(share - 1 + turn * few, few, few)
+        return total + far_spread(slots, far_fetch(slots, far_ids(slots, 0, few), few), few)
+
+    looked = lax.fori_loop(0, turns, fetch_turn, looked)
+
     w_up = columns(late_all, 0, 4)
     w_down = jnp.concatenate(
         [late_all[:, rows_attn : 2 * rows_attn, j : j + D] for j in range(0, 4 * D, D)], 1
     ).reshape(world * rows_down, D)
 
-    position_code = (patch_pos[:, None] == jnp.arange(POSN)[None, :]).astype(bf16)
-    patch_in = jnp.concatenate([patches, position_code], 1)
+    def patch_rows_of(pixels):
+        position_code = (patch_pos[:, None] == jnp.arange(POSN)[None, :]).astype(bf16)
+        return jnp.concatenate([pixels, position_code], 1)
+
+    patch_in = patch_rows_of(patches)
     from_patch = jnp.dot(patch_in, w_patch, preferred_element_type=f32)
     embed_scale = math.sqrt(D)
     embedded = jnp.where(is_patch, from_patch, 0.0) + embed_scale * looked
-    normed_first, first_back = jax.vjp(layer_norm, embedded, gain_all[0])
-    normed_first = normed_first.astype(bf16)
+    normed_first = layer_norm(embedded, gain_all[0]).astype(bf16)
     key_values = jnp.dot(normed_first, w_kv, preferred_element_type=f32).astype(bf16)
 
     pick = first_tok - 1
@@ -722,7 +898,7 @@
     normed_mid, mid_back = jax.vjp(layer_norm, middle_pick, gain_all[1])
     normed_mid = normed_mid.astype(bf16)
     query_all = jnp.dot(normed_first, w_q, preferred_element_type=f32).astype(bf16)
-    attended = attention_all(query_all, key_values)
+    attended = attention_all(after(query_all, attended_pick), key_values)
     normed_mid = after(normed_mid, attended)
     hidden_pick = jnp.dot(normed_mid, w_up, preferred_element_type=f32)
     active_f32, gelu_back = jax.vjp(gelu_tanh, hidden_pick)
@@ -730,38 +906,34 @@
     result_pick = middle_pick + jnp.dot(active_pick, w_down, preferred_element_type=f32)
     final_rows, final_back = jax.vjp(layer_norm, result_pick, gain_all[2])
     own_rows = final_rows.astype(bf16)
-    pieces = ring_rest(first_pieces, (arrived, attended, own_rows))
-    chunks = [table_low, *first_pieces, *pieces]
+    chunks = [table_low, *first_pieces, *ring_middle(first_pieces, (arrived, attended))]
+    half = rows_own // 32 * 16
+    last_up, last_down = after(chunks[-2], own_rows)[:half], after(chunks[-1], own_rows)[half:]
+    chunks += ring_hop(last_up, last_down)
     target_rows = picked_rows(looked, first_tok)
 
     chips = owners // 2
     line = jnp.stack([own_rows] + [along_x(own_rows, step) for step in range(1, chips)])
     group_rows = jnp.stack([line, other_core(line)])
     group_rows = group_rows.reshape(-1, D)
-    near = 5
-    carry = head_scan(group_rows, chunks[:near], last=False)
-    (scanned,) = head_scan(group_rows, chunks[near:], carry)
-    scanned = scanned.reshape(2, chips, LOSS, D + LANES)
-    there = other_core(scanned[1])
-    line = pack_lse(*merge(with_lse(scanned[0]), with_lse(there)))
-    own = with_lse(line[0])
-    for step in range(1, chips):
-        own = merge(own, with_lse(along_x(line[step], -step)))
-    mean_own, own_total = own[0], own[1][:, 0]
+    carry = head_scan(after(group_rows, last_up, last_down), chunks[:5], last=False)
+    mine, theirs = head_scan(group_rows, chunks[5:], carry)
+    (line,) = merge([mine, other_core(theirs)])
+    mean_own, own_total = merge(
+        [line[:LOSS]]
+        + [along_x(line[step * LOSS : (step + 1) * LOSS], -step) for step in range(1, chips)],
+        last=True,
+    )
+    own_total = own_total[:, 0]
 
     picked = jnp.sum(own_rows.astype(f32) * target_rows, 1)
-    scored_all = counts[:, 2].astype(f32)
-    per_task = (task[:, None] == jnp.arange(TASKS)[None, :]).astype(f32)
-    task_total = jnp.sum(per_task * scored_all[:, None], 0)
-    present = jnp.sum((task_total > 0).astype(f32))
-    inverse_seq = jnp.sum(per_task / jnp.maximum(task_total, 1.0)[None, :], 1)
-    row_live = (jnp.arange(LOSS)[None, :] < counts[:, 2:3]).astype(f32) * inverse_seq[:, None]
     own_weight = lax.dynamic_slice_in_dim(row_live, place, 1, 0)[0]
     loss_part = jnp.sum(own_weight * (own_total - picked))
 
-    rows_all = lax.all_gather(
-        pack_lse(own_rows.astype(f32), own_total[:, None]), AXES, axis=0, tiled=True
-    )
+    rows_all = lax.all_gather(after(own_rows, mean_own), AXES, axis=0, tiled=True)
+    high = lax.reduce_precision(own_total, 8, 7)
+    low = lax.reduce_precision(own_total - high, 8, 7)
+    total_row = jnp.concatenate([high, low, own_total - high - low])[None, :]
 
     scaled_weight = (own_weight / present)[:, None]
     grad_rows = scaled_weight * (mean_own - target_rows)
@@ -771,116 +943,118 @@
     grad_middle, grad_gain_mid = mid_back(nt(grad_hidden, w_up))
     grad_middle = grad_result + grad_middle
     grad_branch = grad_middle.astype(bf16)
-    late_mine, late_theirs = grad_pack(
-        [(normed_mid, grad_hidden), (active_pick, grad_second), (attended_pick, grad_branch)],
-        [], world,
-    )
-    late_sum = RingSum(late_mine, late_theirs)
-    grad_attended = late_sum.before(nt(grad_branch, w_out).astype(bf16))
-    late_sum.hop()
+    grad_attended = nt(grad_branch, w_out).astype(bf16)
     grad_q, grad_k, grad_v = attention_back(
         pick_at, query_pick, key_values, attended_pick, grad_attended, lse_pick
     )
-    grad_kv = late_sum.before(jnp.concatenate([grad_k, grad_v], 1))
-    late_sum.hop()
-    def back_in_place(rows, start):
-        whole = jnp.zeros((tokens_here, D), f32)
-        return lax.dynamic_update_slice_in_dim(whole, rows, start, 0)
-
-    grad_normed = nt(grad_kv, w_kv) + back_in_place(nt(grad_q, w_q), pick)
-    grad_normed = late_sum.before(grad_normed)
-    late_sum.hop()
-    grad_embedded, grad_gain_first = first_back(grad_normed)
-    grad_embedded = grad_embedded + back_in_place(grad_middle, pick)
-    grad_looked = (
-        embed_scale * grad_embedded
-        + back_in_place(-scaled_weight * own_rows.astype(f32), first_tok)
-    ).astype(bf16)
-    grad_looked = late_sum.before(grad_looked)
-    packed = far_pack(first_slots, grad_looked, share)
-    grad_patch_rows = jnp.where(is_patch, grad_embedded, 0.0).astype(bf16)
-    grad_gain = jnp.stack([grad_gain_first, grad_gain_mid, grad_gain_last])
-    gain_part = grad_gain.reshape(3, world, cols_gain).transpose(1, 0, 2)
-    gain_part = jnp.pad(gain_part.reshape(world, 3 * cols_gain), ((0, 0), (0, D - 3 * cols_gain)))
+    grad_patch_rows, grad_looked, grad_gain_first = first_back(
+        jnp.reshape(first_tok, (1,)), grad_k, grad_v, w_kv, grad_q, w_q, embedded,
+        gain_all[0:1], grad_middle, -scaled_weight * own_rows.astype(f32),
+    )
+    packed = far_pack(first_slots, grad_looked, share, total_row)
+    grad_arrived = far_send(packed, share)
+    grad_gain = jnp.stack([grad_gain_first[0], grad_gain_mid, grad_gain_last])
     early_mine, early_theirs = grad_pack(
         [
             (normed_pick, grad_q),
             (normed_first, grad_k),
             (normed_first, grad_v),
-            (patch_in, after(grad_patch_rows, packed)),
+            (patch_rows_of(after(patches, packed)), after(grad_patch_rows, packed)),
         ],
-        [gain_part], world,
-    )
-    table_head = head_grad(table_low, after(rows_all, early_theirs), row_live / present)
-    grad_arrived = far_send(packed, share)
-    summed_early = RingSum(early_mine, early_theirs).total()
-    summed_late = late_sum.total(grad_arrived)
-    grad_table = table_head + far_add(grad_arrived, first_ids, share)
-
-    def next_turn(turn, total):
-        slots = far_slots(share + turn * few, few)
-        return total + far_add(
-            far_send(far_pack(slots, grad_looked, few), few), far_ids(slots, 0, few), few
-        )
-
-    grad_table = lax.fori_loop(0, turns, next_turn, grad_table)
-
-    attended = after(attended, late_theirs)
-    branch = jnp.dot(attended, w_out, preferred_element_type=f32)
+        [grad_gain], world,
+    )
+    late_mine, late_theirs = grad_pack(
+        [
+            (normed_mid, after(grad_hidden, early_theirs)),
+            (active_pick, grad_second),
+            (attended_pick, grad_branch),
+        ],
+        [], world,
+    )
+    early_sum = RingSum(early_mine, early_theirs, True)
+    late_sum = RingSum(late_mine, late_theirs)
+    late_sum.ready()
+
+    branch = jnp.dot(after(attended, late_sum.upward), w_out, preferred_element_type=f32)
     middle = embedded + branch
     normed_second = layer_norm(middle, gain_all[1]).astype(bf16)
     hidden = jnp.dot(normed_second, w_up, preferred_element_type=f32)
     second = jnp.dot(gelu_tanh(hidden).astype(bf16), w_down, preferred_element_type=f32)
     result = middle + second
 
+    grad_arrived = after(grad_arrived, normed_second)
+    spare_rows = grad_arrived.reshape(owners, groups, share, D)[:, :, share - 1].astype(f32)
+    total_all = spare_rows[..., :LOSS] + spare_rows[..., LOSS : 2 * LOSS] + spare_rows[..., 2 * LOSS :]
+    total_all = total_all.transpose(1, 0, 2)
+    late_sum.hop(grad_arrived)
+    early_sum.ready(late_sum.upward)
+    head_first = head_grad(
+        table_low, after(rows_all, late_sum.upward, early_sum.upward), total_all, head_weight, 0
+    )
+    late_sum.hop(head_first)
+    early_sum.hop(late_sum.upward)
+    table_head = head_grad(
+        table_low, after(rows_all, late_sum.upward, early_sum.upward), total_all, head_weight, 1,
+        (head_first,),
+    )
+    late_sum.hop(table_head)
+    early_sum.hop(late_sum.upward)
+    grad_table = table_head + far_add(
+        after(grad_arrived, late_sum.upward, early_sum.upward), first_ids, share
+    )
+    late_terms = late_sum.total()
+    (summed_early,) = early_sum.total()
+
+    def next_turn(turn, total):
+        slots = far_slots(share - 1 + turn * few, few, few)
+        return total + far_add(
+            far_send(far_pack(slots, grad_looked, few), few), far_ids(slots, 0, few), few
+        )
+
+    grad_table = lax.fori_loop(0, turns, next_turn, grad_table)
+
     def square_sum(values):
         return jnp.sum(jnp.where(is_valid, jnp.mean(values * values, 1, keepdims=True), 0.0))
 
-    edge = 3 * rows_attn
-    summed_up = unblocks(summed_late[: 4 * rows_attn], rows_attn)
-    summed_down = summed_late[4 * rows_attn : 4 * rows_attn + rows_down]
-    out_at = 4 * rows_attn + rows_down
-    summed_attn = jnp.concatenate(
-        [unblocks(summed_early[:edge], rows_attn), summed_late[out_at : out_at + rows_attn]], 1
-    )
-    summed_patch = summed_early[edge : edge + rows_patch]
-    summed_gain = summed_early[edge + rows_patch, : 3 * cols_gain].reshape(3, cols_gain)
-    gradient_list = (grad_table, summed_patch, summed_attn, summed_up, summed_down, summed_gain)
-    squares = sum((jnp.sum(gradient * gradient) for gradient in gradient_list))
-    totals = sum_everywhere(
-        jnp.stack(
-            [
-                squares,
-                loss_part,
-                square_sum(embedded),
-                square_sum(branch),
-                square_sum(second),
-                square_sum(result),
-            ]
-        )
-    )
-    clip_norm = jnp.sqrt(totals[0])
-    loss_total = totals[1]
-    factor = jnp.minimum(1.0, CLIP_LIMIT / clip_norm)
-    states = (
-        (table, table_mom, table_avg),
-        (patch_w, patch_mom, patch_avg),
-        (attn_w, attn_mom, attn_avg),
-        (up_w, up_mom, up_avg),
-        (down_w, down_mom, down_avg),
-        (gains, gain_mom, gain_avg),
-    )
-    renewed = [
-        renew(state[0], state[1], state[2], gradient, factor)
-        for state, gradient in zip(states, gradient_list)
-    ]
+    edge = 3 * rows_attn + rows_patch
+    summed_gain = lax.dynamic_slice_in_dim(
+        summed_early[edge : edge + 3], place * cols_gain, cols_gain, 1
+    )
+    squares = (
+        jnp.sum(grad_table * grad_table)
+        + jnp.sum(summed_early[:edge] * summed_early[:edge])
+        + jnp.sum(summed_gain * summed_gain)
+    )
+    row = jnp.zeros((1, LANES), f32)
+    lane = lax.broadcasted_iota(jnp.int32, (1, LANES), 1)
+    scalars = (
+        squares, loss_part, square_sum(embedded), square_sum(branch), square_sum(second),
+        square_sum(result),
+    )
+    for at, value in enumerate(scalars):
+        row = jnp.where(lane == at, value, row)
+    summed_late, spread = finish_sum(late_terms, row, world)
+    spread = lax.all_to_all(spread, AXES, 0, 0, tiled=True)
+    *matrices, totals = renew_matrices(
+        spread, summed_early, summed_late,
+        (
+            (patch_w, patch_mom, patch_avg),
+            (attn_w, attn_mom, attn_avg),
+            (up_w, up_mom, up_avg),
+            (down_w, down_mom, down_avg),
+        ),
+    )
+    factor = clip_factor(jnp.sum(spread, 0, keepdims=True))[0, 0]
+    table_new = renew(table, table_mom, table_avg, grad_table, factor)
+    gains_new = renew(gains, gain_mom, gain_avg, summed_gain, factor)
+    clip_norm = jnp.sqrt(totals[0, 0])
+    loss_total = totals[0, 1]
     valid_total = jnp.sum(counts[:, :2].astype(f32))
-    rms_stats = jnp.sqrt(totals[2:6] / valid_total)
-    outputs = []
-    for state in renewed[:-1]:
-        outputs.extend([state[0], state[1], state[2], state[0].astype(bf16)])
-    outputs.extend(renewed[-1])
-    return (*outputs, loss_total, present, clip_norm, rms_stats)
+    rms_stats = jnp.sqrt(totals[0, 2:6] / valid_total)
+    return (
+        *table_new, table_new[0].astype(bf16), *matrices, *gains_new,
+        loss_total, present, clip_norm, rms_stats,
+    )
 
 
 def solution(mesh):

time: 767 us -> 652 us (0.85)
  waiting for transfers between devices: 188 us -> 137 us
  Pallas kernels: 167 us -> 200 us
  local copies, waits for them, and re-layouts: 78.5 us -> 46.9 us
  between operations: 48.8 us -> 24.9 us
  other arithmetic: 108 us -> 84.5 us
  starting transfers between devices: 48.7 us -> 37.2 us
  matrix products: 74.5 us -> 66.8 us
    ppermute x30, waiting for transfers between devices: 117 us -> 54.2 us  [permute(): lax.ppermute(value, axis, [(i, target(i)) for i in range(lax.axis_size(ax...]
    pallas_call x1 -> x7, Pallas kernels: 32.8 us -> 63.1 us  [the longest x2 38.3 us: head_grad(): pl.pallas_call(head_grad_kernel, grid=(part,), in_specs=[whole, pl.BlockS...]
    all_to_all x1, waiting for transfers between devices: 0.01 us -> 24.1 us  [far_send(): lax.all_to_all(packed.reshape(world, share, D), ('mp', 'dp'), split_axis=...]
    all_to_all x1, waiting for transfers between devices: 64.9 us -> 42.3 us  [far_fetch(): lax.all_to_all(rows.reshape(world, share, D), ('mp', 'dp'), split_axis=0,...]
    ppermute x30, starting transfers between devices: 38.2 us -> 27.3 us  [permute(): lax.ppermute(value, axis, [(i, target(i)) for i in range(lax.axis_size(ax...]
    add x3 -> x0, local copies, waits for them, and re-layouts: 10.6 us -> none  [the longest x1 3.7 us: shards(): grad_embedded = grad_embedded + back_in_place(grad_middle, pick)]
    all_gather x2, waiting for transfers between devices: 0.04 us -> 9.85 us  [shards(): lax.all_gather(jnp.pad(w, ((0, -w.shape[0] % 8), (0, 0))), AXES, axis=0,...]
    convert_element_type x6 -> x3, other arithmetic: 15.4 us -> 5.66 us  [hop(): (self.upward.astype(f32) + self.part(self.up_steps - step)).astype(bf16)]
  transfers between devices with their start and end apart: 36 -> 36, of which waited for: 17 -> 10; matrix products, arithmetic and copies ran while one was open for 26% -> 26% of each run, Pallas kernels for 15% -> 26%
where the time goes in v2:
time: 652 us; the launch traced here: 642 us
  Pallas kernels  200 us (31%)
  waiting for transfers between devices  137 us (21%)
  other arithmetic  84.5 us (13%)
  matrix products  66.8 us (10%)
  local copies, waits for them, and re-layouts  46.9 us (7%)
  blocking collectives  44 us (7%)
  starting transfers between devices  37.2 us (6%)
  between operations  24.9 us (4%)
    ppermute x30, waiting for transfers between devices, permute(): lax.ppermute(value, axis, [(i, target(i)) for i in range(lax.axis_size(ax...  54.2 us
    pallas_call x2, Pallas kernels, head_scan(): pl.pallas_call(lambda *refs: head_scan_kernel(*refs, carried=bool(carry),...  48.3 us
    all_to_all x1, blocking collectives, far_ids(): lax.all_to_all(ids, ('mp', 'dp'), split_axis=0, concat_axis=0, tiled=True)  44 us
    all_to_all x1, waiting for transfers between devices, far_fetch(): lax.all_to_all(rows.reshape(world, share, D), ('mp', 'dp'), split_axis=0,...  42.3 us
    pallas_call x2, Pallas kernels, head_grad(): pl.pallas_call(head_grad_kernel, grid=(part,), in_specs=[whole, pl.BlockS...  38.3 us
    pallas_call x1, Pallas kernels, attention_all(): pl.pallas_call(lambda *refs: attention_all_kernel(*refs, block=512), grid...  30.3 us
    ppermute x30, starting transfers between devices, permute(): lax.ppermute(value, axis, [(i, target(i)) for i in range(lax.axis_size(ax...  27.3 us
    all_to_all x1, waiting for transfers between devices, far_send(): lax.all_to_all(packed.reshape(world, share, D), ('mp', 'dp'), split_axis=...  24.1 us
  transfers between devices with their start and end apart: 36, of which 10 were waited for; matrix products, arithmetic and copies ran while one was open for 26% of the time, Pallas kernels for 26%

profile of v2, /device:TPU:0, one launch (start us, length us, event | category | flops | bytes accessed | tf_op | source)
XLA Modules:
  0.0 641.7 jit_solution(2346933781084521628)
XLA Ops:
  15.0 3.0 collective-permute-start.1
  27.0 44.0 %all_to_all.75 = s32[32,1,49]{2,1,0:T(1,128)S(1)} all-to-all(s32[32,1,49]{2,1,0:T(1,128)S(1)} %bitcast.283), channel_id=1, replica_groups=mesh['dp'=8,'mp'=4] {'mp','dp'}, dimensions={0} | all-to-all | bytes 12544 | tf_op jit(solution)/shard_map/all_to_all | solution.py:805
  71.1 6.2 fusion.38
  77.4 3.5 all-to-all-start.5
  89.0 9.9 %all-gather.8.cloned.1.call-done = bf16[1024,3072]{1,0:T(8,128)(2,1)} async-done(((bf16[32,3072]{1,0:T(8,128)(2,1)}), bf16[1024,3072]{1,0:T(8,128)(2,1)}) %all-gather.8.cloned.1.call-update) | async-done | bytes 6291472 | tf_op jit(solution)/shard_map/all_gather | solution.py:769
  101.2 3.3 slice.175
  108.0 3.2 fusion.120
  111.2 42.3 %all-to-all-done.5 = bf16[32,48,768]{2,1,0:T(8,128)(2,1)} async-done(((bf16[32,48,768]{2,1,0:T(8,128)(2,1)}), bf16[32,48,768]{2,1,0:T(8,128)(2,1)}, u32[]{:S(2)}, u32[]{:S(2)}) %all-to-all-start.5) | async-done | bytes 2359328 | tf_op jit(solution)/shard_map/all_to_all | solution.py:816
  155.6 4.5 fusion.31
  160.4 3.8 fusion.127
  169.2 3.9 convolution_convert_fusion.k_ref.v_ref.refs_1_.refs_2_
  173.1 15.8 %attention_pick.1 = (bf16[256,768]{1,0:T(8,128)(2,1)}, f32[6,8,256]{2,1,0:T(8,128)}) custom-call(s32[1]{0:T(128)} %bitcast.11.first_ref, bf16[256,768]{1,0:T(8,128)(2,1)} %convolution_convert_fusion.3.q_ref, bf16[1024,1536]{1,0:T(8,128)(2,1)} %convolution_convert_fusion.k_ref.v_ref.refs_1_.refs_2_, ...), custom_call_target="tpu_custom_call" | custom-call | flops 3221225472 | bytes 4718592 | tf_op jit(solution)/shard_map/attention_pick/pallas_call | solution.py:140
  189.0 4.1 convolution_convert_fusion.1.refs_0_
  194.1 30.3 %attention_all.1 = bf16[1024,768]{1,0:T(8,128)(2,1)} custom-call(bf16[1024,768]{1,0:T(8,128)(2,1)} %convolution_convert_fusion.1.refs_0_, bf16[1024,1536]{1,0:T(8,128)(2,1)} %convolution_convert_fusion.k_ref.v_ref.refs_1_.refs_2_, bf16[1024,1536]{1,0:T(8,128)(2,1)} %convolution_convert_fusion.k_ref.v_ref.refs_1_.refs_2_), custom_call_target="tpu_custom_call" | custom-call | flops 12884901888 | bytes 6291456 | tf_op jit(solution)/shard_map/attention_all/pallas_call | solution.py:98
  226.5 2.8 slice.186
  233.7 3.7 multiply_convert_fusion.1
  244.7 8.9 %collective-permute-done.2 = bf16[256,768]{1,0:T(8,128)(2,1)S(1)} collective-permute-done((bf16[256,768]{1,0:T(8,128)(2,1)S(1)}, bf16[256,768]{1,0:T(8,128)(2,1)S(1)}, u32[]{:S(2)}, u32[]{:S(2)}) %collective-permute-start.2) | collective-permute-done | bytes 393248 | tf_op jit(solution)/shard_map/ppermute | solution.py:446
  253.8 9.2 %collective-permute-done.7.refs_4_ = bf16[1032,768]{1,0:T(8,128)(2,1)} collective-permute-done((bf16[1032,768]{1,0:T(8,128)(2,1)}, bf16[1032,768]{1,0:T(8,128)(2,1)}, u32[]{:S(2)}, u32[]{:S(2)}) %collective-permute-start.7) | collective-permute-done | bytes 1585184 | tf_op jit(solution)/shard_map/ppermute | solution.py:446
  268.8 26.7 %head_scan.2 = (f32[1024,768]{1,0:T(8,128)}, f32[1024,1]{1,0:T(8,128)}) custom-call(bf16[1024,768]{1,0:T(8,128)(2,1)} %bitcast.274, bf16[1032,768]{1,0:T(8,128)(2,1)} %convert_element_type.407.refs_1_.table_ref, bf16[1032,768]{1,0:T(8,128)(2,1)} %collective-permute-done.refs_2_, bf16[1032,768]{1,0:T(8,128)(2,1)} %collective-permute-done.1.refs_3_, ...), custom_call_target="tpu_custom_call" | custom-call | flops 16231956480 | bytes 11071488 | tf_op jit(solution)/shard_map/head_scan/pallas_call | solution.py:387
  296.7 21.5 %head_scan.3 = (bf16[512,896]{1,0:T(8,128)(2,1)}, bf16[512,896]{1,0:T(8,128)(2,1)}) custom-call(bf16[1024,768]{1,0:T(8,128)(2,1)} %bitcast.275, f32[1024,768]{1,0:T(8,128)} %get-tuple-element.206.refs_1_, f32[1024,1]{1,0:T(8,128)} %get-tuple-element.207.refs_2_, bf16[1032,768]{1,0:T(8,128)(2,1)} %collective-permute-done.6.refs_3_, ...), custom_call_target="tpu_custom_call" | custom-call | flops 9739173888 | bytes 7901184 | tf_op jit(solution)/shard_map/head_scan/pallas_call | solution.py:387
  318.4 2.7 collective-permute-done.10.refs_1_
  322.0 3.2 merge.2
  327.2 12.6 %collective-permute-done.11.refs_1_ = bf16[256,896]{1,0:T(8,128)(2,1)S(1)} collective-permute-done((bf16[256,896]{1,0:T(8,128)(2,1)S(1)}, bf16[256,896]{1,0:T(8,128)(2,1)S(1)}, u32[]{:S(2)}, u32[]{:S(2)}) %collective-permute-start.11) | collective-permute-done | bytes 458784 | tf_op jit(solution)/shard_map/ppermute | solution.py:446
  351.9 5.4 fusion.45.refs_2_
  362.8 21.4 %attention_back.1 = (bf16[256,768]{1,0:T(8,128)(2,1)}, bf16[1024,768]{1,0:T(8,128)(2,1)}, bf16[1024,768]{1,0:T(8,128)(2,1)}) custom-call(s32[1]{0:T(128)} %bitcast.11.first_ref, bf16[256,768]{1,0:T(8,128)(2,1)} %convolution_convert_fusion.3.q_ref, bf16[1024,1536]{1,0:T(8,128)(2,1)} %convolution_convert_fusion.k_ref.v_ref.refs_1_.refs_2_, ...), custom_call_target="tpu_custom_call" | custom-call | flops 8053063680 | bytes 7864320 | tf_op jit(solution)/shard_map/attention_back/pallas_call | solution.py:209
  384.2 12.8 %first_back.1 = (bf16[1024,768]{1,0:T(8,128)(2,1)}, bf16[1024,768]{1,0:T(8,128)(2,1)S(1)}, f32[1,768]{1,0:T(1,128)}) custom-call(s32[1]{0:T(128)} %bitcast.27.bounds_ref, bf16[1024,768]{1,0:T(8,128)(2,1)} %get-tuple-element.214.k_ref.refs_4_, bf16[1024,768]{1,0:T(8,128)(2,1)} %get-tuple-element.215.v_ref.refs_6_, bf16[768,1536]{1,0:T(8,128)(2,1)} %bitcast.250, ...), custom_call_target="tpu_custom_call" | custom-call | flops 2415919104 | bytes 12582912 | tf_op jit(solution)/shard_map/first_back/pallas_call | solution.py:280
  397.1 4.8 select_convert_fusion
  403.9 11.4 %grad_pack.2 = (bf16[16,112,768]{2,1,0:T(8,128)(2,1)}, bf16[16,112,768]{2,1,0:T(8,128)(2,1)}) custom-call(s32[1]{0:T(128)} %bitcast.24.refs_0_, bf16[256,768]{1,0:T(8,128)(2,1)} %copy-done.27, bf16[256,768]{1,0:T(8,128)(2,1)} %get-tuple-element.213.q_ref.refs_2_, bf16[1024,768]{1,0:T(8,128)(2,1)} %copy-done.24, ...), custom_call_target="tpu_custom_call" | custom-call | flops 4127195136 | bytes 5505024 | tf_op jit(solution)/shard_map/grad_pack/pallas_call | solution.py:548
  415.3 9.6 %grad_pack.3 = (bf16[16,224,768]{2,1,0:T(8,128)(2,1)}, bf16[16,224,768]{2,1,0:T(8,128)(2,1)}) custom-call(s32[1]{0:T(128)} %bitcast.24.refs_0_, bf16[256,768]{1,0:T(8,128)(2,1)} %copy-done.41, bf16[256,3072]{1,0:T(8,128)(2,1)} %copy-done.84, bf16[256,3072]{1,0:T(8,128)(2,1)} %copy-done.83, bf16[256,768]{1,0:T(8,128)(2,1)} %copy-done.42, ...), custom_call_target="tpu_custom_call" | custom-call | flops 2717908992 | bytes 11010048 | tf_op jit(solution)/shard_map/grad_pack/pallas_call | solution.py:548
  425.4 3.5 all-to-all-start.6
  429.8 11.2 %collective-permute-done.17 = bf16[16,112,768]{2,1,0:T(8,128)(2,1)} collective-permute-done((bf16[16,112,768]{2,1,0:T(8,128)(2,1)}, bf16[16,112,768]{2,1,0:T(8,128)(2,1)}, u32[]{:S(2)}, u32[]{:S(2)}) %collective-permute-start.17) | collective-permute-done | bytes 2752544 | tf_op jit(solution)/shard_map/ppermute | solution.py:446
  441.0 4.9 add_convert_fusion.1
  446.4 3.1 fusion.62
  451.8 3.1 multiply_reduce_fusion.2
  454.9 4.1 copy.101
  463.5 24.1 %all-to-all-done.6 = bf16[32,48,768]{2,1,0:T(8,128)(2,1)} async-done(((bf16[32,48,768]{2,1,0:T(8,128)(2,1)}), bf16[32,48,768]{2,1,0:T(8,128)(2,1)}, u32[]{:S(2)}, u32[]{:S(2)}) %all-to-all-start.6) | async-done | bytes 2359328 | tf_op jit(solution)/shard_map/all_to_all | solution.py:831
  487.5 15.7 %multiply_reduce_fusion.3 = (f32[1024]{0:T(1024)S(1)}, f32[1024,768]{0,1:T(8,128)}) fusion(bf16[3072,768]{1,0:T(8,128)(2,1)} %bitcast.269, bf16[1024,768]{1,0:T(8,128)(2,1)S(1)} %multiply_convert_fusion, bf16[768,3072]{1,0:T(8,128)(2,1)} %bitcast.263), kind=kOutput, calls=%fused_computation.78 | convolution fusion | flops 9693559808 | bytes 14159872 | tf_op jit(solution)/shard_map/dot_general | solution.py:982
  505.0 3.8 copy.103
  521.5 18.5 %head_grad.2.refs_0_ = f32[1032,768]{1,0:T(8,128)} custom-call(bf16[1032,768]{1,0:T(8,128)(2,1)} %convert_element_type.407.refs_1_.table_ref, bf16[8192,768]{1,0:T(8,128)(2,1)} %all-gather.6.cloned.1.call-done.rows_ref, f32[4,1,2048]{2,1,0:T(1,128)} %reshape.629.lse_ref, f32[4,1,2048]{2,1,0:T(1,128)} %fusion.93.weight_ref), custom_call_target="tpu_custom_call" | custom-call | flops 12985565184 | bytes 11046912 | tf_op jit(solution)/shard_map/head_grad/pallas_call | solution.py:429
  548.0 19.8 %head_grad.3 = f32[1032,768]{1,0:T(8,128)} custom-call(bf16[1032,768]{1,0:T(8,128)(2,1)} %convert_element_type.407.refs_1_.table_ref, bf16[8192,768]{1,0:T(8,128)(2,1)} %all-gather.6.cloned.1.call-done.rows_ref, f32[4,1,2048]{2,1,0:T(1,128)} %reshape.629.lse_ref, f32[4,1,2048]{2,1,0:T(1,128)} %fusion.93.weight_ref, f32[1032,768]{1,0:T(8,128)} %head_grad.2.refs_0_), custom_call_target="tpu_custom_call" | custom-call | flops 12985565184 | bytes 11046912 | tf_op jit(solution)/shard_map/head_grad/pallas_call | solution.py:429
  567.8 2.7 fusion.53
  573.5 4.9 fusion.35
  583.5 9.6 %collective-permute-done.28 = bf16[2,224,768]{2,1,0:T(8,128)(2,1)} collective-permute-done((bf16[2,224,768]{2,1,0:T(8,128)(2,1)}, bf16[2,224,768]{2,1,0:T(8,128)(2,1)}, u32[]{:S(2)}, u32[]{:S(2)}) %collective-permute-start.28) | collective-permute-done | bytes 688160 | tf_op jit(solution)/shard_map/ppermute | solution.py:446
  601.1 3.8 compare_select_fusion.7.row_ref
  607.0 2.7 all-to-all-start.7
  610.3 6.5 %all-to-all-done.7 = f32[32,1,128]{2,1,0:T(1,128)S(1)} async-done(((f32[32,1,128]{2,1,0:T(1,128)}), f32[32,1,128]{2,1,0:T(1,128)S(1)}, u32[]{:S(2)}, u32[]{:S(2)}) %all-to-all-start.7) | async-done | bytes 16416 | tf_op jit(solution)/shard_map/all_to_all | solution.py:1037
  617.4 4.3 renew_matrices.1
  625.6 5.1 fusion.112
  (383 shorter events, 130.7 us)
Async XLA Ops:
  7.2 91.6 %all-gather.8.cloned.1.call-start = ((), (), s32[]{:S(2)}) async-start(), calls=%async_computation.9 | async-start | bytes 6488064 | tf_op jit(solution)/shard_map/all_gather | solution.py:769
  10.8 215.7 %all-gather.10.cloned.1.call-start = ((), (), s32[]{:S(2)}) async-start(), calls=%async_computation.10 | async-start | bytes 9732096 | tf_op jit(solution)/shard_map/all_gather | solution.py:769
  15.0 62.3 %collective-permute-start.1 = (bf16[1032,768]{1,0:T(8,128)(2,1)}, bf16[1032,768]{1,0:T(8,128)(2,1)}, u32[]{:S(2)}, u32[]{:S(2)}) collective-permute-start(bf16[1032,768]{1,0:T(8,128)(2,1)} %convert_element_type.407.refs_1_.table_ref), channel_id=1, source_target_pairs={{0,4},{4,12},{8,0},{12,20},{16,8},{20,28},{24,16},{28,24},{1,5},{5... | collective-permute-start | bytes 4755464 | tf_op jit(solution)/shard_map/ppermute | solution.py:446
  18.0 59.4 %collective-permute-start = (bf16[1032,768]{1,0:T(8,128)(2,1)}, bf16[1032,768]{1,0:T(8,128)(2,1)}, u32[]{:S(2)}, u32[]{:S(2)}) collective-permute-start(bf16[1032,768]{1,0:T(8,128)(2,1)} %convert_element_type.407.refs_1_.table_ref), channel_id=1, source_target_pairs={{0,8},{4,0},{8,16},{12,4},{16,24},{20,12},{24,28},{28,20},{1,9},{5... | collective-permute-start | bytes 4755464 | tf_op jit(solution)/shard_map/ppermute | solution.py:446
  24.6 131.0 %copy-start.66 = (s32[1024]{0:T(1024)}, s32[1024]{0:T(1024)S(1)}, u32[]{:S(2)}) copy-start(s32[1024]{0:T(1024)S(1)} %get-tuple-element.417) | copy-start | bytes 12292
  77.4 76.2 %all-to-all-start.5 = ((bf16[32,48,768]{2,1,0:T(8,128)(2,1)}), bf16[32,48,768]{2,1,0:T(8,128)(2,1)}, u32[]{:S(2)}, u32[]{:S(2)}) async-start(bf16[32,48,768]{2,1,0:T(8,128)(2,1)} %bitcast.6), calls=%async_computation.5 | async-start | bytes 4718592 | tf_op jit(solution)/shard_map/all_to_all | solution.py:816
  80.9 440.6 %all-gather.6.cloned.1.call-start = ((), (), s32[]{:S(2)}) async-start(), calls=%async_computation.8 | async-start | bytes 12976128 | tf_op jit(solution)/shard_map/all_gather | solution.py:933
  86.2 74.1 %copy-start.28 = (bf16[1024,128]{1,0:T(8,128)(2,1)}, bf16[1024,128]{1,0:T(8,128)(2,1)S(1)}, u32[]{:S(2)}) copy-start(bf16[1024,128]{1,0:T(8,128)(2,1)S(1)} %fusion.63) | copy-start | bytes 786436
  153.6 70.9 %collective-permute-start.4 = (bf16[1032,768]{1,0:T(8,128)(2,1)}, bf16[1032,768]{1,0:T(8,128)(2,1)}, u32[]{:S(2)}, u32[]{:S(2)}) collective-permute-start(bf16[1032,768]{1,0:T(8,128)(2,1)} %collective-permute-done.refs_2_), channel_id=1, source_target_pairs={{0,8},{4,0},{8,16},{12,4},{16,24},{20,12},{24,28},{28,20},{1,9},{5... | collective-permute-start | bytes 4755464 | tf_op jit(solution)/shard_map/ppermute | solution.py:446
  153.6 70.9 %collective-permute-start.5 = (bf16[1032,768]{1,0:T(8,128)(2,1)}, bf16[1032,768]{1,0:T(8,128)(2,1)}, u32[]{:S(2)}, u32[]{:S(2)}) collective-permute-start(bf16[1032,768]{1,0:T(8,128)(2,1)} %collective-permute-done.1.refs_3_), channel_id=1, source_target_pairs={{0,4},{4,12},{8,0},{12,20},{16,8},{20,28},{24,16},{28,24},{1,5},{5... | collective-permute-start | bytes 4755464 | tf_op jit(solution)/shard_map/ppermute | solution.py:446
  164.3 28.8 %copy-start = (f32[1024,768]{1,0:T(8,128)}, f32[1024,768]{1,0:T(8,128)S(1)}, u32[]{:S(2)}) copy-start(f32[1024,768]{1,0:T(8,128)S(1)} %get-tuple-element.433.x_ref) | copy-start | bytes 9437188
  193.6 30.8 %copy-start.7 = (f32[256,768]{1,0:T(8,128)}, f32[256,768]{1,0:T(8,128)S(1)}, u32[]{:S(2)}) copy-start(f32[256,768]{1,0:T(8,128)S(1)} %get-tuple-element.381) | copy-start | bytes 2359300
  193.6 30.7 %copy-start.50 = (f32[256]{0:T(256)}, f32[256]{0:T(256)S(1)}, u32[]{:S(2)}) copy-start(f32[256]{0:T(256)S(1)} %broadcast_multiply_fusion.4) | copy-start | bytes 3076
  193.9 30.5 %copy-start.57 = (f32[256]{0:T(256)}, f32[256]{0:T(256)S(1)}, u32[]{:S(2)}) copy-start(f32[256]{0:T(256)S(1)} %multiply_reduce_fusion.12) | copy-start | bytes 3076
  193.9 30.5 %copy-start.55 = (f32[256]{0:T(256)}, f32[256]{0:T(256)S(1)}, u32[]{:S(2)}) copy-start(f32[256]{0:T(256)S(1)} %fusion.103) | copy-start | bytes 3076
  194.1 37.8 %copy-start.41 = (bf16[256,768]{1,0:T(8,128)(2,1)}, bf16[256,768]{1,0:T(8,128)(2,1)S(1)}, u32[]{:S(2)}) copy-start(bf16[256,768]{1,0:T(8,128)(2,1)S(1)} %multiply_convert_fusion.4.refs_1_) | copy-start | bytes 1179652
  224.4 38.5 %collective-permute-start.6 = (bf16[1032,768]{1,0:T(8,128)(2,1)}, bf16[1032,768]{1,0:T(8,128)(2,1)}, u32[]{:S(2)}, u32[]{:S(2)}) collective-permute-start(bf16[1032,768]{1,0:T(8,128)(2,1)} %collective-permute-done.4.refs_4_), channel_id=1, source_target_pairs={{0,8},{4,0},{8,16},{12,4},{16,24},{20,12},{24,28},{28,20},{1,9},{5... | collective-permute-start | bytes 4755464 | tf_op jit(solution)/shard_map/ppermute | solution.py:446
  224.5 38.5 %collective-permute-start.7 = (bf16[1032,768]{1,0:T(8,128)(2,1)}, bf16[1032,768]{1,0:T(8,128)(2,1)}, u32[]{:S(2)}, u32[]{:S(2)}) collective-permute-start(bf16[1032,768]{1,0:T(8,128)(2,1)} %collective-permute-done.5.refs_5_), channel_id=1, source_target_pairs={{0,4},{4,12},{8,0},{12,20},{16,8},{20,28},{24,16},{28,24},{1,5},{5... | collective-permute-start | bytes 4755464 | tf_op jit(solution)/shard_map/ppermute | solution.py:446
  242.4 11.2 %collective-permute-start.2 = (bf16[256,768]{1,0:T(8,128)(2,1)S(1)}, bf16[256,768]{1,0:T(8,128)(2,1)S(1)}, u32[]{:S(2)}, u32[]{:S(2)}) collective-permute-start(bf16[256,768]{1,0:T(8,128)(2,1)S(1)} %get-tuple-element.211), channel_id=1, source_target_pairs={{0,2},{1,3},{2,0},{3,1},{4,6},{5,7},{6,4},{7,5},{8,10},{9,11},{10,... | collective-permute-start | bytes 1179656 | tf_op jit(solution)/shard_map/ppermute | solution.py:446
  253.7 13.8 %collective-permute-start.3 = (bf16[2,256,768]{2,1,0:T(8,128)(2,1)S(1)}, bf16[2,256,768]{2,1,0:T(8,128)(2,1)S(1)}, u32[]{:S(2)}, u32[]{:S(2)}) collective-permute-start(bf16[2,256,768]{2,1,0:T(8,128)(2,1)S(1)} %get-tuple-element.407), channel_id=1, source_target_pairs={{0,1},{1,0},{2,3},{3,2},{4,5},{5,4},{6,7},{7,6},{8,9},{9,8},{10,11... | collective-permute-start | bytes 2359304 | tf_op jit(solution)/shard_map/ppermute | solution.py:446
  264.2 31.4 %collective-permute-start.8 = (bf16[512,768]{1,0:T(8,128)(2,1)S(1)}, bf16[512,768]{1,0:T(8,128)(2,1)S(1)}, u32[]{:S(2)}, u32[]{:S(2)}) collective-permute-start(bf16[512,768]{1,0:T(8,128)(2,1)S(1)} %slice.153), channel_id=1, source_target_pairs={{0,8},{4,0},{8,16},{12,4},{16,24},{20,12},{24,28},{28,20},{1,9},{5... | collective-permute-start | bytes 2359304 | tf_op jit(solution)/shard_map/ppermute | solution.py:446
  267.2 28.4 %collective-permute-start.9 = (bf16[520,768]{1,0:T(8,128)(2,1)S(1)}, bf16[520,768]{1,0:T(8,128)(2,1)S(1)}, u32[]{:S(2)}, u32[]{:S(2)}) collective-permute-start(bf16[520,768]{1,0:T(8,128)(2,1)S(1)} %slice.154), channel_id=1, source_target_pairs={{0,4},{4,12},{8,0},{12,20},{16,8},{20,28},{24,16},{28,24},{1,5},{5... | collective-permute-start | bytes 2396168 | tf_op jit(solution)/shard_map/ppermute | solution.py:446
  318.3 29.5 %copy-start.65 = (f32[256]{0:T(256)S(1)}, f32[256]{0:T(256)}, u32[]{:S(2)}) copy-start(f32[256]{0:T(256)} %get-tuple-element.367) | copy-start | bytes 3076
  318.3 30.8 %copy-start.45 = (f32[768]{0:T(1024)S(1)}, f32[768]{0:T(1024)}, u32[]{:S(2)}) copy-start(f32[768]{0:T(1024)} %mul.502) | copy-start | bytes 9220
  318.3 30.8 %copy-start.49 = (f32[256]{0:T(256)S(1)}, f32[256]{0:T(256)}, u32[]{:S(2)}) copy-start(f32[256]{0:T(256)} %copy-done.48) | copy-start | bytes 3076
  318.3 30.8 %copy-start.53 = (f32[256]{0:T(256)S(1)}, f32[256]{0:T(256)}, u32[]{:S(2)}) copy-start(f32[256]{0:T(256)} %copy-done.52) | copy-start | bytes 3076
  318.3 2.7 collective-permute-start.10
  327.2 12.6 %collective-permute-start.11 = (bf16[256,896]{1,0:T(8,128)(2,1)S(1)}, bf16[256,896]{1,0:T(8,128)(2,1)S(1)}, u32[]{:S(2)}, u32[]{:S(2)}) collective-permute-start(bf16[256,896]{1,0:T(8,128)(2,1)S(1)} %get-tuple-element.404), channel_id=1, source_target_pairs={{0,2},{1,3},{2,0},{3,1},{4,6},{5,7},{6,4},{7,5},{8,10},{9,11},{10,... | collective-permute-start | bytes 1376264 | tf_op jit(solution)/shard_map/ppermute | solution.py:446
  424.9 21.4 %collective-permute-start.12 = (bf16[16,224,768]{2,1,0:T(8,128)(2,1)}, bf16[16,224,768]{2,1,0:T(8,128)(2,1)}, u32[]{:S(2)}, u32[]{:S(2)}) collective-permute-start(bf16[16,224,768]{2,1,0:T(8,128)(2,1)} %get-tuple-element.225), channel_id=1, source_target_pairs={{0,1},{1,0},{2,3},{3,2},{4,5},{5,4},{6,7},{7,6},{8,9},{9,8},{10,11... | collective-permute-start | bytes 16515080 | tf_op jit(solution)/shard_map/ppermute | solution.py:446
  424.9 16.1 %collective-permute-start.17 = (bf16[16,112,768]{2,1,0:T(8,128)(2,1)}, bf16[16,112,768]{2,1,0:T(8,128)(2,1)}, u32[]{:S(2)}, u32[]{:S(2)}) collective-permute-start(bf16[16,112,768]{2,1,0:T(8,128)(2,1)} %get-tuple-element.222), channel_id=1, source_target_pairs={{0,1},{1,0},{2,3},{3,2},{4,5},{5,4},{6,7},{7,6},{8,9},{9,8},{10,11... | collective-permute-start | bytes 8257544 | tf_op jit(solution)/shard_map/ppermute | solution.py:446
  425.4 62.1 %all-to-all-start.6 = ((bf16[32,48,768]{2,1,0:T(8,128)(2,1)}), bf16[32,48,768]{2,1,0:T(8,128)(2,1)}, u32[]{:S(2)}, u32[]{:S(2)}) async-start(bf16[32,48,768]{2,1,0:T(8,128)(2,1)} %bitcast.32), calls=%async_computation.6 | async-start | bytes 4718592 | tf_op jit(solution)/shard_map/all_to_all | solution.py:831
  445.9 69.7 %collective-permute-start.18 = (bf16[8,112,768]{2,1,0:T(8,128)(2,1)}, bf16[8,112,768]{2,1,0:T(8,128)(2,1)}, u32[]{:S(2)}, u32[]{:S(2)}) collective-permute-start(bf16[8,112,768]{2,1,0:T(8,128)(2,1)} %get-tuple-element.397), channel_id=1, source_target_pairs={{0,2},{1,3},{2,0},{3,1},{4,6},{5,7},{6,4},{7,5},{8,10},{9,11},{10,... | collective-permute-start | bytes 4128776 | tf_op jit(solution)/shard_map/ppermute | solution.py:446
  449.5 63.4 %collective-permute-start.13 = (bf16[2,224,768]{2,1,0:T(8,128)(2,1)}, bf16[2,224,768]{2,1,0:T(8,128)(2,1)}, u32[]{:S(2)}, u32[]{:S(2)}) collective-permute-start(bf16[2,224,768]{2,1,0:T(8,128)(2,1)} %get-tuple-element.389), channel_id=1, source_target_pairs={{0,8},{4,0},{8,16},{12,4},{16,24},{20,12},{24,28},{28,20},{1,9},{5... | collective-permute-start | bytes 2064392 | tf_op jit(solution)/shard_map/ppermute | solution.py:446
  451.8 61.1 %collective-permute-start.14 = (bf16[2,224,768]{2,1,0:T(8,128)(2,1)}, bf16[2,224,768]{2,1,0:T(8,128)(2,1)}, u32[]{:S(2)}, u32[]{:S(2)}) collective-permute-start(bf16[2,224,768]{2,1,0:T(8,128)(2,1)} %get-tuple-element.388), channel_id=1, source_target_pairs={{0,4},{4,12},{8,0},{12,20},{16,8},{20,28},{24,16},{28,24},{1,5},{5... | collective-permute-start | bytes 2064392 | tf_op jit(solution)/shard_map/ppermute | solution.py:446
  515.6 24.5 %collective-permute-start.15 = (bf16[2,224,768]{2,1,0:T(8,128)(2,1)S(1)}, bf16[2,224,768]{2,1,0:T(8,128)(2,1)S(1)}, u32[]{:S(2)}, u32[]{:S(2)}) collective-permute-start(bf16[2,224,768]{2,1,0:T(8,128)(2,1)S(1)} %get-tuple-element.387), channel_id=1, source_target_pairs={{0,8},{4,0},{8,16},{12,4},{16,24},{20,12},{24,28},{28,20},{1,9},{5... | collective-permute-start | bytes 2064392 | tf_op jit(solution)/shard_map/ppermute | solution.py:446
  517.5 25.1 %collective-permute-start.20 = (bf16[112,768]{1,0:T(8,128)(2,1)}, bf16[112,768]{1,0:T(8,128)(2,1)}, u32[]{:S(2)}, u32[]{:S(2)}) collective-permute-start(bf16[112,768]{1,0:T(8,128)(2,1)} %get-tuple-element.402), channel_id=1, source_target_pairs={{0,4},{4,12},{8,0},{12,20},{16,8},{20,28},{24,16},{28,24},{1,5},{5... | collective-permute-start | bytes 516104 | tf_op jit(solution)/shard_map/ppermute | solution.py:446
  519.5 23.1 %collective-permute-start.19 = (bf16[112,768]{1,0:T(8,128)(2,1)}, bf16[112,768]{1,0:T(8,128)(2,1)}, u32[]{:S(2)}, u32[]{:S(2)}) collective-permute-start(bf16[112,768]{1,0:T(8,128)(2,1)} %get-tuple-element.403), channel_id=1, source_target_pairs={{0,8},{4,0},{8,16},{12,4},{16,24},{20,12},{24,28},{28,20},{1,9},{5... | collective-permute-start | bytes 516104 | tf_op jit(solution)/shard_map/ppermute | solution.py:446
  519.5 20.5 %collective-permute-start.16 = (bf16[2,224,768]{2,1,0:T(8,128)(2,1)S(1)}, bf16[2,224,768]{2,1,0:T(8,128)(2,1)}, u32[]{:S(2)}, u32[]{:S(2)}) collective-permute-start(bf16[2,224,768]{2,1,0:T(8,128)(2,1)S(1)} %get-tuple-element.386), channel_id=1, source_target_pairs={{0,4},{4,12},{8,0},{12,20},{16,8},{20,28},{24,16},{28,24},{1,5},{5... | collective-permute-start | bytes 2064392 | tf_op jit(solution)/shard_map/ppermute | solution.py:446
  542.5 25.3 %collective-permute-start.21 = (bf16[2,224,768]{2,1,0:T(8,128)(2,1)S(1)}, bf16[2,224,768]{2,1,0:T(8,128)(2,1)S(1)}, u32[]{:S(2)}, u32[]{:S(2)}) collective-permute-start(bf16[2,224,768]{2,1,0:T(8,128)(2,1)S(1)} %get-tuple-element.385), channel_id=1, source_target_pairs={{0,8},{4,0},{8,16},{12,4},{16,24},{20,12},{24,28},{28,20},{1,9},{5... | collective-permute-start | bytes 2064392 | tf_op jit(solution)/shard_map/ppermute | solution.py:446
  543.9 26.6 %collective-permute-start.23 = (bf16[112,768]{1,0:T(8,128)(2,1)S(1)}, bf16[112,768]{1,0:T(8,128)(2,1)S(1)}, u32[]{:S(2)}, u32[]{:S(2)}) collective-permute-start(bf16[112,768]{1,0:T(8,128)(2,1)S(1)} %get-tuple-element.401), channel_id=1, source_target_pairs={{0,8},{4,0},{8,16},{12,4},{16,24},{20,12},{24,28},{28,20},{1,9},{5... | collective-permute-start | bytes 516104 | tf_op jit(solution)/shard_map/ppermute | solution.py:446
  545.2 25.3 %collective-permute-start.24 = (bf16[112,768]{1,0:T(8,128)(2,1)S(1)}, bf16[112,768]{1,0:T(8,128)(2,1)S(1)}, u32[]{:S(2)}, u32[]{:S(2)}) collective-permute-start(bf16[112,768]{1,0:T(8,128)(2,1)S(1)} %get-tuple-element.400), channel_id=1, source_target_pairs={{0,4},{4,12},{8,0},{12,20},{16,8},{20,28},{24,16},{28,24},{1,5},{5... | collective-permute-start | bytes 516104 | tf_op jit(solution)/shard_map/ppermute | solution.py:446
  546.0 21.8 %collective-permute-start.22 = (bf16[2,224,768]{2,1,0:T(8,128)(2,1)S(1)}, bf16[2,224,768]{2,1,0:T(8,128)(2,1)S(1)}, u32[]{:S(2)}, u32[]{:S(2)}) collective-permute-start(bf16[2,224,768]{2,1,0:T(8,128)(2,1)S(1)} %get-tuple-element.384), channel_id=1, source_target_pairs={{0,4},{4,12},{8,0},{12,20},{16,8},{20,28},{24,16},{28,24},{1,5},{5... | collective-permute-start | bytes 2064392 | tf_op jit(solution)/shard_map/ppermute | solution.py:446
  572.2 8.0 %collective-permute-start.25 = (bf16[112,768]{1,0:T(8,128)(2,1)}, bf16[112,768]{1,0:T(8,128)(2,1)S(1)}, u32[]{:S(2)}, u32[]{:S(2)}) collective-permute-start(bf16[112,768]{1,0:T(8,128)(2,1)} %fusion.76), channel_id=1, source_target_pairs={{0,8},{4,0},{8,16},{12,4},{16,24},{20,12},{24,28},{28,20},{1,9},{5... | collective-permute-start | bytes 516104 | tf_op jit(solution)/shard_map/ppermute | solution.py:446
  572.2 20.9 %collective-permute-start.28 = (bf16[2,224,768]{2,1,0:T(8,128)(2,1)}, bf16[2,224,768]{2,1,0:T(8,128)(2,1)}, u32[]{:S(2)}, u32[]{:S(2)}) collective-permute-start(bf16[2,224,768]{2,1,0:T(8,128)(2,1)} %fusion.53), channel_id=1, source_target_pairs={{0,8},{4,0},{8,16},{12,4},{16,24},{20,12},{24,28},{28,20},{1,9},{5... | collective-permute-start | bytes 2064392 | tf_op jit(solution)/shard_map/ppermute | solution.py:446
  581.4 15.2 %collective-permute-start.26 = (bf16[112,768]{1,0:T(8,128)(2,1)S(1)}, bf16[112,768]{1,0:T(8,128)(2,1)S(1)}, u32[]{:S(2)}, u32[]{:S(2)}) collective-permute-start(bf16[112,768]{1,0:T(8,128)(2,1)S(1)} %get-tuple-element.398), channel_id=1, source_target_pairs={{0,8},{4,0},{8,16},{12,4},{16,24},{20,12},{24,28},{28,20},{1,9},{5... | collective-permute-start | bytes 516104 | tf_op jit(solution)/shard_map/ppermute | solution.py:446
  583.0 13.7 %collective-permute-start.27 = (bf16[112,768]{1,0:T(8,128)(2,1)S(1)}, bf16[112,768]{1,0:T(8,128)(2,1)S(1)}, u32[]{:S(2)}, u32[]{:S(2)}) collective-permute-start(bf16[112,768]{1,0:T(8,128)(2,1)S(1)} %get-tuple-element.399), channel_id=1, source_target_pairs={{0,4},{4,12},{8,0},{12,20},{16,8},{20,28},{24,16},{28,24},{1,5},{5... | collective-permute-start | bytes 516104 | tf_op jit(solution)/shard_map/ppermute | solution.py:446
  596.0 8.9 %collective-permute-start.29 = (bf16[224,768]{1,0:T(8,128)(2,1)}, bf16[224,768]{1,0:T(8,128)(2,1)}, u32[]{:S(2)}, u32[]{:S(2)}) collective-permute-start(bf16[224,768]{1,0:T(8,128)(2,1)} %get-tuple-element.408), channel_id=1, source_target_pairs={{0,2},{1,3},{2,0},{3,1},{4,6},{5,7},{6,4},{7,5},{8,10},{9,11},{10,... | collective-permute-start | bytes 1032200 | tf_op jit(solution)/shard_map/ppermute | solution.py:446
  607.0 9.8 %all-to-all-start.7 = ((f32[32,1,128]{2,1,0:T(1,128)}), f32[32,1,128]{2,1,0:T(1,128)S(1)}, u32[]{:S(2)}, u32[]{:S(2)}) async-start(f32[32,1,128]{2,1,0:T(1,128)} %bitcast.285), calls=%async_computation.7 | async-start | bytes 32768 | tf_op jit(solution)/shard_map/all_to_all | solution.py:1037
  (78 other events, 515.9 us)
Sparse Core Ops, SparseCore 0:
  11.5 87.2 all-gather.7
  102.3 114.5 all-gather.9
  343.2 99.9 all-gather.5

commit v3 on v2

--- a/solution.py
+++ b/solution.py
@@ -29,6 +29,7 @@
 SCALE_LOG2 = SCALE * math.log2(math.e)
 VMEM = 56 * 2**20
 HEAD_BLOCK = 2048
+SMALL_COST = pl.CostEstimate(flops=1, bytes_accessed=1, transcendentals=0)
 bf16 = jnp.bfloat16
 f32 = jnp.float32
 
@@ -235,6 +236,55 @@
     )(first, queries, key_values, key_values, attended, grad_attended, lse)
 
 
+def layer_stats_kernel(
+    valid_ref, attended_ref, x_ref, wout_ref, wup_ref, wdown_ref, gain_ref, row_ref, out_ref
+):
+    block = x_ref.shape[0]
+    step = pl.program_id(0)
+    embedded = x_ref[...]
+    branch = nn(attended_ref[...], wout_ref[...])
+    middle = embedded + branch
+    normed = layer_norm(middle, gain_ref[...]).astype(bf16)
+    active = gelu_tanh(nn(normed, wup_ref[...])).astype(bf16)
+    second = nn(active, wdown_ref[...])
+    valid = step * block + lax.broadcasted_iota(jnp.int32, (block, 1), 0) < valid_ref[0]
+    lane = lax.broadcasted_iota(jnp.int32, (1, LANES), 1)
+    sums = jnp.zeros((1, LANES), f32)
+    for at, values in enumerate((embedded, branch, second, middle + second)):
+        mean = jnp.where(valid, jnp.mean(values * values, 1, keepdims=True), 0.0)
+        sums = jnp.where(lane == at + 2, jnp.sum(mean, 0, keepdims=True), sums)
+
+    @pl.when(step == 0)
+    def _():
+        out_ref[...] = row_ref[...] + sums
+
+    @pl.when(step > 0)
+    def _():
+        out_ref[...] += sums
+
+
+def layer_stats(valid, attended, embedded, w_out, w_up, w_down, gain, row):
+    length, block = embedded.shape[0], 256
+    blocked = pl.BlockSpec((block, D), lambda i, s: (i, 0))
+
+    def whole(value):
+        return pl.BlockSpec(value.shape, lambda i, s: (0, 0), pipeline_mode=pl.Buffered(1))
+
+    return pl.pallas_call(
+        layer_stats_kernel,
+        grid_spec=pltpu.PrefetchScalarGridSpec(
+            num_scalar_prefetch=1,
+            grid=(length // block,),
+            in_specs=[blocked, blocked] + [whole(v) for v in (w_out, w_up, w_down, gain, row)],
+            out_specs=pl.BlockSpec((1, LANES), lambda i, s: (0, 0)),
+        ),
+        out_shape=jax.ShapeDtypeStruct((1, LANES), f32),
+        compiler_params=pltpu.CompilerParams(vmem_limit_bytes=VMEM),
+        cost_estimate=SMALL_COST,
+        name="layer_stats",
+    )(valid, attended, embedded, w_out, w_up, w_down, gain, row)
+
+
 def first_back_kernel(
     bounds_ref, k_ref, v_ref, wkv_ref, q_ref, wq_ref, x_ref, gain_ref, middle_ref, target_ref,
     patch_ref, looked_ref, dgain_ref, normed, residual, pulled,
@@ -553,9 +603,7 @@
         out_shape=[shape, shape],
         scratch_shapes=scratch,
         compiler_params=pltpu.CompilerParams(vmem_limit_bytes=VMEM),
-        cost_estimate=pl.CostEstimate(
-            flops=flops, bytes_accessed=4 * world // 2 * total * D, transcendentals=0
-        ),
+        cost_estimate=SMALL_COST,
         name="grad_pack",
     )(core, *operands)
 
@@ -644,21 +692,25 @@
     return (weight_new, moment_new, average_new)
 
 
-def finish_sum_kernel(row_ref, *refs):
-    terms, (total_ref, spread_ref) = refs[:-2], refs[-2:]
+def finish_sum_kernel(*refs, count):
+    (row_ref, *square_refs), terms, (total_ref, spread_ref) = (
+        refs[:count], refs[count:-2], refs[-2:]
+    )
     total = sum((term[...].astype(f32) for term in terms[1:]), terms[0][...].astype(f32))
     total_ref[...] = total
     squares = jnp.sum(jnp.sum(total * total, 0, keepdims=True), 1, keepdims=True)
     lane = lax.broadcasted_iota(jnp.int32, (1, LANES), 1)
+    for ref in square_refs:
+        squares = squares + ref[...]
     row = row_ref[...] + jnp.where(lane == 0, squares, 0.0)
     spread_ref[...] = jnp.broadcast_to(row, spread_ref.shape)
 
 
-def finish_sum(terms, row, world):
+def finish_sum(terms, numbers, world):
     vmem = pl.BlockSpec(memory_space=pltpu.VMEM)
     return pl.pallas_call(
-        finish_sum_kernel,
-        in_specs=[vmem] * (1 + len(terms)),
+        lambda *refs: finish_sum_kernel(*refs, count=len(numbers)),
+        in_specs=[vmem] * (len(numbers) + len(terms)),
         out_specs=[vmem] * 2,
         out_shape=[
             jax.ShapeDtypeStruct(terms[0].shape, f32),
@@ -666,7 +718,7 @@
         ],
         compiler_params=pltpu.CompilerParams(vmem_limit_bytes=VMEM),
         name="finish_sum",
-    )(row, *terms)
+    )(*numbers, *terms)
 
 
 def clip_factor(totals):
@@ -777,7 +829,6 @@
     positions = jnp.arange(tokens_here, dtype=jnp.int32)
     is_patch = (positions < first_tok)[:, None]
     is_token = (positions >= first_tok) & (positions < first_tok + alive)
-    is_valid = (positions < first_tok + alive)[:, None]
     target_owner = owner[:, 0]
 
     share = -(-3 * tokens_here // (2 * world) // 16) * 16
@@ -917,6 +968,7 @@
     group_rows = jnp.stack([line, other_core(line)])
     group_rows = group_rows.reshape(-1, D)
     carry = head_scan(after(group_rows, last_up, last_down), chunks[:5], last=False)
+    rows_sent = after(own_rows, carry[0], chunks[-1], chunks[-2])
     mine, theirs = head_scan(group_rows, chunks[5:], carry)
     (line,) = merge([mine, other_core(theirs)])
     mean_own, own_total = merge(
@@ -930,7 +982,7 @@
     own_weight = lax.dynamic_slice_in_dim(row_live, place, 1, 0)[0]
     loss_part = jnp.sum(own_weight * (own_total - picked))
 
-    rows_all = lax.all_gather(after(own_rows, mean_own), AXES, axis=0, tiled=True)
+    rows_all = lax.all_gather(rows_sent, AXES, axis=0, tiled=True)
     high = lax.reduce_precision(own_total, 8, 7)
     low = lax.reduce_precision(own_total - high, 8, 7)
     total_row = jnp.concatenate([high, low, own_total - high - low])[None, :]
@@ -943,15 +995,22 @@
     grad_middle, grad_gain_mid = mid_back(nt(grad_hidden, w_up))
     grad_middle = grad_result + grad_middle
     grad_branch = grad_middle.astype(bf16)
-    grad_attended = nt(grad_branch, w_out).astype(bf16)
+    late_mine, late_theirs = grad_pack(
+        [(normed_mid, grad_hidden), (active_pick, grad_second), (attended_pick, grad_branch)],
+        [], world,
+    )
+    grad_attended = after(nt(grad_branch, w_out).astype(bf16), late_theirs)
     grad_q, grad_k, grad_v = attention_back(
         pick_at, query_pick, key_values, attended_pick, grad_attended, lse_pick
     )
+    late_sum = RingSum(late_mine, late_theirs, gate=grad_q)
+    late_sum.ready()
     grad_patch_rows, grad_looked, grad_gain_first = first_back(
-        jnp.reshape(first_tok, (1,)), grad_k, grad_v, w_kv, grad_q, w_q, embedded,
-        gain_all[0:1], grad_middle, -scaled_weight * own_rows.astype(f32),
-    )
-    packed = far_pack(first_slots, grad_looked, share, total_row)
+        jnp.reshape(first_tok, (1,)), after(grad_k, late_sum.upward), grad_v, w_kv, grad_q, w_q,
+        embedded, gain_all[0:1], grad_middle, -scaled_weight * own_rows.astype(f32),
+    )
+    late_sum.hop(grad_looked)
+    packed = far_pack(first_slots, after(grad_looked, late_sum.upward), share, total_row)
     grad_arrived = far_send(packed, share)
     grad_gain = jnp.stack([grad_gain_first[0], grad_gain_mid, grad_gain_last])
     early_mine, early_theirs = grad_pack(
@@ -963,30 +1022,19 @@
         ],
         [grad_gain], world,
     )
-    late_mine, late_theirs = grad_pack(
-        [
-            (normed_mid, after(grad_hidden, early_theirs)),
-            (active_pick, grad_second),
-            (attended_pick, grad_branch),
-        ],
-        [], world,
-    )
-    early_sum = RingSum(early_mine, early_theirs, True)
-    late_sum = RingSum(late_mine, late_theirs)
-    late_sum.ready()
-
-    branch = jnp.dot(after(attended, late_sum.upward), w_out, preferred_element_type=f32)
-    middle = embedded + branch
-    normed_second = layer_norm(middle, gain_all[1]).astype(bf16)
-    hidden = jnp.dot(normed_second, w_up, preferred_element_type=f32)
-    second = jnp.dot(gelu_tanh(hidden).astype(bf16), w_down, preferred_element_type=f32)
-    result = middle + second
-
-    grad_arrived = after(grad_arrived, normed_second)
+
+    lane = lax.broadcasted_iota(jnp.int32, (1, LANES), 1)
+    row = layer_stats(
+        jnp.reshape(first_tok + alive, (1,)), after(attended, early_theirs), embedded, w_out, w_up,
+        w_down, gain_all[1:2], jnp.where(lane == 1, loss_part, 0.0),
+    )
+
+    early_sum = RingSum(early_mine, early_theirs, True, gate=row)
+    grad_arrived = after(grad_arrived, early_sum.terms[0])
+    late_sum.hop(grad_arrived)
     spare_rows = grad_arrived.reshape(owners, groups, share, D)[:, :, share - 1].astype(f32)
     total_all = spare_rows[..., :LOSS] + spare_rows[..., LOSS : 2 * LOSS] + spare_rows[..., 2 * LOSS :]
     total_all = total_all.transpose(1, 0, 2)
-    late_sum.hop(grad_arrived)
     early_sum.ready(late_sum.upward)
     head_first = head_grad(
         table_low, after(rows_all, late_sum.upward, early_sum.upward), total_all, head_weight, 0
@@ -1013,27 +1061,14 @@
 
     grad_table = lax.fori_loop(0, turns, next_turn, grad_table)
 
-    def square_sum(values):
-        return jnp.sum(jnp.where(is_valid, jnp.mean(values * values, 1, keepdims=True), 0.0))
-
     edge = 3 * rows_attn + rows_patch
     summed_gain = lax.dynamic_slice_in_dim(
         summed_early[edge : edge + 3], place * cols_gain, cols_gain, 1
     )
-    squares = (
-        jnp.sum(grad_table * grad_table)
-        + jnp.sum(summed_early[:edge] * summed_early[:edge])
-        + jnp.sum(summed_gain * summed_gain)
-    )
-    row = jnp.zeros((1, LANES), f32)
-    lane = lax.broadcasted_iota(jnp.int32, (1, LANES), 1)
-    scalars = (
-        squares, loss_part, square_sum(embedded), square_sum(branch), square_sum(second),
-        square_sum(result),
-    )
-    for at, value in enumerate(scalars):
-        row = jnp.where(lane == at, value, row)
-    summed_late, spread = finish_sum(late_terms, row, world)
+    squares = [
+        jnp.sum(part * part, keepdims=True) for part in (grad_table, summed_early[:edge], summed_gain)
+    ]
+    summed_late, spread = finish_sum(late_terms, [row, *squares], world)
     spread = lax.all_to_all(spread, AXES, 0, 0, tiled=True)
     *matrices, totals = renew_matrices(
         spread, summed_early, summed_late,

time: 652 us -> 634 us (0.972)
  Pallas kernels: 200 us -> 221 us
  matrix products: 66.8 us -> 46.6 us
  other arithmetic: 84.5 us -> 70.2 us
  starting transfers between devices: 37.2 us -> 44.2 us
    pallas_call x1 -> x2, Pallas kernels: 2.07 us -> 25.3 us  [the longest x1 21.3 us: layer_stats(): pl.pallas_call(layer_stats_kernel, grid_spec=pltpu.PrefetchScalarGridSpec...]
    dot_general x2 -> x0, matrix products: 18.8 us -> none  [the longest x1 15.7 us: shards(): jnp.dot(gelu_tanh(hidden).astype(bf16), w_down, preferred_element_type=f32)]
    all_to_all x1, waiting for transfers between devices: 24.1 us -> 10.4 us  [far_send(): lax.all_to_all(packed.reshape(world, share, D), ('mp', 'dp'), split_axis=...]
    all_to_all x1, waiting for transfers between devices: 42.3 us -> 30.1 us  [far_fetch(): lax.all_to_all(rows.reshape(world, share, D), ('mp', 'dp'), split_axis=0,...]
    ppermute x30, waiting for transfers between devices: 54.2 us -> 65.8 us  [permute(): lax.ppermute(value, axis, [(i, target(i)) for i in range(lax.axis_size(ax...]
    all_gather x2, waiting for transfers between devices: 9.85 us -> 20.4 us  [shards(): lax.all_gather(jnp.pad(w, ((0, -w.shape[0] % 8), (0, 0))), AXES, axis=0,...]
    reduce_sum x10 -> x3, other arithmetic: 11.2 us -> 2.77 us  [shards(): jnp.sum(part * part, keepdims=True)]
    dot_general x2 -> x0, local copies, waits for them, and re-layouts: 7.95 us -> none  [the longest x1 4.11 us: shards(): jnp.dot(after(attended, late_sum.upward), w_out, preferred_element_type=f32)]
  transfers between devices with their start and end apart: 36 -> 36, of which waited for: 10 -> 18; matrix products, arithmetic and copies ran while one was open for 26% -> 21% of each run, Pallas kernels for 26% -> 34%
where the time goes in v3:
time: 634 us; the launch traced here: 624 us
  Pallas kernels  221 us (35%)
  waiting for transfers between devices  133 us (21%)
  other arithmetic  70.2 us (11%)
  matrix products  46.6 us (7%)
  local copies, waits for them, and re-layouts  44.3 us (7%)
  starting transfers between devices  44.2 us (7%)
  blocking collectives  42 us (7%)
  between operations  22.4 us (4%)
    ppermute x30, waiting for transfers between devices, permute(): lax.ppermute(value, axis, [(i, target(i)) for i in range(lax.axis_size(ax...  65.8 us
    pallas_call x2, Pallas kernels, head_scan(): pl.pallas_call(lambda *refs: head_scan_kernel(*refs, carried=bool(carry),...  47.6 us
    all_to_all x1, blocking collectives, far_ids(): lax.all_to_all(ids, ('mp', 'dp'), split_axis=0, concat_axis=0, tiled=True)  42 us
    pallas_call x2, Pallas kernels, head_grad(): pl.pallas_call(head_grad_kernel, grid=(part,), in_specs=[whole, pl.BlockS...  37.2 us
    ppermute x30, starting transfers between devices, permute(): lax.ppermute(value, axis, [(i, target(i)) for i in range(lax.axis_size(ax...  32.2 us
    all_to_all x1, waiting for transfers between devices, far_fetch(): lax.all_to_all(rows.reshape(world, share, D), ('mp', 'dp'), split_axis=0,...  30.1 us
    pallas_call x1, Pallas kernels, attention_all(): pl.pallas_call(lambda *refs: attention_all_kernel(*refs, block=512), grid...  29.9 us
    pallas_call x1, Pallas kernels, layer_stats(): pl.pallas_call(layer_stats_kernel, grid_spec=pltpu.PrefetchScalarGridSpec...  21.3 us
  transfers between devices with their start and end apart: 36, of which 18 were waited for; matrix products, arithmetic and copies ran while one was open for 21% of the time, Pallas kernels for 34%

profile of v3, /device:TPU:0, one launch (start us, length us, event | category | flops | bytes accessed | tf_op | source)
XLA Modules:
  0.0 623.9 jit_solution(494057704324769335)
XLA Ops:
  12.9 3.1 collective-permute-start
  25.8 42.0 %all_to_all.75 = s32[32,1,49]{2,1,0:T(1,128)S(1)} all-to-all(s32[32,1,49]{2,1,0:T(1,128)S(1)} %bitcast.275), channel_id=1, replica_groups=mesh['dp'=8,'mp'=4] {'mp','dp'}, dimensions={0} | all-to-all | bytes 12544 | tf_op jit(solution)/shard_map/all_to_all | solution.py:856
  68.0 4.8 fusion.28
  72.8 3.5 all-to-all-start.5
  84.4 20.4 %all-gather.8.cloned.1.call-done = bf16[1024,3072]{1,0:T(8,128)(2,1)} async-done(((bf16[32,3072]{1,0:T(8,128)(2,1)}), bf16[1024,3072]{1,0:T(8,128)(2,1)}) %all-gather.8.cloned.1.call-update) | async-done | bytes 6291472 | tf_op jit(solution)/shard_map/all_gather | solution.py:821
  104.8 3.3 slice.177
  112.3 3.2 fusion.105
  115.5 30.1 %all-to-all-done.5 = bf16[32,48,768]{2,1,0:T(8,128)(2,1)} async-done(((bf16[32,48,768]{2,1,0:T(8,128)(2,1)}), bf16[32,48,768]{2,1,0:T(8,128)(2,1)}, u32[]{:S(2)}, u32[]{:S(2)}) %all-to-all-start.5) | async-done | bytes 2359328 | tf_op jit(solution)/shard_map/all_to_all | solution.py:867
  147.1 4.5 fusion.23
  151.9 3.9 fusion.112
  159.7 3.9 convolution_convert_fusion.k_ref.v_ref.refs_1_.refs_2_
  163.6 15.8 %attention_pick.1 = (bf16[256,768]{1,0:T(8,128)(2,1)}, f32[6,8,256]{2,1,0:T(8,128)}) custom-call(s32[1]{0:T(128)} %bitcast.11.first_ref, bf16[256,768]{1,0:T(8,128)(2,1)} %convolution_convert_fusion.3.q_ref, bf16[1024,1536]{1,0:T(8,128)(2,1)} %convolution_convert_fusion.k_ref.v_ref.refs_1_.refs_2_, ...), custom_call_target="tpu_custom_call" | custom-call | flops 3221225472 | bytes 4718592 | tf_op jit(solution)/shard_map/attention_pick/pallas_call | solution.py:141
  179.4 2.5 convolution_convert_fusion.1.refs_0_
  189.6 29.9 %attention_all.1.attended_ref = bf16[1024,768]{1,0:T(8,128)(2,1)} custom-call(bf16[1024,768]{1,0:T(8,128)(2,1)} %convolution_convert_fusion.1.refs_0_, bf16[1024,1536]{1,0:T(8,128)(2,1)} %convolution_convert_fusion.k_ref.v_ref.refs_1_.refs_2_, bf16[1024,1536]{1,0:T(8,128)(2,1)} %convolution_convert_fusion.k_ref.v_ref.refs_1_.refs_2_), custom_call_target="tpu_custom_call" | custom-call | flops 12884901888 | bytes 6291456 | tf_op jit(solution)/shard_map/attention_all/pallas_call | solution.py:99
  222.3 6.3 %collective-permute-done.4.refs_4_ = bf16[1032,768]{1,0:T(8,128)(2,1)} collective-permute-done((bf16[1032,768]{1,0:T(8,128)(2,1)}, bf16[1032,768]{1,0:T(8,128)(2,1)}, u32[]{:S(2)}, u32[]{:S(2)}) %collective-permute-start.4) | collective-permute-done | bytes 1585184 | tf_op jit(solution)/shard_map/ppermute | solution.py:496
  232.8 2.8 slice.188
  240.1 3.7 multiply_convert_fusion
  250.3 8.8 %collective-permute-done.2 = bf16[256,768]{1,0:T(8,128)(2,1)S(1)} collective-permute-done((bf16[256,768]{1,0:T(8,128)(2,1)S(1)}, bf16[256,768]{1,0:T(8,128)(2,1)S(1)}, u32[]{:S(2)}, u32[]{:S(2)}) %collective-permute-start.2) | collective-permute-done | bytes 393248 | tf_op jit(solution)/shard_map/ppermute | solution.py:496
  259.3 8.1 %collective-permute-done.7.refs_4_ = bf16[1032,768]{1,0:T(8,128)(2,1)} collective-permute-done((bf16[1032,768]{1,0:T(8,128)(2,1)}, bf16[1032,768]{1,0:T(8,128)(2,1)}, u32[]{:S(2)}, u32[]{:S(2)}) %collective-permute-start.7) | collective-permute-done | bytes 1585184 | tf_op jit(solution)/shard_map/ppermute | solution.py:496
  273.8 26.1 %head_scan.2 = (f32[1024,768]{1,0:T(8,128)}, f32[1024,1]{1,0:T(8,128)}) custom-call(bf16[1024,768]{1,0:T(8,128)(2,1)} %bitcast.266, bf16[1032,768]{1,0:T(8,128)(2,1)S(1)} %copy-done.25, bf16[1032,768]{1,0:T(8,128)(2,1)} %collective-permute-done.refs_2_, bf16[1032,768]{1,0:T(8,128)(2,1)} %collective-permute-done.1.refs_3_, ...), custom_call_target="tpu_custom_call" | custom-call | flops 16231956480 | bytes 11071488 | tf_op jit(solution)/shard_map/head_scan/pallas_call | solution.py:437
  300.0 21.5 %head_scan.3 = (bf16[512,896]{1,0:T(8,128)(2,1)}, bf16[512,896]{1,0:T(8,128)(2,1)}) custom-call(bf16[1024,768]{1,0:T(8,128)(2,1)} %bitcast.267, f32[1024,768]{1,0:T(8,128)} %get-tuple-element.210.refs_1_, f32[1024,1]{1,0:T(8,128)} %get-tuple-element.212.refs_2_, bf16[1032,768]{1,0:T(8,128)(2,1)} %collective-permute-done.6.refs_3_, ...), custom_call_target="tpu_custom_call" | custom-call | flops 9739173888 | bytes 7901184 | tf_op jit(solution)/shard_map/head_scan/pallas_call | solution.py:437
  321.6 2.7 collective-permute-done.10.refs_1_
  325.3 3.2 merge.2
  334.5 16.4 %collective-permute-done.11.refs_1_ = bf16[256,896]{1,0:T(8,128)(2,1)} collective-permute-done((bf16[256,896]{1,0:T(8,128)(2,1)}, bf16[256,896]{1,0:T(8,128)(2,1)}, u32[]{:S(2)}, u32[]{:S(2)}) %collective-permute-start.11) | collective-permute-done | bytes 458784 | tf_op jit(solution)/shard_map/ppermute | solution.py:496
  358.3 5.4 fusion.35.refs_2_
  367.0 9.7 %grad_pack.2 = (bf16[16,224,768]{2,1,0:T(8,128)(2,1)}, bf16[16,224,768]{2,1,0:T(8,128)(2,1)}) custom-call(s32[1]{0:T(128)} %bitcast.24.refs_0_, bf16[256,768]{1,0:T(8,128)(2,1)} %copy-done.31, bf16[256,3072]{1,0:T(8,128)(2,1)} %copy-done.29, bf16[256,3072]{1,0:T(8,128)(2,1)} %copy-done.28, bf16[256,768]{1,0:T(8,128)(2,1)} %copy-done.32, ...), custom_call_target="tpu_custom_call" | custom-call | flops 1 | bytes 1 | tf_op jit(solution)/shard_map/grad_pack/pallas_call | solution.py:598
  378.7 21.1 %attention_back.1 = (bf16[256,768]{1,0:T(8,128)(2,1)}, bf16[1024,768]{1,0:T(8,128)(2,1)}, bf16[1024,768]{1,0:T(8,128)(2,1)}) custom-call(s32[1]{0:T(128)} %bitcast.11.first_ref, bf16[256,768]{1,0:T(8,128)(2,1)} %convolution_convert_fusion.3.q_ref, bf16[1024,1536]{1,0:T(8,128)(2,1)} %convolution_convert_fusion.k_ref.v_ref.refs_1_.refs_2_, ...), custom_call_target="tpu_custom_call" | custom-call | flops 8053063680 | bytes 7864320 | tf_op jit(solution)/shard_map/attention_back/pallas_call | solution.py:210
  405.4 12.9 %first_back.1 = (bf16[1024,768]{1,0:T(8,128)(2,1)}, bf16[1024,768]{1,0:T(8,128)(2,1)S(1)}, f32[1,768]{1,0:T(1,128)}) custom-call(s32[1]{0:T(128)} %bitcast.31.bounds_ref, bf16[1024,768]{1,0:T(8,128)(2,1)} %get-tuple-element.223.k_ref.refs_4_, bf16[1024,768]{1,0:T(8,128)(2,1)} %get-tuple-element.224.v_ref.refs_6_, bf16[768,1536]{1,0:T(8,128)(2,1)} %bitcast.249, ...), custom_call_target="tpu_custom_call" | custom-call | flops 2415919104 | bytes 12582912 | tf_op jit(solution)/shard_map/first_back/pallas_call | solution.py:330
  421.2 3.4 fusion.46
  424.5 4.8 select_convert_fusion
  429.3 4.1 all-to-all-start.6
  435.5 11.1 %grad_pack.3 = (bf16[16,112,768]{2,1,0:T(8,128)(2,1)}, bf16[16,112,768]{2,1,0:T(8,128)(2,1)}) custom-call(s32[1]{0:T(128)} %bitcast.24.refs_0_, bf16[256,768]{1,0:T(8,128)(2,1)} %copy-done.18, bf16[256,768]{1,0:T(8,128)(2,1)} %get-tuple-element.220.q_ref.refs_2_, bf16[1024,768]{1,0:T(8,128)(2,1)} %copy-done.4, ...), custom_call_target="tpu_custom_call" | custom-call | flops 1 | bytes 1 | tf_op jit(solution)/shard_map/grad_pack/pallas_call | solution.py:598
  448.8 21.3 %layer_stats.1.refs_0_ = f32[1,128]{1,0:T(1,128)} custom-call(s32[1]{0:T(128)} %bitcast.39.valid_ref, bf16[1024,768]{1,0:T(8,128)(2,1)} %attention_all.1.attended_ref, f32[1024,768]{1,0:T(8,128)} %copy-done, bf16[768,768]{1,0:T(8,128)(2,1)} %bitcast.242, bf16[768,3072]{1,0:T(8,128)(2,1)} %bitcast.234, bf16[3072,768]{1,0:T(8,128)(2,1)} %bitcast.240, ...), custom_call_target="tpu_custom_call" | custom-call | flops 1 | bytes 1 | tf_op jit(solution)/shard_map/layer_stats/pallas_call | solution.py:273
  471.6 3.5 add_convert_fusion.1
  478.9 10.4 %all-to-all-done.6 = bf16[32,48,768]{2,1,0:T(8,128)(2,1)} async-done(((bf16[32,48,768]{2,1,0:T(8,128)(2,1)}), bf16[32,48,768]{2,1,0:T(8,128)(2,1)}, u32[]{:S(2)}, u32[]{:S(2)}) %all-to-all-start.6) | async-done | bytes 2359328 | tf_op jit(solution)/shard_map/all_to_all | solution.py:882
  489.3 6.8 %collective-permute-done.15 = bf16[2,224,768]{2,1,0:T(8,128)(2,1)} collective-permute-done((bf16[2,224,768]{2,1,0:T(8,128)(2,1)}, bf16[2,224,768]{2,1,0:T(8,128)(2,1)}, u32[]{:S(2)}, u32[]{:S(2)}) %collective-permute-start.15) | collective-permute-done | bytes 688160 | tf_op jit(solution)/shard_map/ppermute | solution.py:496
  496.1 4.3 collective-permute-done.16
  500.5 3.7 fusion.44
  504.2 2.6 collective-permute-start.17
  506.8 4.2 collective-permute-done.20
  518.1 18.0 %head_grad.2.refs_0_ = f32[1032,768]{1,0:T(8,128)} custom-call(bf16[1032,768]{1,0:T(8,128)(2,1)S(1)} %copy-done.26, bf16[8192,768]{1,0:T(8,128)(2,1)} %all-gather.6.cloned.1.call-done.rows_ref, f32[4,1,2048]{2,1,0:T(1,128)} %reshape.545.lse_ref, f32[4,1,2048]{2,1,0:T(1,128)} %fusion.83.weight_ref), custom_call_target="tpu_custom_call" | custom-call | flops 12985565184 | bytes 11046912 | tf_op jit(solution)/shard_map/head_grad/pallas_call | solution.py:479
  542.2 19.2 %head_grad.3 = f32[1032,768]{1,0:T(8,128)} custom-call(bf16[1032,768]{1,0:T(8,128)(2,1)S(1)} %copy-done.26, bf16[8192,768]{1,0:T(8,128)(2,1)} %all-gather.6.cloned.1.call-done.rows_ref, f32[4,1,2048]{2,1,0:T(1,128)} %reshape.545.lse_ref, f32[4,1,2048]{2,1,0:T(1,128)} %fusion.83.weight_ref, f32[1032,768]{1,0:T(8,128)} %head_grad.2.refs_0_), custom_call_target="tpu_custom_call" | custom-call | flops 12985565184 | bytes 11046912 | tf_op jit(solution)/shard_map/head_grad/pallas_call | solution.py:479
  567.2 4.9 fusion.25
  583.9 4.0 finish_sum.1
  587.9 4.2 all-to-all-start.7
  592.7 6.5 %all-to-all-done.7 = f32[32,1,128]{2,1,0:T(1,128)S(1)} async-done(((f32[32,1,128]{2,1,0:T(1,128)}), f32[32,1,128]{2,1,0:T(1,128)S(1)}, u32[]{:S(2)}, u32[]{:S(2)}) %all-to-all-start.7) | async-done | bytes 16416 | tf_op jit(solution)/shard_map/all_to_all | solution.py:1072
  599.8 4.3 renew_matrices.1
  608.0 5.1 fusion.98
  (365 shorter events, 135.3 us)
Async XLA Ops:
  7.2 97.6 %all-gather.8.cloned.1.call-start = ((), (), s32[]{:S(2)}) async-start(), calls=%async_computation.9 | async-start | bytes 6488064 | tf_op jit(solution)/shard_map/all_gather | solution.py:821
  10.8 222.0 %all-gather.10.cloned.1.call-start = ((), (), s32[]{:S(2)}) async-start(), calls=%async_computation.10 | async-start | bytes 9732096 | tf_op jit(solution)/shard_map/all_gather | solution.py:821
  12.9 59.8 %copy-start.24 = (bf16[1032,768]{1,0:T(8,128)(2,1)}, bf16[1032,768]{1,0:T(8,128)(2,1)S(1)}, u32[]{:S(2)}) copy-start(bf16[1032,768]{1,0:T(8,128)(2,1)S(1)} %convert_element_type.401.refs_1_.table_ref) | copy-start | bytes 4755460
  12.9 59.8 %collective-permute-start = (bf16[1032,768]{1,0:T(8,128)(2,1)S(1)}, bf16[1032,768]{1,0:T(8,128)(2,1)}, u32[]{:S(2)}, u32[]{:S(2)}) collective-permute-start(bf16[1032,768]{1,0:T(8,128)(2,1)S(1)} %convert_element_type.401.refs_1_.table_ref), channel_id=1, source_target_pairs={{0,8},{4,0},{8,16},{12,4},{16,24},{20,12},{24,28},{28,20},{1,9},{5... | collective-permute-start | bytes 4755464 | tf_op jit(solution)/shard_map/ppermute | solution.py:496
  16.0 56.8 %collective-permute-start.1 = (bf16[1032,768]{1,0:T(8,128)(2,1)S(1)}, bf16[1032,768]{1,0:T(8,128)(2,1)}, u32[]{:S(2)}, u32[]{:S(2)}) collective-permute-start(bf16[1032,768]{1,0:T(8,128)(2,1)S(1)} %convert_element_type.401.refs_1_.table_ref), channel_id=1, source_target_pairs={{0,4},{4,12},{8,0},{12,20},{16,8},{20,28},{24,16},{28,24},{1,5},{5... | collective-permute-start | bytes 4755464 | tf_op jit(solution)/shard_map/ppermute | solution.py:496
  23.4 123.7 %copy-start.69 = (s32[1024]{0:T(1024)}, s32[1024]{0:T(1024)S(1)}, u32[]{:S(2)}) copy-start(s32[1024]{0:T(1024)S(1)} %get-tuple-element.421) | copy-start | bytes 12292
  72.8 72.9 %all-to-all-start.5 = ((bf16[32,48,768]{2,1,0:T(8,128)(2,1)}), bf16[32,48,768]{2,1,0:T(8,128)(2,1)}, u32[]{:S(2)}, u32[]{:S(2)}) async-start(bf16[32,48,768]{2,1,0:T(8,128)(2,1)} %bitcast.6), calls=%async_computation.5 | async-start | bytes 4718592 | tf_op jit(solution)/shard_map/all_to_all | solution.py:867
  76.3 441.8 %all-gather.6.cloned.1.call-start = ((), (), s32[]{:S(2)}) async-start(), calls=%async_computation.8 | async-start | bytes 12976128 | tf_op jit(solution)/shard_map/all_gather | solution.py:985
  78.5 31.1 %copy-start.78 = (f32[32]{0:T(128)}, f32[32]{0:T(128)S(1)}, u32[]{:S(2)}) copy-start(f32[32]{0:T(128)S(1)} %fusion.85) | copy-start | bytes 388
  81.7 70.1 %copy-start.35 = (bf16[1024,128]{1,0:T(8,128)(2,1)}, bf16[1024,128]{1,0:T(8,128)(2,1)S(1)}, u32[]{:S(2)}) copy-start(bf16[1024,128]{1,0:T(8,128)(2,1)S(1)} %fusion.53) | copy-start | bytes 786436
  182.0 46.6 %collective-permute-start.4 = (bf16[1032,768]{1,0:T(8,128)(2,1)}, bf16[1032,768]{1,0:T(8,128)(2,1)}, u32[]{:S(2)}, u32[]{:S(2)}) collective-permute-start(bf16[1032,768]{1,0:T(8,128)(2,1)} %collective-permute-done.refs_2_), channel_id=1, source_target_pairs={{0,8},{4,0},{8,16},{12,4},{16,24},{20,12},{24,28},{28,20},{1,9},{5... | collective-permute-start | bytes 4755464 | tf_op jit(solution)/shard_map/ppermute | solution.py:496
  182.0 48.8 %collective-permute-start.5 = (bf16[1032,768]{1,0:T(8,128)(2,1)}, bf16[1032,768]{1,0:T(8,128)(2,1)}, u32[]{:S(2)}, u32[]{:S(2)}) collective-permute-start(bf16[1032,768]{1,0:T(8,128)(2,1)} %collective-permute-done.1.refs_3_), channel_id=1, source_target_pairs={{0,4},{4,12},{8,0},{12,20},{16,8},{20,28},{24,16},{28,24},{1,5},{5... | collective-permute-start | bytes 4755464 | tf_op jit(solution)/shard_map/ppermute | solution.py:496
  189.6 48.6 %copy-start.31 = (bf16[256,768]{1,0:T(8,128)(2,1)}, bf16[256,768]{1,0:T(8,128)(2,1)S(1)}, u32[]{:S(2)}) copy-start(bf16[256,768]{1,0:T(8,128)(2,1)S(1)} %multiply_convert_fusion.3.refs_1_) | copy-start | bytes 1179652
  230.7 36.7 %collective-permute-start.7 = (bf16[1032,768]{1,0:T(8,128)(2,1)}, bf16[1032,768]{1,0:T(8,128)(2,1)}, u32[]{:S(2)}, u32[]{:S(2)}) collective-permute-start(bf16[1032,768]{1,0:T(8,128)(2,1)} %collective-permute-done.5.refs_5_), channel_id=1, source_target_pairs={{0,4},{4,12},{8,0},{12,20},{16,8},{20,28},{24,16},{28,24},{1,5},{5... | collective-permute-start | bytes 4755464 | tf_op jit(solution)/shard_map/ppermute | solution.py:496
  232.2 36.7 %collective-permute-start.6 = (bf16[1032,768]{1,0:T(8,128)(2,1)}, bf16[1032,768]{1,0:T(8,128)(2,1)}, u32[]{:S(2)}, u32[]{:S(2)}) collective-permute-start(bf16[1032,768]{1,0:T(8,128)(2,1)} %collective-permute-done.4.refs_4_), channel_id=1, source_target_pairs={{0,8},{4,0},{8,16},{12,4},{16,24},{20,12},{24,28},{28,20},{1,9},{5... | collective-permute-start | bytes 4755464 | tf_op jit(solution)/shard_map/ppermute | solution.py:496
  248.8 10.3 %collective-permute-start.2 = (bf16[256,768]{1,0:T(8,128)(2,1)S(1)}, bf16[256,768]{1,0:T(8,128)(2,1)S(1)}, u32[]{:S(2)}, u32[]{:S(2)}) collective-permute-start(bf16[256,768]{1,0:T(8,128)(2,1)S(1)} %get-tuple-element.211), channel_id=1, source_target_pairs={{0,2},{1,3},{2,0},{3,1},{4,6},{5,7},{6,4},{7,5},{8,10},{9,11},{10,... | collective-permute-start | bytes 1179656 | tf_op jit(solution)/shard_map/ppermute | solution.py:496
  259.2 13.3 %collective-permute-start.3 = (bf16[2,256,768]{2,1,0:T(8,128)(2,1)S(1)}, bf16[2,256,768]{2,1,0:T(8,128)(2,1)S(1)}, u32[]{:S(2)}, u32[]{:S(2)}) collective-permute-start(bf16[2,256,768]{2,1,0:T(8,128)(2,1)S(1)} %get-tuple-element.411), channel_id=1, source_target_pairs={{0,1},{1,0},{2,3},{3,2},{4,5},{5,4},{6,7},{7,6},{8,9},{9,8},{10,11... | collective-permute-start | bytes 2359304 | tf_op jit(solution)/shard_map/ppermute | solution.py:496
  270.3 29.7 %collective-permute-start.8 = (bf16[520,768]{1,0:T(8,128)(2,1)S(1)}, bf16[520,768]{1,0:T(8,128)(2,1)}, u32[]{:S(2)}, u32[]{:S(2)}) collective-permute-start(bf16[520,768]{1,0:T(8,128)(2,1)S(1)} %slice.155), channel_id=1, source_target_pairs={{0,4},{4,12},{8,0},{12,20},{16,8},{20,28},{24,16},{28,24},{1,5},{5... | collective-permute-start | bytes 2396168 | tf_op jit(solution)/shard_map/ppermute | solution.py:496
  271.8 28.2 %collective-permute-start.9 = (bf16[512,768]{1,0:T(8,128)(2,1)S(1)}, bf16[512,768]{1,0:T(8,128)(2,1)}, u32[]{:S(2)}, u32[]{:S(2)}) collective-permute-start(bf16[512,768]{1,0:T(8,128)(2,1)S(1)} %slice.154), channel_id=1, source_target_pairs={{0,8},{4,0},{8,16},{12,4},{16,24},{20,12},{24,28},{28,20},{1,9},{5... | collective-permute-start | bytes 2359304 | tf_op jit(solution)/shard_map/ppermute | solution.py:496
  321.5 2.7 collective-permute-start.10
  325.2 29.1 %copy-start.68 = (f32[256]{0:T(256)S(1)}, f32[256]{0:T(256)}, u32[]{:S(2)}) copy-start(f32[256]{0:T(256)} %get-tuple-element.373) | copy-start | bytes 3076
  325.2 30.4 %copy-start.49 = (f32[768]{0:T(1024)S(1)}, f32[768]{0:T(1024)}, u32[]{:S(2)}) copy-start(f32[768]{0:T(1024)} %mul.450) | copy-start | bytes 9220
  325.2 30.4 %copy-start.53 = (f32[256]{0:T(256)S(1)}, f32[256]{0:T(256)}, u32[]{:S(2)}) copy-start(f32[256]{0:T(256)} %copy-done.52) | copy-start | bytes 3076
  325.2 30.4 %copy-start.57 = (f32[256]{0:T(256)S(1)}, f32[256]{0:T(256)}, u32[]{:S(2)}) copy-start(f32[256]{0:T(256)} %copy-done.56) | copy-start | bytes 3076
  328.5 29.2 %copy-start.63 = (f32[256]{0:T(256)S(1)}, f32[256]{0:T(256)}, u32[]{:S(2)}) copy-start(f32[256]{0:T(256)} %copy-done.62) | copy-start | bytes 3076
  330.7 20.2 %collective-permute-start.11 = (bf16[256,896]{1,0:T(8,128)(2,1)}, bf16[256,896]{1,0:T(8,128)(2,1)}, u32[]{:S(2)}, u32[]{:S(2)}) collective-permute-start(bf16[256,896]{1,0:T(8,128)(2,1)} %get-tuple-element.408), channel_id=1, source_target_pairs={{0,2},{1,3},{2,0},{3,1},{4,6},{5,7},{6,4},{7,5},{8,10},{9,11},{10,... | collective-permute-start | bytes 1376264 | tf_op jit(solution)/shard_map/ppermute | solution.py:496
  376.7 23.1 %collective-permute-start.12 = (bf16[16,224,768]{2,1,0:T(8,128)(2,1)}, bf16[16,224,768]{2,1,0:T(8,128)(2,1)}, u32[]{:S(2)}, u32[]{:S(2)}) collective-permute-start(bf16[16,224,768]{2,1,0:T(8,128)(2,1)} %get-tuple-element.217), channel_id=1, source_target_pairs={{0,1},{1,0},{2,3},{3,2},{4,5},{5,4},{6,7},{7,6},{8,9},{9,8},{10,11... | collective-permute-start | bytes 16515080 | tf_op jit(solution)/shard_map/ppermute | solution.py:496
  402.2 17.8 %collective-permute-start.13 = (bf16[2,224,768]{2,1,0:T(8,128)(2,1)S(1)}, bf16[2,224,768]{2,1,0:T(8,128)(2,1)S(1)}, u32[]{:S(2)}, u32[]{:S(2)}) collective-permute-start(bf16[2,224,768]{2,1,0:T(8,128)(2,1)S(1)} %get-tuple-element.393), channel_id=1, source_target_pairs={{0,8},{4,0},{8,16},{12,4},{16,24},{20,12},{24,28},{28,20},{1,9},{5... | collective-permute-start | bytes 2064392 | tf_op jit(solution)/shard_map/ppermute | solution.py:496
  403.5 17.7 %collective-permute-start.14 = (bf16[2,224,768]{2,1,0:T(8,128)(2,1)S(1)}, bf16[2,224,768]{2,1,0:T(8,128)(2,1)S(1)}, u32[]{:S(2)}, u32[]{:S(2)}) collective-permute-start(bf16[2,224,768]{2,1,0:T(8,128)(2,1)S(1)} %get-tuple-element.392), channel_id=1, source_target_pairs={{0,4},{4,12},{8,0},{12,20},{16,8},{20,28},{24,16},{28,24},{1,5},{5... | collective-permute-start | bytes 2064392 | tf_op jit(solution)/shard_map/ppermute | solution.py:496
  429.3 60.0 %all-to-all-start.6 = ((bf16[32,48,768]{2,1,0:T(8,128)(2,1)}), bf16[32,48,768]{2,1,0:T(8,128)(2,1)}, u32[]{:S(2)}, u32[]{:S(2)}) async-start(bf16[32,48,768]{2,1,0:T(8,128)(2,1)} %bitcast.34), calls=%async_computation.6 | async-start | bytes 4718592 | tf_op jit(solution)/shard_map/all_to_all | solution.py:882
  446.6 23.5 %collective-permute-start.19 = (bf16[16,112,768]{2,1,0:T(8,128)(2,1)}, bf16[16,112,768]{2,1,0:T(8,128)(2,1)S(1)}, u32[]{:S(2)}, u32[]{:S(2)}) collective-permute-start(bf16[16,112,768]{2,1,0:T(8,128)(2,1)} %get-tuple-element.237), channel_id=1, source_target_pairs={{0,1},{1,0},{2,3},{3,2},{4,5},{5,4},{6,7},{7,6},{8,9},{9,8},{10,11... | collective-permute-start | bytes 8257544 | tf_op jit(solution)/shard_map/ppermute | solution.py:496
  475.1 86.3 %copy-start.17 = (bf16[8,1,112,768]{3,2,1,0:T(8,128)(2,1)}, bf16[8,1,112,768]{3,2,1,0:T(8,128)(2,1)S(1)}, u32[]{:S(2)}) copy-start(bf16[8,1,112,768]{3,2,1,0:T(8,128)(2,1)S(1)} %get-tuple-element.400) | copy-start | bytes 4128772
  475.1 35.9 %collective-permute-start.20 = (bf16[8,112,768]{2,1,0:T(8,128)(2,1)}, bf16[8,112,768]{2,1,0:T(8,128)(2,1)}, u32[]{:S(2)}, u32[]{:S(2)}) collective-permute-start(bf16[8,112,768]{2,1,0:T(8,128)(2,1)} %get-tuple-element.401), channel_id=1, source_target_pairs={{0,2},{1,3},{2,0},{3,1},{4,6},{5,7},{6,4},{7,5},{8,10},{9,11},{10,... | collective-permute-start | bytes 4128776 | tf_op jit(solution)/shard_map/ppermute | solution.py:496
  476.8 19.3 %collective-permute-start.15 = (bf16[2,224,768]{2,1,0:T(8,128)(2,1)}, bf16[2,224,768]{2,1,0:T(8,128)(2,1)}, u32[]{:S(2)}, u32[]{:S(2)}) collective-permute-start(bf16[2,224,768]{2,1,0:T(8,128)(2,1)} %get-tuple-element.391), channel_id=1, source_target_pairs={{0,8},{4,0},{8,16},{12,4},{16,24},{20,12},{24,28},{28,20},{1,9},{5... | collective-permute-start | bytes 2064392 | tf_op jit(solution)/shard_map/ppermute | solution.py:496
  478.3 22.2 %collective-permute-start.16 = (bf16[2,224,768]{2,1,0:T(8,128)(2,1)}, bf16[2,224,768]{2,1,0:T(8,128)(2,1)}, u32[]{:S(2)}, u32[]{:S(2)}) collective-permute-start(bf16[2,224,768]{2,1,0:T(8,128)(2,1)} %get-tuple-element.390), channel_id=1, source_target_pairs={{0,4},{4,12},{8,0},{12,20},{16,8},{20,28},{24,16},{28,24},{1,5},{5... | collective-permute-start | bytes 2064392 | tf_op jit(solution)/shard_map/ppermute | solution.py:496
  489.3 28.8 %copy-start.26 = (bf16[1032,768]{1,0:T(8,128)(2,1)S(1)}, bf16[1032,768]{1,0:T(8,128)(2,1)}, u32[]{:S(2)}) copy-start(bf16[1032,768]{1,0:T(8,128)(2,1)} %get-tuple-element.671) | copy-start | bytes 4755460
  504.2 32.0 %collective-permute-start.17 = (bf16[2,224,768]{2,1,0:T(8,128)(2,1)}, bf16[2,224,768]{2,1,0:T(8,128)(2,1)}, u32[]{:S(2)}, u32[]{:S(2)}) collective-permute-start(bf16[2,224,768]{2,1,0:T(8,128)(2,1)} %get-tuple-element.389), channel_id=1, source_target_pairs={{0,8},{4,0},{8,16},{12,4},{16,24},{20,12},{24,28},{28,20},{1,9},{5... | collective-permute-start | bytes 2064392 | tf_op jit(solution)/shard_map/ppermute | solution.py:496
  512.8 23.4 %collective-permute-start.18 = (bf16[2,224,768]{2,1,0:T(8,128)(2,1)}, bf16[2,224,768]{2,1,0:T(8,128)(2,1)}, u32[]{:S(2)}, u32[]{:S(2)}) collective-permute-start(bf16[2,224,768]{2,1,0:T(8,128)(2,1)} %get-tuple-element.388), channel_id=1, source_target_pairs={{0,4},{4,12},{8,0},{12,20},{16,8},{20,28},{24,16},{28,24},{1,5},{5... | collective-permute-start | bytes 2064392 | tf_op jit(solution)/shard_map/ppermute | solution.py:496
  515.3 23.5 %collective-permute-start.21 = (bf16[112,768]{1,0:T(8,128)(2,1)}, bf16[112,768]{1,0:T(8,128)(2,1)S(1)}, u32[]{:S(2)}, u32[]{:S(2)}) collective-permute-start(bf16[112,768]{1,0:T(8,128)(2,1)} %get-tuple-element.407), channel_id=1, source_target_pairs={{0,8},{4,0},{8,16},{12,4},{16,24},{20,12},{24,28},{28,20},{1,9},{5... | collective-permute-start | bytes 516104 | tf_op jit(solution)/shard_map/ppermute | solution.py:496
  516.6 22.3 %collective-permute-start.22 = (bf16[112,768]{1,0:T(8,128)(2,1)S(1)}, bf16[112,768]{1,0:T(8,128)(2,1)S(1)}, u32[]{:S(2)}, u32[]{:S(2)}) collective-permute-start(bf16[112,768]{1,0:T(8,128)(2,1)S(1)} %get-tuple-element.406), channel_id=1, source_target_pairs={{0,4},{4,12},{8,0},{12,20},{16,8},{20,28},{24,16},{28,24},{1,5},{5... | collective-permute-start | bytes 516104 | tf_op jit(solution)/shard_map/ppermute | solution.py:496
  538.0 23.4 %collective-permute-start.23 = (bf16[2,224,768]{2,1,0:T(8,128)(2,1)S(1)}, bf16[2,224,768]{2,1,0:T(8,128)(2,1)S(1)}, u32[]{:S(2)}, u32[]{:S(2)}) collective-permute-start(bf16[2,224,768]{2,1,0:T(8,128)(2,1)S(1)} %fusion.43), channel_id=1, source_target_pairs={{0,8},{4,0},{8,16},{12,4},{16,24},{20,12},{24,28},{28,20},{1,9},{5... | collective-permute-start | bytes 2064392 | tf_op jit(solution)/shard_map/ppermute | solution.py:496
  540.0 21.4 %collective-permute-start.24 = (bf16[112,768]{1,0:T(8,128)(2,1)S(1)}, bf16[112,768]{1,0:T(8,128)(2,1)S(1)}, u32[]{:S(2)}, u32[]{:S(2)}) collective-permute-start(bf16[112,768]{1,0:T(8,128)(2,1)S(1)} %get-tuple-element.405), channel_id=1, source_target_pairs={{0,8},{4,0},{8,16},{12,4},{16,24},{20,12},{24,28},{28,20},{1,9},{5... | collective-permute-start | bytes 516104 | tf_op jit(solution)/shard_map/ppermute | solution.py:496
  540.5 20.9 %collective-permute-start.25 = (bf16[112,768]{1,0:T(8,128)(2,1)S(1)}, bf16[112,768]{1,0:T(8,128)(2,1)S(1)}, u32[]{:S(2)}, u32[]{:S(2)}) collective-permute-start(bf16[112,768]{1,0:T(8,128)(2,1)S(1)} %get-tuple-element.404), channel_id=1, source_target_pairs={{0,4},{4,12},{8,0},{12,20},{16,8},{20,28},{24,16},{28,24},{1,5},{5... | collective-permute-start | bytes 516104 | tf_op jit(solution)/shard_map/ppermute | solution.py:496
  562.6 9.6 %collective-permute-start.26 = (bf16[112,768]{1,0:T(8,128)(2,1)S(1)}, bf16[112,768]{1,0:T(8,128)(2,1)S(1)}, u32[]{:S(2)}, u32[]{:S(2)}) collective-permute-start(bf16[112,768]{1,0:T(8,128)(2,1)S(1)} %fusion.66), channel_id=1, source_target_pairs={{0,8},{4,0},{8,16},{12,4},{16,24},{20,12},{24,28},{28,20},{1,9},{5... | collective-permute-start | bytes 516104 | tf_op jit(solution)/shard_map/ppermute | solution.py:496
  565.8 18.1 %collective-permute-start.29 = (bf16[224,768]{1,0:T(8,128)(2,1)}, bf16[224,768]{1,0:T(8,128)(2,1)}, u32[]{:S(2)}, u32[]{:S(2)}) collective-permute-start(bf16[224,768]{1,0:T(8,128)(2,1)} %get-tuple-element.412), channel_id=1, source_target_pairs={{0,2},{1,3},{2,0},{3,1},{4,6},{5,7},{6,4},{7,5},{8,10},{9,11},{10,... | collective-permute-start | bytes 1032200 | tf_op jit(solution)/shard_map/ppermute | solution.py:496
  574.1 5.6 collective-permute-start.27
  575.8 5.5 collective-permute-start.28
  587.9 11.3 %all-to-all-start.7 = ((f32[32,1,128]{2,1,0:T(1,128)}), f32[32,1,128]{2,1,0:T(1,128)S(1)}, u32[]{:S(2)}, u32[]{:S(2)}) async-start(f32[32,1,128]{2,1,0:T(1,128)} %bitcast.277), calls=%async_computation.7 | async-start | bytes 32768 | tf_op jit(solution)/shard_map/all_to_all | solution.py:1072
  (75 other events, 422.9 us)
Sparse Core Ops, SparseCore 0:
  11.5 93.2 all-gather.7
  108.3 101.5 all-gather.9
  300.1 103.3 all-gather.5

commit v4 on v3

--- a/solution.py
+++ b/solution.py
@@ -470,23 +470,23 @@
         out_ref[...] += part
 
 
-def head_grad(table_low, rows, lse, weight, half, carry=()):
+def head_grad(table_low, rows, lse, weight, first, quarters, carry=()):
     vocab, count, block = table_low.shape[0], rows.shape[0], HEAD_BLOCK
     steps = count // block
-    part = steps // 2
-    stat = pl.BlockSpec((1, 1, block), lambda i: (i + half * part, 0, 0))
+    start, part = steps * first // 4, steps * quarters // 4
+    stat = pl.BlockSpec((1, 1, block), lambda i: (i + start, 0, 0))
     whole = pl.BlockSpec((vocab, D), lambda i: (0, 0))
     return pl.pallas_call(
         head_grad_kernel,
         grid=(part,),
-        in_specs=[whole, pl.BlockSpec((block, D), lambda i: (i + half * part, 0)), stat, stat]
+        in_specs=[whole, pl.BlockSpec((block, D), lambda i: (i + start, 0)), stat, stat]
         + [whole] * len(carry),
         out_specs=whole,
         out_shape=jax.ShapeDtypeStruct((vocab, D), f32),
         compiler_params=pltpu.CompilerParams(vmem_limit_bytes=VMEM),
         cost_estimate=pl.CostEstimate(
-            flops=2 * count * vocab * D, bytes_accessed=count * D + 6 * vocab * D,
-            transcendentals=count * vocab // 2,
+            flops=quarters * count * vocab * D, bytes_accessed=count * D + 6 * vocab * D,
+            transcendentals=quarters * count * vocab // 4,
         ),
         name="head_grad",
     )(table_low, rows, lse.reshape(steps, 1, block), weight, *carry)
@@ -845,9 +845,9 @@
     far_row = identity - dest * rows_own
     most = jnp.max(jnp.sum(leads_to.astype(jnp.int32), 0))
 
-    def far_slots(start, share, limit):
+    def far_slots(start, share):
         within = far_rank - start
-        fits = is_token & (within >= 0) & (within < limit)
+        fits = is_token & (within >= 0) & (within < share)
         return jnp.where(fits, dest * share + within, -1)
 
     def far_ids(slots, extra, share):
@@ -855,10 +855,10 @@
         ids = jnp.concatenate([ids, jnp.full((world, 1), extra, jnp.int32)], 1)
         return lax.all_to_all(ids, ("mp", "dp"), split_axis=0, concat_axis=0, tiled=True)
 
-    first_slots = far_slots(0, share, share - 1)
+    first_slots = far_slots(0, share)
     first_ids = far_ids(first_slots, most, share)
     few = 16
-    turns = (jnp.max(first_ids[:, share]) - (share - 1) + few - 1) // few
+    turns = (jnp.max(first_ids[:, share]) - share + few - 1) // few
 
     def far_fetch(slots, ids, share):
         spread = one_hot(ids[:, :share].reshape(-1), rows_own)
@@ -871,12 +871,10 @@
     def far_spread(slots, arrived, share):
         return jnp.dot(one_hot(slots, world * share), arrived, preferred_element_type=f32)
 
-    def far_pack(slots, values, share, extra=None):
-        rows = jnp.dot(one_hot(slots, world * share).T, values, preferred_element_type=f32)
-        if extra is not None:
-            spare = lax.broadcasted_iota(jnp.int32, (world * share, 1), 0) % share == share - 1
-            rows = jnp.where(spare, extra, rows)
-        return rows.astype(bf16)
+    def far_pack(slots, values, share):
+        return jnp.dot(
+            one_hot(slots, world * share).T, values, preferred_element_type=f32
+        ).astype(bf16)
 
     def far_send(packed, share):
         return lax.all_to_all(
@@ -914,7 +912,7 @@
     looked = far_spread(first_slots, arrived, share)
 
     def fetch_turn(turn, total):
-        slots = far_slots(share - 1 + turn * few, few, few)
+        slots = far_slots(share + turn * few, few)
         return total + far_spread(slots, far_fetch(slots, far_ids(slots, 0, few), few), few)
 
     looked = lax.fori_loop(0, turns, fetch_turn, looked)
@@ -983,9 +981,9 @@
     loss_part = jnp.sum(own_weight * (own_total - picked))
 
     rows_all = lax.all_gather(rows_sent, AXES, axis=0, tiled=True)
-    high = lax.reduce_precision(own_total, 8, 7)
-    low = lax.reduce_precision(own_total - high, 8, 7)
-    total_row = jnp.concatenate([high, low, own_total - high - low])[None, :]
+    total_all = lax.all_to_all(
+        jnp.broadcast_to(own_total[None, :], (world, LOSS)), AXES, 0, 0, tiled=True
+    )
 
     scaled_weight = (own_weight / present)[:, None]
     grad_rows = scaled_weight * (mean_own - target_rows)
@@ -1006,11 +1004,11 @@
     late_sum = RingSum(late_mine, late_theirs, gate=grad_q)
     late_sum.ready()
     grad_patch_rows, grad_looked, grad_gain_first = first_back(
-        jnp.reshape(first_tok, (1,)), after(grad_k, late_sum.upward), grad_v, w_kv, grad_q, w_q,
+        jnp.reshape(first_tok, (1,)), after(grad_k, late_sum.upward, total_all), grad_v, w_kv, grad_q, w_q,
         embedded, gain_all[0:1], grad_middle, -scaled_weight * own_rows.astype(f32),
     )
     late_sum.hop(grad_looked)
-    packed = far_pack(first_slots, after(grad_looked, late_sum.upward), share, total_row)
+    packed = far_pack(first_slots, after(grad_looked, late_sum.upward), share)
     grad_arrived = far_send(packed, share)
     grad_gain = jnp.stack([grad_gain_first[0], grad_gain_mid, grad_gain_last])
     early_mine, early_theirs = grad_pack(
@@ -1030,31 +1028,31 @@
     )
 
     early_sum = RingSum(early_mine, early_theirs, True, gate=row)
-    grad_arrived = after(grad_arrived, early_sum.terms[0])
+    head_part = head_grad(
+        table_low, after(rows_all, early_sum.terms[0]), total_all, head_weight, 0, 2
+    )
+    grad_arrived = after(grad_arrived, head_part)
     late_sum.hop(grad_arrived)
-    spare_rows = grad_arrived.reshape(owners, groups, share, D)[:, :, share - 1].astype(f32)
-    total_all = spare_rows[..., :LOSS] + spare_rows[..., LOSS : 2 * LOSS] + spare_rows[..., 2 * LOSS :]
-    total_all = total_all.transpose(1, 0, 2)
-    early_sum.ready(late_sum.upward)
-    head_first = head_grad(
-        table_low, after(rows_all, late_sum.upward, early_sum.upward), total_all, head_weight, 0
-    )
-    late_sum.hop(head_first)
+    head_part = head_part + far_add(after(grad_arrived, late_sum.upward), first_ids, share)
+    early_sum.ready(head_part)
+    head_part = head_grad(
+        table_low, after(rows_all, late_sum.upward, early_sum.upward), total_all, head_weight, 2, 1,
+        (head_part,),
+    )
+    late_sum.hop(head_part)
     early_sum.hop(late_sum.upward)
     table_head = head_grad(
-        table_low, after(rows_all, late_sum.upward, early_sum.upward), total_all, head_weight, 1,
-        (head_first,),
+        table_low, after(rows_all, late_sum.upward, early_sum.upward), total_all, head_weight, 3, 1,
+        (head_part,),
     )
     late_sum.hop(table_head)
     early_sum.hop(late_sum.upward)
-    grad_table = table_head + far_add(
-        after(grad_arrived, late_sum.upward, early_sum.upward), first_ids, share
-    )
+    grad_table = table_head
     late_terms = late_sum.total()
     (summed_early,) = early_sum.total()
 
     def next_turn(turn, total):
-        slots = far_slots(share - 1 + turn * few, few, few)
+        slots = far_slots(share + turn * few, few)
         return total + far_add(
             far_send(far_pack(slots, grad_looked, few), few), far_ids(slots, 0, few), few
         )

time: 634 us -> 627 us (0.989)
  waiting for transfers between devices: 133 us -> 117 us
  starting transfers between devices: 44.2 us -> 51.4 us
    all_to_all x1, waiting for transfers between devices: 10.4 us -> 0.01 us  [far_send(): lax.all_to_all(packed.reshape(world, share, D), ('mp', 'dp'), split_axis=...]
    ppermute x30, waiting for transfers between devices: 65.8 us -> 57.3 us  [permute(): lax.ppermute(value, axis, [(i, target(i)) for i in range(lax.axis_size(ax...]
    pallas_call x2 -> x3, Pallas kernels: 37.2 us -> 39.4 us  [head_grad(): pl.pallas_call(head_grad_kernel, grid=(part,), in_specs=[whole, pl.BlockS...]
    unnamed x177 -> x188, local copies, waits for them, and re-layouts: 13.3 us -> 14.2 us
  transfers between devices with their start and end apart: 36 -> 37, of which waited for: 18 -> 19; matrix products, arithmetic and copies ran while one was open for 21% -> 21% of each run, Pallas kernels for 34% -> 35%
where the time goes in v4:
time: 627 us; the launch traced here: 617 us
  Pallas kernels  224 us (36%)
  waiting for transfers between devices  117 us (19%)
  other arithmetic  67.1 us (11%)
  starting transfers between devices  51.4 us (8%)
  matrix products  48.2 us (8%)
  local copies, waits for them, and re-layouts  44.8 us (7%)
  blocking collectives  42 us (7%)
  between operations  22.4 us (4%)
    ppermute x30, waiting for transfers between devices, permute(): lax.ppermute(value, axis, [(i, target(i)) for i in range(lax.axis_size(ax...  57.3 us
    pallas_call x2, Pallas kernels, head_scan(): pl.pallas_call(lambda *refs: head_scan_kernel(*refs, carried=bool(carry),...  47.6 us
    all_to_all x1, blocking collectives, far_ids(): lax.all_to_all(ids, ('mp', 'dp'), split_axis=0, concat_axis=0, tiled=True)  42 us
    pallas_call x3, Pallas kernels, head_grad(): pl.pallas_call(head_grad_kernel, grid=(part,), in_specs=[whole, pl.BlockS...  39.4 us
    ppermute x30, starting transfers between devices, permute(): lax.ppermute(value, axis, [(i, target(i)) for i in range(lax.axis_size(ax...  35.8 us
    all_to_all x1, waiting for transfers between devices, far_fetch(): lax.all_to_all(rows.reshape(world, share, D), ('mp', 'dp'), split_axis=0,...  31.1 us
    pallas_call x1, Pallas kernels, attention_all(): pl.pallas_call(lambda *refs: attention_all_kernel(*refs, block=512), grid...  29.9 us
    pallas_call x1, Pallas kernels, layer_stats(): pl.pallas_call(layer_stats_kernel, grid_spec=pltpu.PrefetchScalarGridSpec...  21.7 us
  transfers between devices with their start and end apart: 37, of which 19 were waited for; matrix products, arithmetic and copies ran while one was open for 21% of the time, Pallas kernels for 35%

profile of v4, /device:TPU:0, one launch (start us, length us, event | category | flops | bytes accessed | tf_op | source)
XLA Modules:
  0.0 617.4 jit_solution(18094802937334671789)
XLA Ops:
  12.9 3.1 collective-permute-start
  25.8 42.0 %all_to_all.81 = s32[32,1,49]{2,1,0:T(1,128)S(1)} all-to-all(s32[32,1,49]{2,1,0:T(1,128)S(1)} %bitcast.269), channel_id=1, replica_groups=mesh['dp'=8,'mp'=4] {'mp','dp'}, dimensions={0} | all-to-all | bytes 12544 | tf_op jit(solution)/shard_map/all_to_all | solution.py:856
  68.0 4.8 fusion.29
  72.8 3.5 all-to-all-start.5
  84.4 19.6 %all-gather.8.cloned.1.call-done = bf16[1024,3072]{1,0:T(8,128)(2,1)} async-done(((bf16[32,3072]{1,0:T(8,128)(2,1)}), bf16[1024,3072]{1,0:T(8,128)(2,1)}) %all-gather.8.cloned.1.call-update) | async-done | bytes 6291472 | tf_op jit(solution)/shard_map/all_gather | solution.py:821
  103.9 3.2 slice.161
  111.4 3.2 fusion.101
  114.6 31.1 %all-to-all-done.5 = bf16[32,48,768]{2,1,0:T(8,128)(2,1)} async-done(((bf16[32,48,768]{2,1,0:T(8,128)(2,1)}), bf16[32,48,768]{2,1,0:T(8,128)(2,1)}, u32[]{:S(2)}, u32[]{:S(2)}) %all-to-all-start.5) | async-done | bytes 2359328 | tf_op jit(solution)/shard_map/all_to_all | solution.py:867
  147.1 4.5 fusion.23
  151.9 3.9 fusion.107
  159.6 3.9 convolution_convert_fusion.k_ref.v_ref.refs_1_.refs_2_
  163.6 15.8 %attention_pick.1 = (bf16[256,768]{1,0:T(8,128)(2,1)}, f32[6,8,256]{2,1,0:T(8,128)}) custom-call(s32[1]{0:T(128)} %bitcast.11.first_ref, bf16[256,768]{1,0:T(8,128)(2,1)} %convolution_convert_fusion.3.q_ref, bf16[1024,1536]{1,0:T(8,128)(2,1)} %convolution_convert_fusion.k_ref.v_ref.refs_1_.refs_2_, ...), custom_call_target="tpu_custom_call" | custom-call | flops 3221225472 | bytes 4718592 | tf_op jit(solution)/shard_map/attention_pick/pallas_call | solution.py:141
  189.6 29.9 %attention_all.1.attended_ref = bf16[1024,768]{1,0:T(8,128)(2,1)} custom-call(bf16[1024,768]{1,0:T(8,128)(2,1)} %convolution_convert_fusion.1.refs_0_, bf16[1024,1536]{1,0:T(8,128)(2,1)} %convolution_convert_fusion.k_ref.v_ref.refs_1_.refs_2_, bf16[1024,1536]{1,0:T(8,128)(2,1)} %convolution_convert_fusion.k_ref.v_ref.refs_1_.refs_2_), custom_call_target="tpu_custom_call" | custom-call | flops 12884901888 | bytes 6291456 | tf_op jit(solution)/shard_map/attention_all/pallas_call | solution.py:99
  222.3 4.5 collective-permute-done.4.refs_4_
  230.9 2.8 slice.172
  238.2 3.7 multiply_convert_fusion
  248.2 9.2 %collective-permute-done.2 = bf16[256,768]{1,0:T(8,128)(2,1)S(1)} collective-permute-done((bf16[256,768]{1,0:T(8,128)(2,1)S(1)}, bf16[256,768]{1,0:T(8,128)(2,1)S(1)}, u32[]{:S(2)}, u32[]{:S(2)}) %collective-permute-start.2) | collective-permute-done | bytes 393248 | tf_op jit(solution)/shard_map/ppermute | solution.py:496
  257.6 7.8 %collective-permute-done.7.refs_4_ = bf16[1032,768]{1,0:T(8,128)(2,1)} collective-permute-done((bf16[1032,768]{1,0:T(8,128)(2,1)}, bf16[1032,768]{1,0:T(8,128)(2,1)}, u32[]{:S(2)}, u32[]{:S(2)}) %collective-permute-start.7) | collective-permute-done | bytes 1585184 | tf_op jit(solution)/shard_map/ppermute | solution.py:496
  272.0 26.1 %head_scan.2 = (f32[1024,768]{1,0:T(8,128)}, f32[1024,1]{1,0:T(8,128)}) custom-call(bf16[1024,768]{1,0:T(8,128)(2,1)} %bitcast.261, bf16[1032,768]{1,0:T(8,128)(2,1)S(1)} %copy-done.25, bf16[1032,768]{1,0:T(8,128)(2,1)} %collective-permute-done.refs_2_, bf16[1032,768]{1,0:T(8,128)(2,1)} %collective-permute-done.1.refs_3_, ...), custom_call_target="tpu_custom_call" | custom-call | flops 16231956480 | bytes 11071488 | tf_op jit(solution)/shard_map/head_scan/pallas_call | solution.py:437
  298.2 21.5 %head_scan.3 = (bf16[512,896]{1,0:T(8,128)(2,1)}, bf16[512,896]{1,0:T(8,128)(2,1)}) custom-call(bf16[1024,768]{1,0:T(8,128)(2,1)} %bitcast.262, f32[1024,768]{1,0:T(8,128)} %get-tuple-element.211.refs_1_, f32[1024,1]{1,0:T(8,128)} %get-tuple-element.213.refs_2_, bf16[1032,768]{1,0:T(8,128)(2,1)} %collective-permute-done.6.refs_3_, ...), custom_call_target="tpu_custom_call" | custom-call | flops 9739173888 | bytes 7901184 | tf_op jit(solution)/shard_map/head_scan/pallas_call | solution.py:437
  319.8 2.7 collective-permute-done.10.refs_1_
  323.5 3.2 merge.2
  332.2 16.0 %collective-permute-done.11.refs_1_ = bf16[256,896]{1,0:T(8,128)(2,1)} collective-permute-done((bf16[256,896]{1,0:T(8,128)(2,1)}, bf16[256,896]{1,0:T(8,128)(2,1)}, u32[]{:S(2)}, u32[]{:S(2)}) %collective-permute-start.11) | collective-permute-done | bytes 458784 | tf_op jit(solution)/shard_map/ppermute | solution.py:496
  355.6 5.4 fusion.36.refs_2_
  364.4 9.7 %grad_pack.2 = (bf16[16,224,768]{2,1,0:T(8,128)(2,1)}, bf16[16,224,768]{2,1,0:T(8,128)(2,1)}) custom-call(s32[1]{0:T(128)} %bitcast.24.refs_0_, bf16[256,768]{1,0:T(8,128)(2,1)} %copy-done.32, bf16[256,3072]{1,0:T(8,128)(2,1)} %copy-done.30, bf16[256,3072]{1,0:T(8,128)(2,1)} %copy-done.29, bf16[256,768]{1,0:T(8,128)(2,1)} %copy-done.33, ...), custom_call_target="tpu_custom_call" | custom-call | flops 1 | bytes 1 | tf_op jit(solution)/shard_map/grad_pack/pallas_call | solution.py:598
  375.4 21.3 %attention_back.1 = (bf16[256,768]{1,0:T(8,128)(2,1)}, bf16[1024,768]{1,0:T(8,128)(2,1)}, bf16[1024,768]{1,0:T(8,128)(2,1)}) custom-call(s32[1]{0:T(128)} %bitcast.11.first_ref, bf16[256,768]{1,0:T(8,128)(2,1)} %convolution_convert_fusion.3.q_ref, bf16[1024,1536]{1,0:T(8,128)(2,1)} %convolution_convert_fusion.k_ref.v_ref.refs_1_.refs_2_, ...), custom_call_target="tpu_custom_call" | custom-call | flops 8053063680 | bytes 7864320 | tf_op jit(solution)/shard_map/attention_back/pallas_call | solution.py:210
  402.6 13.4 %first_back.1 = (bf16[1024,768]{1,0:T(8,128)(2,1)}, bf16[1024,768]{1,0:T(8,128)(2,1)}, f32[1,768]{1,0:T(1,128)}) custom-call(s32[1]{0:T(128)} %bitcast.31.bounds_ref, bf16[1024,768]{1,0:T(8,128)(2,1)} %get-tuple-element.224.k_ref.refs_4_, bf16[1024,768]{1,0:T(8,128)(2,1)} %get-tuple-element.225.v_ref.refs_6_, bf16[768,1536]{1,0:T(8,128)(2,1)} %bitcast.244, ...), custom_call_target="tpu_custom_call" | custom-call | flops 2415919104 | bytes 12582912 | tf_op jit(solution)/shard_map/first_back/pallas_call | solution.py:330
  418.2 3.5 fusion.47
  422.3 3.8 all-to-all-start.7
  426.2 4.7 fusion.28
  433.4 3.6 all-to-all-start.6
  439.1 11.3 %grad_pack.3 = (bf16[16,112,768]{2,1,0:T(8,128)(2,1)}, bf16[16,112,768]{2,1,0:T(8,128)(2,1)}) custom-call(s32[1]{0:T(128)} %bitcast.24.refs_0_, bf16[256,768]{1,0:T(8,128)(2,1)} %copy-done.18, bf16[256,768]{1,0:T(8,128)(2,1)} %get-tuple-element.221.q_ref.refs_2_, bf16[1024,768]{1,0:T(8,128)(2,1)} %copy-done.4, ...), custom_call_target="tpu_custom_call" | custom-call | flops 1 | bytes 1 | tf_op jit(solution)/shard_map/grad_pack/pallas_call | solution.py:598
  454.4 21.7 %layer_stats.1.refs_0_ = f32[1,128]{1,0:T(1,128)} custom-call(s32[1]{0:T(128)} %bitcast.40.valid_ref, bf16[1024,768]{1,0:T(8,128)(2,1)} %attention_all.1.attended_ref, f32[1024,768]{1,0:T(8,128)} %copy-done, bf16[768,768]{1,0:T(8,128)(2,1)} %bitcast.237, bf16[768,3072]{1,0:T(8,128)(2,1)} %bitcast.229, bf16[3072,768]{1,0:T(8,128)(2,1)} %bitcast.235, ...), custom_call_target="tpu_custom_call" | custom-call | flops 1 | bytes 1 | tf_op jit(solution)/shard_map/layer_stats/pallas_call | solution.py:273
  477.7 3.7 add_convert_fusion.1
  483.1 18.0 %head_grad.3 = f32[1032,768]{1,0:T(8,128)} custom-call(bf16[1032,768]{1,0:T(8,128)(2,1)S(1)} %copy-done.26, bf16[8192,768]{1,0:T(8,128)(2,1)} %all-gather.6.cloned.1.call-done.rows_ref, f32[4,1,2048]{2,1,0:T(1,128)} %bitcast.270, f32[4,1,2048]{2,1,0:T(1,128)} %fusion.84.weight_ref), custom_call_target="tpu_custom_call" | custom-call | flops 12985565184 | bytes 11046912 | tf_op jit(solution)/shard_map/head_grad/pallas_call | solution.py:479
  501.1 2.8 fusion.45
  503.9 5.6 collective-permute-start.17
  509.5 6.6 %fusion.25.refs_0_ = f32[1032,768]{1,0:T(8,128)} fusion(f32[1032,768]{1,0:T(8,128)S(1)} %copy-done.90, bf16[1536,768]{1,0:T(8,128)(2,1)} %bitcast.35, s32[1536]{0:T(1024)S(1)} %copy-done.71), kind=kOutput, calls=%fused_computation.49 | convolution fusion | flops 2437171200 | bytes 8706048 | tf_op jit(solution)/shard_map/dot_general | solution.py:38
  521.1 11.5 %head_grad.4.refs_0_ = f32[1032,768]{1,0:T(8,128)} custom-call(bf16[1032,768]{1,0:T(8,128)(2,1)S(1)} %copy-done.26, bf16[8192,768]{1,0:T(8,128)(2,1)} %all-gather.6.cloned.1.call-done.rows_ref, f32[4,1,2048]{2,1,0:T(1,128)} %bitcast.271, f32[4,1,2048]{2,1,0:T(1,128)} %fusion.84.weight_ref, f32[1032,768]{1,0:T(8,128)} %fusion.25.refs_0_), custom_call_target="tpu_custom_call" | custom-call | flops 6492782592 | bytes 11046912 | tf_op jit(solution)/shard_map/head_grad/pallas_call | solution.py:479
  540.5 9.9 %head_grad.5 = f32[1032,768]{1,0:T(8,128)S(1)} custom-call(bf16[1032,768]{1,0:T(8,128)(2,1)S(1)} %copy-done.27, bf16[8192,768]{1,0:T(8,128)(2,1)} %all-gather.6.cloned.1.call-done.rows_ref, f32[4,1,2048]{2,1,0:T(1,128)} %bitcast.272, f32[4,1,2048]{2,1,0:T(1,128)} %fusion.84.weight_ref, f32[1032,768]{1,0:T(8,128)} %head_grad.4.refs_0_), custom_call_target="tpu_custom_call" | custom-call | flops 6492782592 | bytes 11046912 | tf_op jit(solution)/shard_map/head_grad/pallas_call | solution.py:479
  559.0 3.5 collective-permute-done.26
  568.5 2.5 collective-permute-start.29
  573.6 2.7 collective-permute-done.29.refs_5_
  577.0 4.0 finish_sum.1
  581.0 4.6 all-to-all-start.8
  586.2 6.5 %all-to-all-done.8 = f32[32,1,128]{2,1,0:T(1,128)S(1)} async-done(((f32[32,1,128]{2,1,0:T(1,128)}), f32[32,1,128]{2,1,0:T(1,128)S(1)}, u32[]{:S(2)}, u32[]{:S(2)}) %all-to-all-start.8) | async-done | bytes 16416 | tf_op jit(solution)/shard_map/all_to_all | solution.py:1070
  593.3 4.3 renew_matrices.1
  601.5 5.1 fusion.94
  (373 shorter events, 139.1 us)
Async XLA Ops:
  7.2 96.7 %all-gather.8.cloned.1.call-start = ((), (), s32[]{:S(2)}) async-start(), calls=%async_computation.10 | async-start | bytes 6488064 | tf_op jit(solution)/shard_map/all_gather | solution.py:821
  10.8 220.2 %all-gather.10.cloned.1.call-start = ((), (), s32[]{:S(2)}) async-start(), calls=%async_computation.11 | async-start | bytes 9732096 | tf_op jit(solution)/shard_map/all_gather | solution.py:821
  12.9 59.8 %copy-start.24 = (bf16[1032,768]{1,0:T(8,128)(2,1)}, bf16[1032,768]{1,0:T(8,128)(2,1)S(1)}, u32[]{:S(2)}) copy-start(bf16[1032,768]{1,0:T(8,128)(2,1)S(1)} %convert_element_type.395.refs_1_.table_ref) | copy-start | bytes 4755460
  12.9 59.8 %collective-permute-start = (bf16[1032,768]{1,0:T(8,128)(2,1)S(1)}, bf16[1032,768]{1,0:T(8,128)(2,1)}, u32[]{:S(2)}, u32[]{:S(2)}) collective-permute-start(bf16[1032,768]{1,0:T(8,128)(2,1)S(1)} %convert_element_type.395.refs_1_.table_ref), channel_id=1, source_target_pairs={{0,8},{4,0},{8,16},{12,4},{16,24},{20,12},{24,28},{28,20},{1,9},{5... | collective-permute-start | bytes 4755464 | tf_op jit(solution)/shard_map/ppermute | solution.py:496
  16.0 56.8 %collective-permute-start.1 = (bf16[1032,768]{1,0:T(8,128)(2,1)S(1)}, bf16[1032,768]{1,0:T(8,128)(2,1)}, u32[]{:S(2)}, u32[]{:S(2)}) collective-permute-start(bf16[1032,768]{1,0:T(8,128)(2,1)S(1)} %convert_element_type.395.refs_1_.table_ref), channel_id=1, source_target_pairs={{0,4},{4,12},{8,0},{12,20},{16,8},{20,28},{24,16},{28,24},{1,5},{5... | collective-permute-start | bytes 4755464 | tf_op jit(solution)/shard_map/ppermute | solution.py:496
  23.4 123.7 %copy-start.75 = (s32[1024]{0:T(1024)}, s32[1024]{0:T(1024)S(1)}, u32[]{:S(2)}) copy-start(s32[1024]{0:T(1024)S(1)} %get-tuple-element.423) | copy-start | bytes 12292
  72.8 72.9 %all-to-all-start.5 = ((bf16[32,48,768]{2,1,0:T(8,128)(2,1)}), bf16[32,48,768]{2,1,0:T(8,128)(2,1)}, u32[]{:S(2)}, u32[]{:S(2)}) async-start(bf16[32,48,768]{2,1,0:T(8,128)(2,1)} %bitcast.6), calls=%async_computation.5 | async-start | bytes 4718592 | tf_op jit(solution)/shard_map/all_to_all | solution.py:867
  76.3 406.7 %all-gather.6.cloned.1.call-start = ((), (), s32[]{:S(2)}) async-start(), calls=%async_computation.9 | async-start | bytes 12976128 | tf_op jit(solution)/shard_map/all_gather | solution.py:983
  78.4 30.3 %copy-start.84 = (f32[32]{0:T(128)}, f32[32]{0:T(128)S(1)}, u32[]{:S(2)}) copy-start(f32[32]{0:T(128)S(1)} %fusion.85) | copy-start | bytes 388
  81.6 70.2 %copy-start.36 = (bf16[1024,128]{1,0:T(8,128)(2,1)}, bf16[1024,128]{1,0:T(8,128)(2,1)S(1)}, u32[]{:S(2)}) copy-start(bf16[1024,128]{1,0:T(8,128)(2,1)S(1)} %fusion.54) | copy-start | bytes 786436
  182.0 44.8 %collective-permute-start.4 = (bf16[1032,768]{1,0:T(8,128)(2,1)}, bf16[1032,768]{1,0:T(8,128)(2,1)}, u32[]{:S(2)}, u32[]{:S(2)}) collective-permute-start(bf16[1032,768]{1,0:T(8,128)(2,1)} %collective-permute-done.refs_2_), channel_id=1, source_target_pairs={{0,8},{4,0},{8,16},{12,4},{16,24},{20,12},{24,28},{28,20},{1,9},{5... | collective-permute-start | bytes 4755464 | tf_op jit(solution)/shard_map/ppermute | solution.py:496
  182.0 46.9 %collective-permute-start.5 = (bf16[1032,768]{1,0:T(8,128)(2,1)}, bf16[1032,768]{1,0:T(8,128)(2,1)}, u32[]{:S(2)}, u32[]{:S(2)}) collective-permute-start(bf16[1032,768]{1,0:T(8,128)(2,1)} %collective-permute-done.1.refs_3_), channel_id=1, source_target_pairs={{0,4},{4,12},{8,0},{12,20},{16,8},{20,28},{24,16},{28,24},{1,5},{5... | collective-permute-start | bytes 4755464 | tf_op jit(solution)/shard_map/ppermute | solution.py:496
  189.6 46.8 %copy-start.32 = (bf16[256,768]{1,0:T(8,128)(2,1)}, bf16[256,768]{1,0:T(8,128)(2,1)S(1)}, u32[]{:S(2)}) copy-start(bf16[256,768]{1,0:T(8,128)(2,1)S(1)} %multiply_convert_fusion.3.refs_1_) | copy-start | bytes 1179652
  228.9 36.5 %collective-permute-start.7 = (bf16[1032,768]{1,0:T(8,128)(2,1)}, bf16[1032,768]{1,0:T(8,128)(2,1)}, u32[]{:S(2)}, u32[]{:S(2)}) collective-permute-start(bf16[1032,768]{1,0:T(8,128)(2,1)} %collective-permute-done.5.refs_5_), channel_id=1, source_target_pairs={{0,4},{4,12},{8,0},{12,20},{16,8},{20,28},{24,16},{28,24},{1,5},{5... | collective-permute-start | bytes 4755464 | tf_op jit(solution)/shard_map/ppermute | solution.py:496
  230.6 36.7 %collective-permute-start.6 = (bf16[1032,768]{1,0:T(8,128)(2,1)}, bf16[1032,768]{1,0:T(8,128)(2,1)}, u32[]{:S(2)}, u32[]{:S(2)}) collective-permute-start(bf16[1032,768]{1,0:T(8,128)(2,1)} %collective-permute-done.4.refs_4_), channel_id=1, source_target_pairs={{0,8},{4,0},{8,16},{12,4},{16,24},{20,12},{24,28},{28,20},{1,9},{5... | collective-permute-start | bytes 4755464 | tf_op jit(solution)/shard_map/ppermute | solution.py:496
  247.0 10.5 %collective-permute-start.2 = (bf16[256,768]{1,0:T(8,128)(2,1)S(1)}, bf16[256,768]{1,0:T(8,128)(2,1)S(1)}, u32[]{:S(2)}, u32[]{:S(2)}) collective-permute-start(bf16[256,768]{1,0:T(8,128)(2,1)S(1)} %get-tuple-element.212), channel_id=1, source_target_pairs={{0,2},{1,3},{2,0},{3,1},{4,6},{5,7},{6,4},{7,5},{8,10},{9,11},{10,... | collective-permute-start | bytes 1179656 | tf_op jit(solution)/shard_map/ppermute | solution.py:496
  257.5 13.2 %collective-permute-start.3 = (bf16[2,256,768]{2,1,0:T(8,128)(2,1)S(1)}, bf16[2,256,768]{2,1,0:T(8,128)(2,1)S(1)}, u32[]{:S(2)}, u32[]{:S(2)}) collective-permute-start(bf16[2,256,768]{2,1,0:T(8,128)(2,1)S(1)} %get-tuple-element.413), channel_id=1, source_target_pairs={{0,1},{1,0},{2,3},{3,2},{4,5},{5,4},{6,7},{7,6},{8,9},{9,8},{10,11... | collective-permute-start | bytes 2359304 | tf_op jit(solution)/shard_map/ppermute | solution.py:496
  268.5 29.7 %collective-permute-start.8 = (bf16[520,768]{1,0:T(8,128)(2,1)S(1)}, bf16[520,768]{1,0:T(8,128)(2,1)}, u32[]{:S(2)}, u32[]{:S(2)}) collective-permute-start(bf16[520,768]{1,0:T(8,128)(2,1)S(1)} %slice.143), channel_id=1, source_target_pairs={{0,4},{4,12},{8,0},{12,20},{16,8},{20,28},{24,16},{28,24},{1,5},{5... | collective-permute-start | bytes 2396168 | tf_op jit(solution)/shard_map/ppermute | solution.py:496
  270.1 28.0 %collective-permute-start.9 = (bf16[512,768]{1,0:T(8,128)(2,1)S(1)}, bf16[512,768]{1,0:T(8,128)(2,1)}, u32[]{:S(2)}, u32[]{:S(2)}) collective-permute-start(bf16[512,768]{1,0:T(8,128)(2,1)S(1)} %slice.142), channel_id=1, source_target_pairs={{0,8},{4,0},{8,16},{12,4},{16,24},{20,12},{24,28},{28,20},{1,9},{5... | collective-permute-start | bytes 2359304 | tf_op jit(solution)/shard_map/ppermute | solution.py:496
  319.7 2.7 collective-permute-start.10
  323.4 28.2 %copy-start.74 = (f32[256]{0:T(256)S(1)}, f32[256]{0:T(256)}, u32[]{:S(2)}) copy-start(f32[256]{0:T(256)} %get-tuple-element.375) | copy-start | bytes 3076
  323.5 29.5 %copy-start.54 = (f32[768]{0:T(1024)S(1)}, f32[768]{0:T(1024)}, u32[]{:S(2)}) copy-start(f32[768]{0:T(1024)} %mul.446) | copy-start | bytes 9220
  323.5 29.6 %copy-start.59 = (f32[256]{0:T(256)S(1)}, f32[256]{0:T(256)}, u32[]{:S(2)}) copy-start(f32[256]{0:T(256)} %copy-done.58) | copy-start | bytes 3076
  323.5 29.6 %copy-start.63 = (f32[256]{0:T(256)S(1)}, f32[256]{0:T(256)}, u32[]{:S(2)}) copy-start(f32[256]{0:T(256)} %copy-done.62) | copy-start | bytes 3076
  326.7 28.3 %copy-start.69 = (f32[256]{0:T(256)S(1)}, f32[256]{0:T(256)}, u32[]{:S(2)}) copy-start(f32[256]{0:T(256)} %copy-done.68) | copy-start | bytes 3076
  328.9 19.3 %collective-permute-start.11 = (bf16[256,896]{1,0:T(8,128)(2,1)}, bf16[256,896]{1,0:T(8,128)(2,1)}, u32[]{:S(2)}, u32[]{:S(2)}) collective-permute-start(bf16[256,896]{1,0:T(8,128)(2,1)} %get-tuple-element.410), channel_id=1, source_target_pairs={{0,2},{1,3},{2,0},{3,1},{4,6},{5,7},{6,4},{7,5},{8,10},{9,11},{10,... | collective-permute-start | bytes 1376264 | tf_op jit(solution)/shard_map/ppermute | solution.py:496
  374.1 22.6 %collective-permute-start.12 = (bf16[16,224,768]{2,1,0:T(8,128)(2,1)}, bf16[16,224,768]{2,1,0:T(8,128)(2,1)}, u32[]{:S(2)}, u32[]{:S(2)}) collective-permute-start(bf16[16,224,768]{2,1,0:T(8,128)(2,1)} %get-tuple-element.218), channel_id=1, source_target_pairs={{0,1},{1,0},{2,3},{3,2},{4,5},{5,4},{6,7},{7,6},{8,9},{9,8},{10,11... | collective-permute-start | bytes 16515080 | tf_op jit(solution)/shard_map/ppermute | solution.py:496
  398.8 18.0 %collective-permute-start.13 = (bf16[2,224,768]{2,1,0:T(8,128)(2,1)S(1)}, bf16[2,224,768]{2,1,0:T(8,128)(2,1)S(1)}, u32[]{:S(2)}, u32[]{:S(2)}) collective-permute-start(bf16[2,224,768]{2,1,0:T(8,128)(2,1)S(1)} %get-tuple-element.395), channel_id=1, source_target_pairs={{0,8},{4,0},{8,16},{12,4},{16,24},{20,12},{24,28},{28,20},{1,9},{5... | collective-permute-start | bytes 2064392 | tf_op jit(solution)/shard_map/ppermute | solution.py:496
  400.4 17.8 %collective-permute-start.14 = (bf16[2,224,768]{2,1,0:T(8,128)(2,1)S(1)}, bf16[2,224,768]{2,1,0:T(8,128)(2,1)S(1)}, u32[]{:S(2)}, u32[]{:S(2)}) collective-permute-start(bf16[2,224,768]{2,1,0:T(8,128)(2,1)S(1)} %get-tuple-element.394), channel_id=1, source_target_pairs={{0,4},{4,12},{8,0},{12,20},{16,8},{20,28},{24,16},{28,24},{1,5},{5... | collective-permute-start | bytes 2064392 | tf_op jit(solution)/shard_map/ppermute | solution.py:496
  422.3 11.1 %all-to-all-start.7 = ((f32[32,1,256]{2,1,0:T(1,128)}), f32[32,1,256]{2,1,0:T(1,128)S(1)}, u32[]{:S(2)}, u32[]{:S(2)}) async-start(f32[32,1,256]{2,1,0:T(1,128)} %broadcast_in_dim.185), calls=%async_computation.7 | async-start | bytes 65536 | tf_op jit(solution)/shard_map/all_to_all | solution.py:984
  433.4 67.7 %all-to-all-start.6 = ((bf16[32,48,768]{2,1,0:T(8,128)(2,1)}), bf16[32,48,768]{2,1,0:T(8,128)(2,1)}, u32[]{:S(2)}, u32[]{:S(2)}) async-start(bf16[32,48,768]{2,1,0:T(8,128)(2,1)} %bitcast.34), calls=%async_computation.6 | async-start | bytes 4718592 | tf_op jit(solution)/shard_map/all_to_all | solution.py:880
  450.4 25.8 %collective-permute-start.19 = (bf16[16,112,768]{2,1,0:T(8,128)(2,1)}, bf16[16,112,768]{2,1,0:T(8,128)(2,1)S(1)}, u32[]{:S(2)}, u32[]{:S(2)}) collective-permute-start(bf16[16,112,768]{2,1,0:T(8,128)(2,1)} %get-tuple-element.240), channel_id=1, source_target_pairs={{0,1},{1,0},{2,3},{3,2},{4,5},{5,4},{6,7},{7,6},{8,9},{9,8},{10,11... | collective-permute-start | bytes 8257544 | tf_op jit(solution)/shard_map/ppermute | solution.py:496
  452.4 48.7 %collective-permute-start.15 = (bf16[2,224,768]{2,1,0:T(8,128)(2,1)}, bf16[2,224,768]{2,1,0:T(8,128)(2,1)}, u32[]{:S(2)}, u32[]{:S(2)}) collective-permute-start(bf16[2,224,768]{2,1,0:T(8,128)(2,1)} %get-tuple-element.393), channel_id=1, source_target_pairs={{0,8},{4,0},{8,16},{12,4},{16,24},{20,12},{24,28},{28,20},{1,9},{5... | collective-permute-start | bytes 2064392 | tf_op jit(solution)/shard_map/ppermute | solution.py:496
  454.1 47.0 %collective-permute-start.16 = (bf16[2,224,768]{2,1,0:T(8,128)(2,1)}, bf16[2,224,768]{2,1,0:T(8,128)(2,1)}, u32[]{:S(2)}, u32[]{:S(2)}) collective-permute-start(bf16[2,224,768]{2,1,0:T(8,128)(2,1)} %get-tuple-element.392), channel_id=1, source_target_pairs={{0,4},{4,12},{8,0},{12,20},{16,8},{20,28},{24,16},{28,24},{1,5},{5... | collective-permute-start | bytes 2064392 | tf_op jit(solution)/shard_map/ppermute | solution.py:496
  481.4 55.7 %copy-start.17 = (bf16[8,1,112,768]{3,2,1,0:T(8,128)(2,1)}, bf16[8,1,112,768]{3,2,1,0:T(8,128)(2,1)S(1)}, u32[]{:S(2)}) copy-start(bf16[8,1,112,768]{3,2,1,0:T(8,128)(2,1)S(1)} %get-tuple-element.402) | copy-start | bytes 4128772
  481.4 35.3 %collective-permute-start.20 = (bf16[8,112,768]{2,1,0:T(8,128)(2,1)}, bf16[8,112,768]{2,1,0:T(8,128)(2,1)}, u32[]{:S(2)}, u32[]{:S(2)}) collective-permute-start(bf16[8,112,768]{2,1,0:T(8,128)(2,1)} %get-tuple-element.403), channel_id=1, source_target_pairs={{0,2},{1,3},{2,0},{3,1},{4,6},{5,7},{6,4},{7,5},{8,10},{9,11},{10,... | collective-permute-start | bytes 4128776 | tf_op jit(solution)/shard_map/ppermute | solution.py:496
  503.9 28.7 %collective-permute-start.17 = (bf16[2,224,768]{2,1,0:T(8,128)(2,1)S(1)}, bf16[2,224,768]{2,1,0:T(8,128)(2,1)S(1)}, u32[]{:S(2)}, u32[]{:S(2)}) collective-permute-start(bf16[2,224,768]{2,1,0:T(8,128)(2,1)S(1)} %get-tuple-element.391), channel_id=1, source_target_pairs={{0,8},{4,0},{8,16},{12,4},{16,24},{20,12},{24,28},{28,20},{1,9},{5... | collective-permute-start | bytes 2064392 | tf_op jit(solution)/shard_map/ppermute | solution.py:496
  516.7 18.1 %collective-permute-start.18 = (bf16[2,224,768]{2,1,0:T(8,128)(2,1)S(1)}, bf16[2,224,768]{2,1,0:T(8,128)(2,1)S(1)}, u32[]{:S(2)}, u32[]{:S(2)}) collective-permute-start(bf16[2,224,768]{2,1,0:T(8,128)(2,1)S(1)} %get-tuple-element.390), channel_id=1, source_target_pairs={{0,4},{4,12},{8,0},{12,20},{16,8},{20,28},{24,16},{28,24},{1,5},{5... | collective-permute-start | bytes 2064392 | tf_op jit(solution)/shard_map/ppermute | solution.py:496
  517.8 19.2 %collective-permute-start.21 = (bf16[112,768]{1,0:T(8,128)(2,1)S(1)}, bf16[112,768]{1,0:T(8,128)(2,1)S(1)}, u32[]{:S(2)}, u32[]{:S(2)}) collective-permute-start(bf16[112,768]{1,0:T(8,128)(2,1)S(1)} %get-tuple-element.409), channel_id=1, source_target_pairs={{0,8},{4,0},{8,16},{12,4},{16,24},{20,12},{24,28},{28,20},{1,9},{5... | collective-permute-start | bytes 516104 | tf_op jit(solution)/shard_map/ppermute | solution.py:496
  519.9 17.2 %collective-permute-start.22 = (bf16[112,768]{1,0:T(8,128)(2,1)S(1)}, bf16[112,768]{1,0:T(8,128)(2,1)S(1)}, u32[]{:S(2)}, u32[]{:S(2)}) collective-permute-start(bf16[112,768]{1,0:T(8,128)(2,1)S(1)} %get-tuple-element.408), channel_id=1, source_target_pairs={{0,4},{4,12},{8,0},{12,20},{16,8},{20,28},{24,16},{28,24},{1,5},{5... | collective-permute-start | bytes 516104 | tf_op jit(solution)/shard_map/ppermute | solution.py:496
  536.6 15.9 %collective-permute-start.25 = (bf16[2,224,768]{2,1,0:T(8,128)(2,1)S(1)}, bf16[2,224,768]{2,1,0:T(8,128)(2,1)S(1)}, u32[]{:S(2)}, u32[]{:S(2)}) collective-permute-start(bf16[2,224,768]{2,1,0:T(8,128)(2,1)S(1)} %fusion.44), channel_id=1, source_target_pairs={{0,8},{4,0},{8,16},{12,4},{16,24},{20,12},{24,28},{28,20},{1,9},{5... | collective-permute-start | bytes 2064392 | tf_op jit(solution)/shard_map/ppermute | solution.py:496
  538.2 16.1 %collective-permute-start.23 = (bf16[112,768]{1,0:T(8,128)(2,1)S(1)}, bf16[112,768]{1,0:T(8,128)(2,1)S(1)}, u32[]{:S(2)}, u32[]{:S(2)}) collective-permute-start(bf16[112,768]{1,0:T(8,128)(2,1)S(1)} %get-tuple-element.407), channel_id=1, source_target_pairs={{0,8},{4,0},{8,16},{12,4},{16,24},{20,12},{24,28},{28,20},{1,9},{5... | collective-permute-start | bytes 516104 | tf_op jit(solution)/shard_map/ppermute | solution.py:496
  540.0 14.4 %collective-permute-start.24 = (bf16[112,768]{1,0:T(8,128)(2,1)S(1)}, bf16[112,768]{1,0:T(8,128)(2,1)S(1)}, u32[]{:S(2)}, u32[]{:S(2)}) collective-permute-start(bf16[112,768]{1,0:T(8,128)(2,1)S(1)} %get-tuple-element.406), channel_id=1, source_target_pairs={{0,4},{4,12},{8,0},{12,20},{16,8},{20,28},{24,16},{28,24},{1,5},{5... | collective-permute-start | bytes 516104 | tf_op jit(solution)/shard_map/ppermute | solution.py:496
  556.1 6.4 %collective-permute-start.26 = (bf16[112,768]{1,0:T(8,128)(2,1)}, bf16[112,768]{1,0:T(8,128)(2,1)S(1)}, u32[]{:S(2)}, u32[]{:S(2)}) collective-permute-start(bf16[112,768]{1,0:T(8,128)(2,1)} %fusion.64), channel_id=1, source_target_pairs={{0,8},{4,0},{8,16},{12,4},{16,24},{20,12},{24,28},{28,20},{1,9},{5... | collective-permute-start | bytes 516104 | tf_op jit(solution)/shard_map/ppermute | solution.py:496
  563.8 7.3 %collective-permute-start.27 = (bf16[112,768]{1,0:T(8,128)(2,1)S(1)}, bf16[112,768]{1,0:T(8,128)(2,1)S(1)}, u32[]{:S(2)}, u32[]{:S(2)}) collective-permute-start(bf16[112,768]{1,0:T(8,128)(2,1)S(1)} %get-tuple-element.404), channel_id=1, source_target_pairs={{0,8},{4,0},{8,16},{12,4},{16,24},{20,12},{24,28},{28,20},{1,9},{5... | collective-permute-start | bytes 516104 | tf_op jit(solution)/shard_map/ppermute | solution.py:496
  564.8 6.3 %collective-permute-start.28 = (bf16[112,768]{1,0:T(8,128)(2,1)S(1)}, bf16[112,768]{1,0:T(8,128)(2,1)S(1)}, u32[]{:S(2)}, u32[]{:S(2)}) collective-permute-start(bf16[112,768]{1,0:T(8,128)(2,1)S(1)} %get-tuple-element.405), channel_id=1, source_target_pairs={{0,4},{4,12},{8,0},{12,20},{16,8},{20,28},{24,16},{28,24},{1,5},{5... | collective-permute-start | bytes 516104 | tf_op jit(solution)/shard_map/ppermute | solution.py:496
  568.5 7.8 %collective-permute-start.29 = (bf16[224,768]{1,0:T(8,128)(2,1)S(1)}, bf16[224,768]{1,0:T(8,128)(2,1)S(1)}, u32[]{:S(2)}, u32[]{:S(2)}) collective-permute-start(bf16[224,768]{1,0:T(8,128)(2,1)S(1)} %get-tuple-element.414), channel_id=1, source_target_pairs={{0,2},{1,3},{2,0},{3,1},{4,6},{5,7},{6,4},{7,5},{8,10},{9,11},{10,... | collective-permute-start | bytes 1032200 | tf_op jit(solution)/shard_map/ppermute | solution.py:496
  581.0 11.6 %all-to-all-start.8 = ((f32[32,1,128]{2,1,0:T(1,128)}), f32[32,1,128]{2,1,0:T(1,128)S(1)}, u32[]{:S(2)}, u32[]{:S(2)}) async-start(f32[32,1,128]{2,1,0:T(1,128)} %bitcast.274), calls=%async_computation.8 | async-start | bytes 32768 | tf_op jit(solution)/shard_map/all_to_all | solution.py:1070
  (82 other events, 516.4 us)
Sparse Core Ops, SparseCore 0:
  11.5 92.3 all-gather.7
  107.4 97.1 all-gather.9
  298.3 102.8 all-gather.5
